TPU v7x, 256 devices: a whole 4x4x8 slice. The times are simulated.
256 devices in a mesh: sfc: 128 (over z, y, x), lev: 2 (over core).
Axes of the slice: x: 4, y: 4, z: 8, core: 2. Of those that a mesh axis runs over, the one named last changes fastest.
Arguments:
- tracers: float32 [8, 32, 16, 32768], P(None, 'lev', None, 'sfc'), may hold values from -6 to 6
- layer_mass: float32 [32, 16, 32768], P('lev', None, 'sfc'), may hold values from 0.5 to 2
- layer_mass_next: float32 [32, 16, 32768], P('lev', None, 'sfc'), may hold values from 0.5 to 2
- wind: float32 [2, 32, 16, 32768], P(None, 'lev', None, 'sfc'), may hold values from -4 to 4
- spheremp: float32 [16, 32768], P(None, 'sfc'), may hold values from 0.25 to 4
- inverse_mass: float32 [16, 32768], P(None, 'sfc'), may hold values from 0.15 to 0.6
- rec_peer: int32 [8, 32768], P(None, 'sfc'), may hold values from -1 to 127, as said below
- rec_slot: int32 [8, 32768], P(None, 'sfc'), may hold values from 0 to 1023, as said below
- rec_flip: int32 [8, 32768], P(None, 'sfc'), may hold values from 0 to 1, as said below
- publish_list: int32 [8192], P('sfc'), may hold values from -1 to 1023, as said below
- column_slot_table: int32 [4, 32768], P(None, 'sfc'), may hold values from 0 to 163839, as said below
Outputs:
- tracer_mass: float32 [8, 32, 16, 32768], P(None, 'lev', None, 'sfc')
- physics_mix: float32 [8, 32, 163840], P(None, None, ('sfc', 'lev'))
- sigma_mid: float32 [32, 163840], P(None, ('sfc', 'lev'))
Inputs may be any that keep to these rules, and one draw needn't show every extreme that they name: `rec_peer`: records 0 to 3 name the element across sides 0 to 3, records 4 to 7 the element diagonally across corners 0, 3, 12, 15 (sharing only that point); -1 where there is none. A peer differs from the element's own device by 0, 1, -1, 32, -32, 33, 31, 1 - 32 or -1 - 32. No device has more than 46 records naming one other device, and some device has exactly 46. Every point shared by elements is read by each of them from each other. `rec_slot`: A remote record's entry in the peer's publish list is not -1 and names the side that faces the record's element (for corners, a side holding the shared point); a local record's value is 4 n + s2. Records with no peer hold 0. `rec_flip`: side records: 1 where the neighbour's side runs the other way. Corner records: 0 if the shared point is position 0 of the named side, 1 if it is position 3. `publish_list`: each device's 64 entries are distinct values 4 n + s of its own elements, or -1 anywhere in the list; some device has no -1. `column_slot_table`: all distinct. The columns of one device's elements name exactly 8 slots in each block of 1280 consecutive slots.
All inputs are finite; a program needn't handle non-finite values.
Results may differ from a plain program's by a relative error of at most 0.0003.
Values sent between devices are 32-bit elements; how exact they have to be, the bound alone decides.
No kernel may reach another device: no remote copies, remote signals or barrier semaphores. Data moves between devices by JAX's collectives and lax.ppermute only.
A program may use at most 128 MiB of HBM per device.

v0:
```python
import jax
import jax.numpy as jnp
import numpy as np
from jax import lax
from jax.sharding import PartitionSpec as P

NPG = 4
DEV_ROWS = 4


SIDE_POINTS = np.array([[0, 1, 2, 3], [3, 7, 11, 15], [12, 13, 14, 15], [0, 4, 8, 12]])
CORNER_POINTS = [0, 3, 12, 15]
TIME_STEP = 0.05
TOP_PRESSURE = 1.0
MIXING_RATE = 0.8


def passed_along(shard, axis, by):
    peers = lax.axis_size(axis)
    pairs = [(i, i + by) for i in range(peers) if 0 <= i + by < peers]
    return lax.ppermute(shard, axis, pairs)


def lagrange_derivative():
    gll_points = np.array([-1.0, -1.0 / np.sqrt(5.0), 1.0 / np.sqrt(5.0), 1.0])
    barycentric = np.array(
        [
            1.0
            / np.prod(
                [gll_points[source] - gll_points[middle] for middle in range(4) if middle != source]
            )
            for source in range(4)
        ]
    )
    derivative = np.zeros((4, 4))
    for target in range(4):
        for source in range(4):
            if target != source:
                derivative[target, source] = (
                    barycentric[source]
                    / barycentric[target]
                    / (gll_points[target] - gll_points[source])
                )
        derivative[target, target] = -np.sum(derivative[target])
    return derivative


def stacked_derivative():
    lagrange = lagrange_derivative()
    return np.stack([np.kron(np.eye(4), lagrange), np.kron(lagrange, np.eye(4))], axis=1)


def quadrant_table():
    table = np.zeros((4, 16))
    for point in range(16):
        table[2 * (point // 4 // 2) + point % 4 // 2, point] = 1.0
    return table


def placement_table():
    table = np.zeros((8, 4, 16))
    for side in range(4):
        for position in range(4):
            table[side, position, SIDE_POINTS[side, position]] = 1.0
    for corner in range(4):
        table[4 + corner, 0, CORNER_POINTS[corner]] = 1.0
    return table


def side_columns(field):
    sides = field[:, SIDE_POINTS]
    return jnp.swapaxes(sides, 1, 2).reshape(field.shape[0], 4, 4 * field.shape[2])


def side_index(code, elem_count):
    return code % 4 * elem_count + code // 4


def bucket_ranks(targets, active, count):
    one_hot = ((targets[:, None] == jnp.arange(count)[None, :]) & active[:, None]).astype(jnp.int32)
    return jnp.sum(one_hot * jnp.cumsum(one_hot, axis=0), axis=1) - 1


def body(
    tracers,
    layer_mass,
    layer_mass_next,
    wind,
    spheremp,
    inverse_mass,
    rec_peer,
    rec_slot,
    rec_flip,
    publish_list,
    column_slot_table,
):
    highest = lax.Precision.HIGHEST
    own_index = lax.axis_index("sfc")
    sfc_count = lax.axis_size("sfc")
    lev_count = lax.axis_size("lev")
    lev_index = lax.axis_index("lev")
    tracer_count, level_count, point_count, elem_count = tracers.shape
    pub_count = publish_list.shape[0]
    field_count = tracer_count * level_count
    derivative = jnp.asarray(stacked_derivative(), jnp.float32)
    mass = layer_mass[None] * tracers
    fluxes = wind[:, None] * mass[None]
    divergence = jnp.einsum("kaq,atlqe->tlke", derivative, fluxes, precision=highest)
    mass_new = mass - TIME_STEP * divergence
    weighted = (spheremp * mass_new).reshape(field_count, point_count, elem_count)
    table = side_columns(weighted)
    valid = rec_peer >= 0
    peer_clip = jnp.clip(rec_peer, 0, sfc_count - 1)
    remote = valid & (peer_clip != own_index)
    local_code = side_index(jnp.clip(rec_slot, 0, 4 * elem_count - 1), elem_count)
    pub_slot = jnp.clip(rec_slot, 0, pub_count - 1)
    local_data = jnp.take(table, local_code.reshape(-1), axis=2).reshape(
        field_count, 4, 8, elem_count
    )
    publish_index = side_index(jnp.maximum(publish_list, 0), elem_count)
    published = jnp.take(table, publish_index, axis=2)
    block_cols = sfc_count // DEV_ROWS
    offsets = [
        1,
        -1,
        block_cols,
        -block_cols,
        block_cols + 1,
        block_cols - 1,
        1 - block_cols,
        -1 - block_cols,
    ]
    moved = []
    for offset in offsets:
        moved.append(passed_along(published, "sfc", offset))
    stacked = jnp.concatenate(moved, axis=2)
    distance = own_index - peer_clip
    which = jnp.zeros_like(peer_clip)
    for number, offset in enumerate(offsets):
        which = which + number * (distance == offset).astype(jnp.int32)
    remote_data = jnp.take(stacked, (which * pub_count + pub_slot).reshape(-1), axis=2).reshape(
        field_count, 4, 8, elem_count
    )
    values = jnp.where(remote[None, None], remote_data, local_data)
    values = jnp.where(valid[None, None], values, jnp.zeros_like(values))
    values = jnp.where(rec_flip[None, None] == 1, values[:, ::-1], values)
    place = jnp.asarray(placement_table(), jnp.float32)
    contrib = jnp.einsum("rmk,fmre->fke", place, values, precision=highest)
    assembled = weighted + contrib
    tracer_mass = inverse_mass * assembled.reshape(
        tracer_count, level_count, point_count, elem_count
    )
    quadrant = jnp.asarray(quadrant_table(), jnp.float32)
    mix_num = jnp.einsum("ck,tlke->tlce", quadrant, spheremp * tracer_mass, precision=highest)
    mass_den = jnp.einsum(
        "ck,lke->lce", quadrant, spheremp[None] * layer_mass_next, precision=highest
    )
    area_pg = jnp.einsum("ck,ke->ce", quadrant, spheremp, precision=highest)
    mixing_ratio_columns = mix_num / mass_den[None]
    thickness_columns = mass_den / area_pg[None]
    column_total = NPG * elem_count
    mix_flat = mixing_ratio_columns.reshape(field_count, column_total)
    thick_flat = thickness_columns.reshape(level_count, column_total)
    column_flat = column_slot_table.reshape(-1)
    phys_dev = 5 * NPG * elem_count // (4 * lev_count)
    group_width = phys_dev * lev_count
    destination = column_flat // group_width
    within = column_flat % group_width
    per_peer = column_total // sfc_count
    column_rank = bucket_ranks(destination, jnp.ones_like(destination, dtype=bool), sfc_count)
    send_mix = (
        jnp.zeros((field_count, sfc_count, per_peer), jnp.float32)
        .at[:, destination, column_rank]
        .set(mix_flat, mode="drop")
    )
    send_thick = (
        jnp.zeros((level_count, sfc_count, per_peer), jnp.float32)
        .at[:, destination, column_rank]
        .set(thick_flat, mode="drop")
    )
    send_slot = (
        jnp.full((1, sfc_count, per_peer), -1.0, jnp.float32)
        .at[0, destination, column_rank]
        .set(within.astype(jnp.float32), mode="drop")
    )
    recv_mix, recv_thick, recv_slot = (
        lax.all_to_all(send_mix, "sfc", split_axis=1, concat_axis=1, tiled=True),
        lax.all_to_all(send_thick, "sfc", split_axis=1, concat_axis=1, tiled=True),
        lax.all_to_all(send_slot, "sfc", split_axis=1, concat_axis=1, tiled=True),
    )
    arrived = sfc_count * per_peer
    mix_cols = recv_mix.reshape(tracer_count, level_count, arrived)
    thick_cols = recv_thick.reshape(level_count, arrived)
    full_mix, full_thick = (
        lax.all_gather(mix_cols, "lev", axis=1, tiled=True),
        lax.all_gather(thick_cols, "lev", axis=0, tiled=True),
    )
    slot_ids = recv_slot.reshape(arrived).astype(jnp.int32)
    position = slot_ids - lev_index * phys_dev
    keep = (slot_ids >= 0) & (position >= 0) & (position < phys_dev)
    target = jnp.where(keep, position, phys_dev)
    level_total = full_thick.shape[0]
    physics_mixing_ratio = (
        jnp.zeros((tracer_count, level_total, phys_dev), jnp.float32)
        .at[:, :, target]
        .set(full_mix, mode="drop")
    )
    physics_layer_thickness = (
        jnp.zeros((level_total, phys_dev), jnp.float32).at[:, target].set(full_thick, mode="drop")
    )
    live_flags = jnp.zeros((phys_dev,), jnp.float32).at[target].set(1.0, mode="drop")
    column_sum = jnp.sum(physics_layer_thickness, axis=0)
    above = jnp.cumsum(physics_layer_thickness, axis=0) - physics_layer_thickness
    sigma_mid = (
        live_flags[None]
        * (TOP_PRESSURE + above + 0.5 * physics_layer_thickness)
        / (TOP_PRESSURE + column_sum)[None]
    )
    mean_mix = (
        jnp.sum(physics_layer_thickness[None] * physics_mixing_ratio, axis=1)
        / (column_sum + 1.0 - live_flags)[None]
    )
    physics_mix = physics_mixing_ratio + MIXING_RATE * sigma_mid[None] * (
        mean_mix[:, None] - physics_mixing_ratio
    )
    return (tracer_mass, physics_mix, sigma_mid)


def solution(mesh):
    in_specs = (
        P(None, "lev", None, "sfc"),
        P("lev", None, "sfc"),
        P("lev", None, "sfc"),
        P(None, "lev", None, "sfc"),
        P(None, "sfc"),
        P(None, "sfc"),
        P(None, "sfc"),
        P(None, "sfc"),
        P(None, "sfc"),
        P("sfc"),
        P(None, "sfc"),
    )
    out_specs = (
        P(None, "lev", None, "sfc"),
        P(None, None, ("sfc", "lev")),
        P(None, ("sfc", "lev")),
    )
    return jax.shard_map(body, mesh=mesh, in_specs=in_specs, out_specs=out_specs, check_vma=False)
```

profile of v0, /device:TPU:1, one launch (start us, length us, event | category | flops | bytes accessed | tf_op | source)
XLA Modules:
  0.0 286.2 jit_solution(7357383601875746026)
XLA Ops:
  7.2 2.0 broadcast_multiply_fusion
  9.2 2.6 fusion.2
  11.9 1.3 copy-done
  13.2 1.2 copy.49
  14.4 2.0 gather_fusion
  16.5 2.0 copy.50
  18.6 0.7 gather_fusion.1
  19.4 4.0 %collective-permute-start = (f32[128,4,64]{0,1,2:T(4,128)S(1)}, f32[128,4,64]{0,1,2:T(4,128)S(1)}, u32[]{:S(2)}, u32[]{:S(2)}) collective-permute-start(f32[128,4,64]{0,1,2:T(4,128)S(1)} %select_bitcast_fusion), channel_id=1, source_target_pairs={{0,2},{2,4},{4,6},{6,8},{8,10},{10,12},{12,14},{14,16},{16,18},{18... | collective-permute-start | bytes 393224 | tf_op jit(solution)/shard_map/ppermute | solution.py:21
  23.4 1.3 collective-permute-start.1
  24.7 10.0 %collective-permute-start.2 = (f32[128,4,64]{0,1,2:T(4,128)S(1)}, f32[128,4,64]{0,1,2:T(4,128)S(1)}, u32[]{:S(2)}, u32[]{:S(2)}) collective-permute-start(f32[128,4,64]{0,1,2:T(4,128)S(1)} %select_bitcast_fusion), channel_id=1, source_target_pairs={{0,64},{2,66},{4,68},{6,70},{8,72},{10,74},{12,76},{14,78},{16,80}... | collective-permute-start | bytes 393224 | tf_op jit(solution)/shard_map/ppermute | solution.py:21
  34.7 1.3 collective-permute-start.3
  36.0 3.4 %collective-permute-start.4 = (f32[128,4,64]{0,1,2:T(4,128)S(1)}, f32[128,4,64]{0,1,2:T(4,128)S(1)}, u32[]{:S(2)}, u32[]{:S(2)}) collective-permute-start(f32[128,4,64]{0,1,2:T(4,128)S(1)} %select_bitcast_fusion), channel_id=1, source_target_pairs={{0,66},{2,68},{4,70},{6,72},{8,74},{10,76},{12,78},{14,80},{16,82}... | collective-permute-start | bytes 393224 | tf_op jit(solution)/shard_map/ppermute | solution.py:21
  39.6 0.2 fusion.19
  40.1 0.4 fusion.16
  40.7 4.3 %scatter_custom_fusion.3 = f32[1024]{0:T(1024)S(1)} fusion(s32[1024]{0:T(1024)S(1)} %broadcast_select_fusion.1, f32[1024]{0:T(1024)S(1)} %get-tuple-element.26, f32[]{:T(128)} %constant.199.clone.1), kind=kCustom, calls=%fused_computation.110 | custom fusion | bytes 4100
  45.0 0.7 copy.55
  45.8 15.8 %all-to-all-start = ((f32[1,128,8]{2,0,1:T(1,128)}), f32[1,128,8]{2,0,1:T(1,128)S(1)}, u32[]{:S(2)}, u32[]{:S(2)}) async-start(f32[1,128,8]{2,0,1:T(1,128)} %copy.55), calls=%async_computation | async-start | bytes 131072 | tf_op jit(solution)/shard_map/all_to_all | solution.py:189
  62.1 1.9 broadcast_divide_fusion.1
  64.0 15.4 %gather_fusion.3 = f32[2048,128,4]{1,2,0:T(4,128)} fusion(f32[128,4,1024]{0,1,2:T(4,128)S(1)} %bitcast.117, s32[2048]{0:T(1024)S(1)} %broadcast_clamp_fusion), kind=kCustom, calls=%fused_computation.3 | custom fusion | bytes 8396800 | tf_op jit(solution)/shard_map/jit(_take)/gather | solution.py:117
  79.3 6.0 %copy.52 = f32[128,4,8,256]{3,2,1,0:T(8,128)} copy(f32[128,4,8,256]{0,1,3,2:T(4,128)} %bitcast.120) | data formatting | bytes 8388608 | tf_op jit(solution)/shard_map/jit(_take)/gather | solution.py:117
  85.3 6.8 %collective-permute-start.5 = (f32[128,4,64]{0,1,2:T(4,128)S(1)}, f32[128,4,64]{0,1,2:T(4,128)S(1)}, u32[]{:S(2)}, u32[]{:S(2)}) collective-permute-start(f32[128,4,64]{0,1,2:T(4,128)S(1)} %select_bitcast_fusion), channel_id=1, source_target_pairs={{0,62},{2,64},{4,66},{6,68},{8,70},{10,72},{12,74},{14,76},{16,78}... | collective-permute-start | bytes 393224 | tf_op jit(solution)/shard_map/ppermute | solution.py:21
  92.2 1.3 collective-permute-start.6
  93.5 1.5 collective-permute-start.7
  95.1 7.0 %collective-permute-done.6 = f32[128,4,64]{0,1,2:T(4,128)S(1)} collective-permute-done((f32[128,4,64]{0,1,2:T(4,128)S(1)}, f32[128,4,64]{0,1,2:T(4,128)S(1)}, u32[]{:S(2)}, u32[]{:S(2)}) %collective-permute-start.6) | collective-permute-done | bytes 131104 | tf_op jit(solution)/shard_map/ppermute | solution.py:21
  102.1 2.8 collective-permute-done.7
  104.9 15.4 %gather_fusion.2 = f32[2048,128,4]{1,2,0:T(4,128)} fusion(f32[128,4,512]{0,1,2:T(4,128)S(1)} %constant_dynamic-update-slice_fusion, s32[2048]{0:T(1024)S(1)} %broadcast_clamp_fusion.1), kind=kCustom, calls=%fused_computation.2 | custom fusion | bytes 8396800 | tf_op jit(solution)/shard_map/jit(_take)/gather | solution.py:141
  120.3 6.0 %copy.51 = f32[128,4,8,256]{3,2,1,0:T(8,128)} copy(f32[128,4,8,256]{0,1,3,2:T(4,128)} %bitcast.121) | data formatting | bytes 8388608 | tf_op jit(solution)/shard_map/jit(_take)/gather | solution.py:141
  126.3 4.5 %select_select_fusion = f32[128,4,8,256]{3,2,1,0:T(8,128)S(1)} fusion(f32[128,4,8,256]{3,2,1,0:T(8,128)} %copy.52, f32[128,4,8,256]{3,2,1,0:T(8,128)} %copy.51, pred[8,256]{1,0:T(8,128)(4,1)S(1)} %get-tuple-element.21, pred[8,256]{1,0:T(8,128)(4,1)S(1)} %get-tuple-element.14, pred[8,256]{1,0:T(8,128)(4,1)S(1)} %get-tuple-element.23, ...), kind=kLoop, calls=%fused_computation.11 | loop fusion | flops 4194304 | bytes 12591104 | tf_op jit(solution)/shard_map/jit(_where)/select_n | solution.py:145
  130.8 0.7 reverse_select_fusion
  131.6 0.8 copy-done.1
  132.4 2.6 bitcast_add_fusion
  135.0 0.2 broadcast_multiply_fusion.1
  135.2 1.3 copy-done.2
  136.6 1.3 fusion.12
  138.0 0.2 copy.56
  138.2 3.3 %scatter_custom_fusion.4 = f32[128,1024]{0,1:T(8,128)S(1)} fusion(s32[1024]{0:T(1024)S(1)} %broadcast_select_fusion, f32[128,1024]{0,1:T(8,128)S(1)} %copy.56, f32[]{:T(128)} %constant.198.clone.1), kind=kCustom, calls=%fused_computation.32 | custom fusion | bytes 1048580
  141.4 1.1 copy.88
  142.5 15.9 %all-to-all-start.1 = ((f32[128,128,8]{0,2,1:T(8,128)}), f32[128,128,8]{0,2,1:T(8,128)S(1)}, u32[]{:S(2)}, u32[]{:S(2)}) async-start(f32[128,128,8]{0,2,1:T(8,128)} %bitcast.113), calls=%async_computation.1 | async-start | bytes 1048576 | tf_op jit(solution)/shard_map/all_to_all | solution.py:187
  158.4 0.2 copy.73
  158.6 3.2 %scatter_custom_fusion.5 = f32[16,1024]{0,1:T(8,128)S(1)} fusion(s32[1024]{0:T(1024)S(1)} %broadcast_select_fusion, f32[1024,16]{1,0:T(8,128)S(1)} %bitcast.130, f32[]{:T(128)} %constant.198.clone.1), kind=kCustom, calls=%fused_computation.40 | custom fusion | bytes 65540
  161.8 0.3 copy.89
  162.2 0.9 reshape.439
  163.0 0.2 subtract_reduce_fusion
  163.3 10.1 %all-to-all-done.1 = f32[128,128,8]{0,2,1:T(8,128)S(1)} async-done(((f32[128,128,8]{0,2,1:T(8,128)}), f32[128,128,8]{0,2,1:T(8,128)S(1)}, u32[]{:S(2)}, u32[]{:S(2)}) %all-to-all-start.1) | async-done | bytes 524320 | tf_op jit(solution)/shard_map/all_to_all | solution.py:187
  173.4 6.1 %all-to-all-start.2 = ((f32[128,1,128]{2,1,0:T(1,128)}), f32[128,1,128]{2,1,0:T(1,128)S(1)}, u32[]{:S(2)}, u32[]{:S(2)}) async-start(f32[128,1,128]{2,1,0:T(1,128)} %reshape.439), calls=%async_computation.2 | async-start | bytes 131072 | tf_op jit(solution)/shard_map/all_to_all | solution.py:188
  179.6 2.5 reshape.324
  182.2 3.6 %copy.58 = f32[8,16,1024]{2,0,1:T(8,128)} copy(f32[8,16,1024]{1,0,2:T(8,128)} %reshape.324) | data formatting | bytes 1048576 | tf_op jit(solution)/shard_map/reshape | solution.py:192
  185.8 0.2 compare_reduce_fusion
  186.2 4.3 %scatter_custom_fusion.1 = f32[640]{0:T(1024)S(1)} fusion(s32[1024]{0:T(1024)S(1)} %bitcast.140, f32[1024]{0:T(1024)S(1)} %broadcast.364, f32[]{:T(128)} %constant.198.clone.1), kind=kCustom, calls=%fused_computation.113 | custom fusion | bytes 2564 | tf_op jit(solution)/shard_map/scatter | solution.py:211
  190.5 0.5 broadcast.417
  191.0 0.8 reduce.16
  191.8 0.2 reshape.440
  192.2 8.8 %all_gather.7 = f32[32,1024]{1,0:T(8,128)S(1)} all-gather(f32[16,1024]{1,0:T(8,128)S(1)} %copy.62), channel_id=1, replica_groups=mesh['sfc'=128,'lev'=2] {'lev'}, dimensions={0}, use_global_device_ids=true | all-gather | bytes 196608 | tf_op jit(solution)/shard_map/all_gather | solution.py:196
  201.0 0.2 copy.63
  201.2 3.4 %scatter_custom_fusion.2 = f32[32,640]{0,1:T(8,128)S(1)} fusion(s32[1024]{0:T(1024)S(1)} %bitcast.141, f32[1024,32]{1,0:T(8,128)S(1)} %copy.63, f32[]{:T(128)} %constant.198.clone.1), kind=kCustom, calls=%fused_computation.48 | custom fusion | bytes 81924 | tf_op jit(solution)/shard_map/scatter | solution.py:209
  204.7 0.2 reduce_sum.28
  205.1 0.7 broadcast_multiply_fusion.2
  205.9 1.8 all-gather.2.cloned.1.call-done
  207.7 3.7 %copy.59 = f32[1024,8,32]{2,1,0:T(8,128)} copy(f32[1024,8,32]{0,1,2:T(8,128)} %bitcast.128) | data formatting | bytes 2097152 | tf_op jit(solution)/shard_map/all_gather | solution.py:195
  211.4 0.2 broadcast_in_dim.126
  211.6 61.9 %scatter_fusion = f32[8,32,640]{1,0,2:T(8,128)S(1)} fusion(f32[8,32,640]{1,0,2:T(8,128)S(1)} %broadcast_in_dim.126, s32[1024]{0:T(1024)S(1)} %bitcast.142, f32[1024,8,32]{2,1,0:T(8,128)} %copy.59), kind=kCustom, calls=%fused_computation.4 | custom fusion | bytes 3149824 | tf_op jit(solution)/shard_map/scatter | solution.py:206
  273.4 0.8 multiply_reduce_fusion
  274.4 2.0 multiply_add_fusion
  276.3 3.0 %copy.68 = f32[8,32,640]{2,1,0:T(8,128)} copy(f32[8,32,640]{1,0,2:T(8,128)} %multiply_add_fusion) | data formatting | bytes 1310720
  (109 shorter events, 2.5 us)
Async XLA Ops:
  7.2 2.0 copy-start.7
  7.2 2.0 copy-start.4
  7.2 2.0 copy-start.3
  11.8 1.3 copy-start
  11.8 2.5 copy-start.18
  11.9 2.5 copy-start.17
  16.5 23.0 %copy-start.8 = (s32[4,256]{1,0:T(4,128)S(1)}, s32[4,256]{1,0:T(4,128)}, u32[]{:S(2)}) copy-start(s32[4,256]{1,0:T(4,128)} %param.26) | copy-start | bytes 12292
  18.5 22.0 %copy-start.13 = (s32[3]{0:T(128)S(1)}, s32[3]{0:T(128)}, u32[]{:S(2)}) copy-start(s32[3]{0:T(128)} %constant.215) | copy-start | bytes 40
  18.5 22.1 %copy-start.16 = (s32[3]{0:T(128)S(1)}, s32[3]{0:T(128)}, u32[]{:S(2)}) copy-start(s32[3]{0:T(128)} %constant.212) | copy-start | bytes 40
  18.5 43.1 %copy-start.10 = (s32[8,256]{1,0:T(8,128)S(1)}, s32[8,256]{1,0:T(8,128)}, u32[]{:S(2)}) copy-start(s32[8,256]{1,0:T(8,128)} %param.23) | copy-start | bytes 24580
  18.5 43.1 %copy-start.11 = (s32[8,256]{1,0:T(8,128)S(1)}, s32[8,256]{1,0:T(8,128)}, u32[]{:S(2)}) copy-start(s32[8,256]{1,0:T(8,128)} %param.22) | copy-start | bytes 24580
  18.5 43.2 %copy-start.9 = (s32[8,256]{1,0:T(8,128)S(1)}, s32[8,256]{1,0:T(8,128)}, u32[]{:S(2)}) copy-start(s32[8,256]{1,0:T(8,128)} %param.24) | copy-start | bytes 24580
  18.6 43.2 %copy-start.15 = (s32[2]{0:T(128)S(1)}, s32[2]{0:T(128)}, u32[]{:S(2)}) copy-start(s32[2]{0:T(128)} %constant.221) | copy-start | bytes 28
  18.6 43.3 %copy-start.14 = (s32[2]{0:T(128)S(1)}, s32[2]{0:T(128)}, u32[]{:S(2)}) copy-start(s32[2]{0:T(128)} %constant.218) | copy-start | bytes 28
  18.6 43.4 %copy-start.12 = (f32[4,16]{1,0:T(4,128)S(1)}, f32[4,16]{1,0:T(4,128)}, u32[]{:S(2)}) copy-start(f32[4,16]{1,0:T(4,128)} %constant.210.clone) | copy-start | bytes 772
  18.6 43.5 %copy-start.20 = (f32[4,16,1]{1,0,2:T(4,128)S(1)}, f32[4,16,1]{1,0,2:T(4,128)}, u32[]{:S(2)}) copy-start(f32[4,16,1]{1,0,2:T(4,128)} %constant.239) | copy-start | bytes 772
  19.4 65.9 %collective-permute-start = (f32[128,4,64]{0,1,2:T(4,128)S(1)}, f32[128,4,64]{0,1,2:T(4,128)S(1)}, u32[]{:S(2)}, u32[]{:S(2)}) collective-permute-start(f32[128,4,64]{0,1,2:T(4,128)S(1)} %select_bitcast_fusion), channel_id=1, source_target_pairs={{0,2},{2,4},{4,6},{6,8},{8,10},{10,12},{12,14},{14,16},{16,18},{18... | collective-permute-start | bytes 393224 | tf_op jit(solution)/shard_map/ppermute | solution.py:21
  23.4 68.8 %collective-permute-start.1 = (f32[128,4,64]{0,1,2:T(4,128)S(1)}, f32[128,4,64]{0,1,2:T(4,128)S(1)}, u32[]{:S(2)}, u32[]{:S(2)}) collective-permute-start(f32[128,4,64]{0,1,2:T(4,128)S(1)} %select_bitcast_fusion), channel_id=1, source_target_pairs={{2,0},{4,2},{6,4},{8,6},{10,8},{12,10},{14,12},{16,14},{18,16},{20... | collective-permute-start | bytes 393224 | tf_op jit(solution)/shard_map/ppermute | solution.py:21
  24.7 68.8 %collective-permute-start.2 = (f32[128,4,64]{0,1,2:T(4,128)S(1)}, f32[128,4,64]{0,1,2:T(4,128)S(1)}, u32[]{:S(2)}, u32[]{:S(2)}) collective-permute-start(f32[128,4,64]{0,1,2:T(4,128)S(1)} %select_bitcast_fusion), channel_id=1, source_target_pairs={{0,64},{2,66},{4,68},{6,70},{8,72},{10,74},{12,76},{14,78},{16,80}... | collective-permute-start | bytes 393224 | tf_op jit(solution)/shard_map/ppermute | solution.py:21
  34.7 60.3 %collective-permute-start.3 = (f32[128,4,64]{0,1,2:T(4,128)S(1)}, f32[128,4,64]{0,1,2:T(4,128)S(1)}, u32[]{:S(2)}, u32[]{:S(2)}) collective-permute-start(f32[128,4,64]{0,1,2:T(4,128)S(1)} %select_bitcast_fusion), channel_id=1, source_target_pairs={{64,0},{66,2},{68,4},{70,6},{72,8},{74,10},{76,12},{78,14},{80,16}... | collective-permute-start | bytes 393224 | tf_op jit(solution)/shard_map/ppermute | solution.py:21
  36.0 59.1 %collective-permute-start.4 = (f32[128,4,64]{0,1,2:T(4,128)S(1)}, f32[128,4,64]{0,1,2:T(4,128)S(1)}, u32[]{:S(2)}, u32[]{:S(2)}) collective-permute-start(f32[128,4,64]{0,1,2:T(4,128)S(1)} %select_bitcast_fusion), channel_id=1, source_target_pairs={{0,66},{2,68},{4,70},{6,72},{8,74},{10,76},{12,78},{14,80},{16,82}... | collective-permute-start | bytes 393224 | tf_op jit(solution)/shard_map/ppermute | solution.py:21
  45.8 96.8 %all-to-all-start = ((f32[1,128,8]{2,0,1:T(1,128)}), f32[1,128,8]{2,0,1:T(1,128)S(1)}, u32[]{:S(2)}, u32[]{:S(2)}) async-start(f32[1,128,8]{2,0,1:T(1,128)} %copy.55), calls=%async_computation | async-start | bytes 131072 | tf_op jit(solution)/shard_map/all_to_all | solution.py:189
  85.3 9.7 %collective-permute-start.5 = (f32[128,4,64]{0,1,2:T(4,128)S(1)}, f32[128,4,64]{0,1,2:T(4,128)S(1)}, u32[]{:S(2)}, u32[]{:S(2)}) collective-permute-start(f32[128,4,64]{0,1,2:T(4,128)S(1)} %select_bitcast_fusion), channel_id=1, source_target_pairs={{0,62},{2,64},{4,66},{6,68},{8,70},{10,72},{12,74},{14,76},{16,78}... | collective-permute-start | bytes 393224 | tf_op jit(solution)/shard_map/ppermute | solution.py:21
  92.2 9.9 %collective-permute-start.6 = (f32[128,4,64]{0,1,2:T(4,128)S(1)}, f32[128,4,64]{0,1,2:T(4,128)S(1)}, u32[]{:S(2)}, u32[]{:S(2)}) collective-permute-start(f32[128,4,64]{0,1,2:T(4,128)S(1)} %select_bitcast_fusion), channel_id=1, source_target_pairs={{62,0},{64,2},{66,4},{68,6},{70,8},{72,10},{74,12},{76,14},{78,16}... | collective-permute-start | bytes 393224 | tf_op jit(solution)/shard_map/ppermute | solution.py:21
  93.5 11.4 %collective-permute-start.7 = (f32[128,4,64]{0,1,2:T(4,128)S(1)}, f32[128,4,64]{0,1,2:T(4,128)S(1)}, u32[]{:S(2)}, u32[]{:S(2)}) collective-permute-start(f32[128,4,64]{0,1,2:T(4,128)S(1)} %select_bitcast_fusion), channel_id=1, source_target_pairs={{66,0},{68,2},{70,4},{72,6},{74,8},{76,10},{78,12},{80,14},{82,16}... | collective-permute-start | bytes 393224 | tf_op jit(solution)/shard_map/ppermute | solution.py:21
  130.8 1.6 copy-start.1
  130.8 1.6 copy-start.6
  132.4 2.6 copy-start.5
  135.0 1.6 copy-start.19
  135.0 1.6 copy-start.21
  135.2 1.3 copy-start.2
  142.5 30.9 %all-to-all-start.1 = ((f32[128,128,8]{0,2,1:T(8,128)}), f32[128,128,8]{0,2,1:T(8,128)S(1)}, u32[]{:S(2)}, u32[]{:S(2)}) async-start(f32[128,128,8]{0,2,1:T(8,128)} %bitcast.113), calls=%async_computation.1 | async-start | bytes 1048576 | tf_op jit(solution)/shard_map/all_to_all | solution.py:187
  173.4 17.1 %all-to-all-start.2 = ((f32[128,1,128]{2,1,0:T(1,128)}), f32[128,1,128]{2,1,0:T(1,128)S(1)}, u32[]{:S(2)}, u32[]{:S(2)}) async-start(f32[128,1,128]{2,1,0:T(1,128)} %reshape.439), calls=%async_computation.2 | async-start | bytes 131072 | tf_op jit(solution)/shard_map/all_to_all | solution.py:188
  179.6 28.1 %all-gather.2.cloned.1.call-start = ((), (), s32[]{:S(2)}) async-start(), calls=%async_computation.3 | async-start | bytes 1572864 | tf_op jit(solution)/shard_map/all_gather | solution.py:195
Sparse Core Ops, SparseCore 0:
  185.9 21.7 all-gather.1
where the time goes:
time: 290 us; the launch traced here: 286 us
  local copies, waits for them, and re-layouts  151 us (52%)
  starting transfers between devices  67.4 us (23%)
  waiting for transfers between devices  21.7 us (7%)
  between operations  14.9 us (5%)
  other arithmetic  13.8 us (5%)
  blocking collectives  8.8 us (3%)
  matrix products  8.46 us (3%)
    scatter x1, local copies, waits for them, and re-layouts, body(): physics_mixing_ratio = jnp.zeros((tracer_count, level_total, phys_dev), j...  61.9 us
    ppermute x8, starting transfers between devices, passed_along(): return lax.ppermute(shard, axis, pairs)  29.5 us
    gather x2, local copies, waits for them, and re-layouts, body(): jnp.take(stacked, (which * pub_count + pub_slot).reshape(-1), axis=2)  21.4 us
    gather x2, local copies, waits for them, and re-layouts, body(): jnp.take(table, local_code.reshape(-1), axis=2)  21.4 us
    unnamed x66, local copies, waits for them, and re-layouts  20.1 us
    all_to_all x1, starting transfers between devices, body(): lax.all_to_all(send_mix, 'sfc', split_axis=1, concat_axis=1, tiled=True)  15.9 us
    all_to_all x1, starting transfers between devices, body(): lax.all_to_all(send_slot, 'sfc', split_axis=1, concat_axis=1, tiled=True)  15.8 us
    all_to_all x1, waiting for transfers between devices, body(): lax.all_to_all(send_mix, 'sfc', split_axis=1, concat_axis=1, tiled=True)  10.1 us
  transfers between devices with their start and end apart: 12, of which 4 were waited for; matrix products, arithmetic and copies ran while one was open for 31% of the time, Pallas kernels for 0%

commit v1 on v0

v1 whole, which is shorter than its diff:
```python
import functools

import jax
import jax.numpy as jnp
import numpy as np
from jax import lax
from jax.experimental import pallas as pl
from jax.experimental.pallas import tpu as pltpu
from jax.sharding import PartitionSpec as P

F32 = jnp.float32
BF16 = jnp.bfloat16
NPG = 4
DEV_ROWS = 4
SIDE_POINTS = [[0, 1, 2, 3], [3, 7, 11, 15], [12, 13, 14, 15], [0, 4, 8, 12]]
CORNER_POINTS = [0, 3, 12, 15]
CORNER_SIDES = [[(0, 0), (3, 0)], [(0, 3), (1, 0)], [(2, 0), (3, 3)], [(1, 3), (2, 3)]]
EDGE_SLOTS = [(s, m) for s in range(4) for m in (1, 2)]
TIME_STEP = 0.05
TOP_PRESSURE = 1.0
MIXING_RATE = 0.8
PER_SIDE = 16
ROWS = 10


def lagrange_derivative():
    gll_points = np.array([-1.0, -1.0 / np.sqrt(5.0), 1.0 / np.sqrt(5.0), 1.0])
    barycentric = np.array(
        [
            1.0
            / np.prod(
                [gll_points[source] - gll_points[middle] for middle in range(4) if middle != source]
            )
            for source in range(4)
        ]
    )
    derivative = np.zeros((4, 4))
    for target in range(4):
        for source in range(4):
            if target != source:
                derivative[target, source] = (
                    barycentric[source]
                    / barycentric[target]
                    / (gll_points[target] - gll_points[source])
                )
        derivative[target, target] = -np.sum(derivative[target])
    return derivative


def iota(shape, dim):
    return lax.broadcasted_iota(jnp.int32, shape, dim)


def hot(mask):
    return jnp.where(mask, 1.0, 0.0).astype(BF16)


def split(x, axis=0):
    high = x.astype(BF16)
    low = (x - high.astype(F32)).astype(BF16)
    return jnp.concatenate([high, low], axis=axis)


def dot_nn(a, b):
    return lax.dot_general(a, b, (((1,), (0,)), ((), ())), preferred_element_type=F32)


def dot_nt(a, b):
    return lax.dot_general(a, b, (((1,), (1,)), ((), ())), preferred_element_type=F32)


def wide(ref, first=0):
    return jnp.concatenate([ref[first + s : first + s + 1, :] for s in range(4)], axis=1)


def facing(peer, own, block_cols):
    ahead = peer - own
    code = jnp.full_like(peer, -1)
    for number, offset in enumerate((1, -1, block_cols, -block_cols)):
        code = jnp.where(ahead == offset, number, code)
    return jnp.where(peer >= 0, code, -1)


def ranks(direction, entry):
    count = direction.shape[1]
    code = jnp.where(direction >= 0, direction * 64 + entry, -1)
    found = jnp.where(iota((256, count), 0) == code, 1.0, 0.0)
    present = jnp.max(found, axis=1, keepdims=True)
    row, col = iota((256, 256), 0), iota((256, 256), 1)
    before = hot((col < row) & (col // 64 == row // 64))
    below = dot_nn(before, jnp.broadcast_to(present, (256, 128)).astype(BF16))
    rank = jnp.sum(found * below[:, :1], axis=0, keepdims=True)
    return rank.astype(jnp.int32)


def flux_kernel(block_cols, own_ref, tr_ref, lm_ref, wd_ref, sph_ref, peer_ref, slot_ref, x_ref, msg_ref, info_ref):
    half = pl.program_id(0)
    deriv = lagrange_derivative() * TIME_STEP
    levels = lm_ref.shape[0] // 16
    tracers = tr_ref.shape[0] // lm_ref.shape[0]
    elems = peer_ref.shape[1]
    lanes = tr_ref.shape[1]

    def one(t, carry):
        mass, fa, fb = [], [], []
        for k in range(16):
            tr = tr_ref[pl.ds(t * (levels * 16) + k, levels, stride=16), :]
            mk = tr * lm_ref[pl.ds(k, levels, stride=16), :]
            mass.append(mk)
            fa.append(mk * wd_ref[pl.ds(k, levels, stride=16), :])
            fb.append(mk * wd_ref[pl.ds(levels * 16 + k, levels, stride=16), :])
        for k in range(16):
            j, i = k // 4, k % 4
            value = mass[k]
            for other in range(4):
                if abs(deriv[i, other]) > 1e-12:
                    value = value - deriv[i, other] * fa[4 * j + other]
                if abs(deriv[j, other]) > 1e-12:
                    value = value - deriv[j, other] * fb[4 * other + i]
            x_ref[k, pl.ds(pl.multiple_of(t * levels, levels), levels), :] = value * sph_ref[k : k + 1, :]
        return carry

    lax.fori_loop(0, tracers, one, 0)

    @pl.when(half == 0)
    def _():
        direction = facing(wide(peer_ref), own_ref[0], block_cols)
        rank = ranks(direction, jnp.clip(wide(slot_ref), 0, 63))
        usable = (direction >= 0) & (rank < PER_SIDE)
        base = jnp.where(usable, direction * 64 + rank, -1000)
        info_ref[...] = jnp.broadcast_to(base, info_ref.shape)
        msg_ref[...] = jnp.zeros_like(msg_ref)

    lane = iota((256, lanes), 0)
    total = None
    for group in [[pair] for pair in EDGE_SLOTS] + CORNER_SIDES:
        pick = None
        for s, m in group:
            base = info_ref[:1, pl.ds(pl.multiple_of(s * elems + half * lanes, lanes), lanes)]
            here = lane == base + m * PER_SIDE
            pick = here if pick is None else pick | here
        s, m = group[0]
        part = dot_nt(split(x_ref[SIDE_POINTS[s][m]]), hot(pick))
        total = part if total is None else total + part
    fields = total.shape[0] // 2
    msg_ref[...] += total[:fields] + total[fields:]


def local_kernel(block_cols, own_ref, x_ref, peer_ref, slot_ref, flip_ref, pub_ref, info_ref, xd_ref, far_ref, mid_ref):
    own = own_ref[0]
    elems = peer_ref.shape[1]
    fields = x_ref.shape[1]
    sides = 4 * elems
    peer, slot, flip = wide(peer_ref), wide(slot_ref), wide(flip_ref)
    at = iota((1, sides), 1)
    own_code = 4 * (at % elems) + at // elems
    match = jnp.where(pub_ref[...] == own_code, 1.0, 0.0)
    place = jnp.sum(match * iota((64, sides), 0).astype(F32), axis=0, keepdims=True).astype(jnp.int32)
    direction = facing(peer, own, block_cols)
    rank = ranks(direction, place)
    usable = (direction >= 0) & (rank < PER_SIDE)
    start = jnp.where(direction == 0, 64, jnp.where(direction == 1, 0, jnp.where(direction == 2, 192, 128)))
    recv = jnp.where(usable, start + rank, -1000)

    def arrive(s, m):
        cols = slice(s * elems, (s + 1) * elems)
        turned = jnp.where(flip[:, cols] == 1, 3 - m, m)
        return recv[:, cols] + turned * PER_SIDE

    lane = iota((256, elems), 0)
    corner_far = []
    for c in range(4):
        (sa, ma), (sb, mb) = CORNER_SIDES[c]
        corner_far.append(hot((lane == arrive(sa, ma)) | (lane == arrive(sb, mb))))
    corner_far = jnp.concatenate(corner_far, axis=1)
    for number, (s, m) in enumerate(EDGE_SLOTS):
        far_ref[4 + number] = hot(lane == arrive(s, m))
    base = info_ref[:1, :]
    second = jnp.where(base >= 128, base - 128, -1000)
    lane128 = iota((128, elems), 0)
    sent = []
    for c in range(4):
        pick = None
        for s, m in CORNER_SIDES[c]:
            here = lane128 == second[:, s * elems : (s + 1) * elems] + m * PER_SIDE
            pick = here if pick is None else pick | here
        sent.append(hot(pick))
    mid_ref[...] = dot_nt(corner_far[:128], jnp.concatenate(sent, axis=1)).astype(BF16)

    local = peer == own
    slot_c = jnp.clip(slot, 0, 4 * elems - 1)
    near = jnp.where(local, slot_c % 4 * elems + slot_c // 4, -1)

    def corner_source(code, end, ok):
        side = code % 4
        corner = jnp.where(side == 1, 1, jnp.where(side == 2, 2, 0)) + end * jnp.where(side % 2 == 1, 2, 1)
        return jnp.where(ok, corner * elems + code // 4, -1)

    cpeer, cslot, cflip = wide(peer_ref, 4), wide(slot_ref, 4), wide(flip_ref, 4)
    third = corner_source(jnp.clip(cslot, 0, 4 * elems - 1), cflip, cpeer == own)
    source = iota((sides, elems), 0)
    corners = jnp.concatenate([x_ref[p] for p in CORNER_POINTS], axis=1)
    corners_hl = split(corners)
    lhs = jnp.concatenate([corners_hl, corner_far], axis=0)
    for c in range(4):
        cols = slice(c * elems, (c + 1) * elems)
        weight = jnp.where(source == third[:, cols], 1.0, 0.0)
        for s, m in CORNER_SIDES[c]:
            own_cols = slice(s * elems, (s + 1) * elems)
            end = jnp.where(flip[:, own_cols] == 1, 1 - m // 3, m // 3)
            code = corner_source(slot_c[:, own_cols], end, local[:, own_cols])
            weight = weight + jnp.where(source == code, 1.0, 0.0)
        got = dot_nn(lhs, weight.astype(BF16))
        xd_ref[CORNER_POINTS[c]] = corners[:, cols] + got[:fields] + got[fields : 2 * fields]
        far_ref[c] = corner_far[:, cols] + got[2 * fields :].astype(BF16)
    inner = []
    for m in (1, 2):
        inner.append(split(jnp.concatenate([x_ref[SIDE_POINTS[s][m]] for s in range(4)], axis=1)))
    inner = jnp.concatenate(inner, axis=0)
    for s in range(4):
        cols = slice(s * elems, (s + 1) * elems)
        got = dot_nn(inner, hot(source == near[:, cols]))
        one = got[:fields] + got[fields : 2 * fields]
        two = got[2 * fields : 3 * fields] + got[3 * fields :]
        turned = flip[:, cols] == 1
        for m, mine, swapped in ((1, one, two), (2, two, one)):
            p = SIDE_POINTS[s][m]
            xd_ref[p] = x_ref[p] + jnp.where(turned, swapped, mine)
    for p in (5, 6, 9, 10):
        xd_ref[p] = x_ref[p]


def merge(odd, a, b):
    low = iota(a.shape, 1) < 64
    lower = jnp.where(odd == 1, a, b)
    upper = jnp.where(odd == 1, b, a)
    return jnp.where(low, lower, upper)


def middle_kernel(odd_ref, a_ref, b_ref, msg_ref, mid_ref, got_ref, out_ref):
    got = merge(odd_ref[0], a_ref[...], b_ref[...])
    got_ref[...] = got
    fields = got.shape[0]
    add = dot_nn(split(got), mid_ref[...])
    out_ref[...] = msg_ref[:, 128:] + add[:fields] + add[fields:]


def sort_kernel(group_width, slot_ref, lmn_a_ref, lmn_b_ref, sph_ref, order_ref, rden_ref, rows_ref):
    elems = sph_ref.shape[1]
    levels = lmn_a_ref.shape[0] // 16
    sph = sph_ref[...]
    thicks = []
    for c in range(4):
        den, area = None, None
        for k in range(16):
            if 2 * (k // 8) + k % 4 // 2 != c:
                continue
            weight = sph[k : k + 1, :]
            term = [ref[pl.ds(k, levels, stride=16), :] for ref in (lmn_a_ref, lmn_b_ref)]
            term = jnp.concatenate(term, axis=1) * weight
            den = term if den is None else den + term
            area = weight if area is None else area + weight
        rden_ref[c] = 1.0 / den
        thicks.append(den / area)
    thick = jnp.concatenate(thicks, axis=1)
    total = 4 * elems
    slot = wide(slot_ref)
    slot_f = slot.astype(F32)
    dest = jnp.floor((slot_f + 0.5) * (1.0 / group_width)).astype(jnp.int32)
    within = (slot - dest * group_width).astype(F32)
    peers = rows_ref.shape[1]
    to = jnp.where(iota((peers, total), 0) == dest, 1.0, 0.0)
    to_b = to.astype(BF16)
    upto = hot(iota((128, 128), 0) < iota((128, 128), 1))
    base = jnp.zeros((peers, 1), F32)
    parts = []
    for block in range(total // 128):
        cols = slice(block * 128, block * 128 + 128)
        parts.append(dot_nn(to_b[:, cols], upto) + base)
        base = base + jnp.sum(to[:, cols], axis=1, keepdims=True)
    rank = jnp.sum(to * jnp.concatenate(parts, axis=1), axis=0, keepdims=True).astype(jnp.int32)
    key = dest * 8 + rank
    for block in range(total // 128):
        order_ref[block * 128 : block * 128 + 128, :] = hot(iota((128, total), 0) + block * 128 == key)
    at = iota((128, total), 0)
    spread = jnp.where(at // levels == rank, jnp.concatenate([thick] * (128 // levels), axis=0), 0.0)
    ids = jnp.where(at == rank, within, 0.0)
    both = jnp.concatenate([split(spread), split(ids)], axis=0)
    got = dot_nt(to_b, both)
    rows_ref[0] = got[:, :128] + got[:, 128:256]
    rows_ref[1] = got[:, 256:384] + got[:, 384:]


def finish_kernel(
    odd_ref, xd_ref, one_ref, a_ref, b_ref, far_ref, sph_ref, inv_ref, rden_ref, order_ref, rows_ref, tm_ref, out_ref, mix_ref
):
    half = pl.program_id(0)
    fields, lanes = xd_ref.shape[1], xd_ref.shape[2]
    levels = rden_ref.shape[1]
    two = merge(odd_ref[0], a_ref[...], b_ref[...])
    got = split(jnp.concatenate([one_ref[...], two], axis=1))
    number = {p: c for c, p in enumerate(CORNER_POINTS)}
    for index, (s, m) in enumerate(EDGE_SLOTS):
        number[SIDE_POINTS[s][m]] = 4 + index
    sums = [None] * 4
    for k in range(16):
        value = xd_ref[k]
        if k in number:
            far = dot_nn(got, far_ref[number[k]])
            value = value + far[:fields] + far[fields:]
        value = value * inv_ref[k : k + 1, :]
        tm_ref[pl.ds(k, fields, stride=16), :] = value
        c = 2 * (k // 8) + k % 4 // 2
        term = value * sph_ref[k : k + 1, :]
        sums[c] = term if sums[c] is None else sums[c] + term
    for c in range(4):
        mix = sums[c] * jnp.concatenate([rden_ref[c]] * (fields // levels), axis=0)
        mix_ref[:, pl.ds(pl.multiple_of(c * 2 * lanes + half * lanes, lanes), lanes)] = split(mix)

    @pl.when(half == 1)
    def _():
        mix_hl = mix_ref[...]
        peers = rows_ref.shape[1]
        chunk = 128
        for block in range(peers * 8 // chunk):
            res = dot_nt(order_ref[block * chunk : (block + 1) * chunk, :], mix_hl)
            res = res[:, :fields] + res[:, fields:]
            for d in range(chunk // 8):
                row = (block * (chunk // 8) + d) * ROWS
                out_ref[row : row + 8, :] = res[d * 8 : d * 8 + 8, :]
        out_ref[pl.ds(8, peers, stride=ROWS), :] = rows_ref[0]
        out_ref[pl.ds(9, peers, stride=ROWS), :] = rows_ref[1]


def physics_kernel(lev_ref, own_ref, par_ref, mix_ref, sig_ref):
    lev = lev_ref[0]
    total, fields = own_ref.shape
    peers = total // ROWS
    levels2, slots = sig_ref.shape
    levels = levels2 // 2
    tracers = fields // levels
    first = jnp.where(lev == 0, own_ref[...], par_ref[...])
    last = jnp.where(lev == 0, par_ref[...], own_ref[...])
    thick_own = own_ref[pl.ds(8, peers, stride=ROWS), :]
    thick_par = par_ref[pl.ds(8, peers, stride=ROWS), :]
    thick_first = jnp.where(lev == 0, thick_own, thick_par)
    thick_last = jnp.where(lev == 0, thick_par, thick_own)
    ids = own_ref[pl.ds(9, peers, stride=ROWS), :]
    at = iota((peers, total), 1)
    spread = hot(at // ROWS == iota((peers, total), 0))
    ids_t = jnp.transpose(ids)[:16, :]
    cand = dot_nn(split(ids_t), spread)
    cand = cand[:16] + cand[16:]
    spot = iota((16, total), 1) % ROWS
    key = jnp.sum(jnp.where((spot == iota((16, total), 0)) & (spot < 8), cand, 0.0), axis=0, keepdims=True)
    key = jnp.where(iota((1, total), 1) % ROWS < 8, key, -1e6).astype(jnp.int32)
    key = key - lev * slots
    spread_t = hot(iota((total, peers), 0) // ROWS == iota((total, peers), 1))
    thick_hl = jnp.concatenate([split(thick_first, axis=1), split(thick_last, axis=1)], axis=1)
    rows = dot_nn(spread_t, thick_hl)
    keep = iota((total, 128), 1) // levels == iota((total, 128), 0) % ROWS
    fold_row = iota((128, 128), 0) % levels
    fold_col = iota((128, 128), 1)
    narrow = None
    for number in range(2):
        mine = rows[:, number * 256 : number * 256 + 128] + rows[:, number * 256 + 128 : number * 256 + 256]
        mine = split(jnp.where(keep, mine, 0.0), axis=0)
        fold = hot(fold_col == fold_row + number * levels)
        part = dot_nn(mine, fold)
        part = part[:total] + part[total:]
        narrow = part if narrow is None else narrow + part
    narrow = jnp.where(iota((total, 128), 1) == levels2, 1.0, narrow)
    stack = jnp.concatenate([first, last, narrow], axis=1)
    stack = split(stack, axis=1)
    width = 2 * fields + 128
    chunk = 128
    outs = []
    for block in range(slots // chunk):
        pick = hot(iota((chunk, total), 0) + block * chunk == key)
        got = dot_nn(pick, stack)
        outs.append(jnp.transpose(got[:, :width] + got[:, width:]))
    for block in range(slots // chunk):
        got = outs[block]
        cols = slice(block * chunk, (block + 1) * chunk)
        thick = got[2 * fields : 2 * fields + levels2]
        live = got[2 * fields + levels2 : 2 * fields + levels2 + 1]
        running = jnp.zeros_like(live)
        above = []
        for level in range(levels2):
            above.append(running)
            running = running + thick[level : level + 1]
        above = jnp.concatenate(above, axis=0)
        scale = live / (TOP_PRESSURE + running)
        sigma = (TOP_PRESSURE + above + 0.5 * thick) * scale
        sig_ref[:, cols] = sigma
        share = 1.0 / (running + 1.0 - live)
        for t in range(tracers):
            mix = jnp.concatenate(
                [got[t * levels : (t + 1) * levels], got[fields + t * levels : fields + (t + 1) * levels]], axis=0
            )
            mean = jnp.sum(thick * mix, axis=0, keepdims=True) * share
            mix_ref[t * levels2 : (t + 1) * levels2, cols] = mix + MIXING_RATE * sigma * (mean - mix)


def whole(shape):
    if shape == (1,):
        return pl.BlockSpec(memory_space=pltpu.SMEM)
    return pl.BlockSpec(shape, lambda i: (0,) * len(shape))


def halved(shape, fixed=None):
    lead = (0,) * (len(shape) - 1)
    block = shape[:-1] + (shape[-1] // 2,)
    return pl.BlockSpec(block, lambda i: lead + ((i if fixed is None else fixed),))


def call(kernel, outs, ins, steps=1, ins_half=None, outs_half=(), scratch=(), vmem=40):
    ins_half = ins_half or {}
    in_specs, out_specs = [], []
    for number, value in enumerate(ins):
        if number in ins_half:
            in_specs.append(halved(value.shape, ins_half[number]))
        else:
            in_specs.append(whole(value.shape))
    for number, (shape, kind) in enumerate(outs):
        out_specs.append(halved(shape) if number in outs_half else whole(shape))
    return pl.pallas_call(
        kernel,
        grid=(steps,),
        out_shape=[jax.ShapeDtypeStruct(shape, kind) for shape, kind in outs],
        in_specs=in_specs,
        out_specs=out_specs,
        scratch_shapes=list(scratch),
        compiler_params=pltpu.CompilerParams(vmem_limit_bytes=vmem * 1024 * 1024),
    )(*ins)


def swap(value, step, parity, count, row=None):
    pairs = []
    for i in range(count - step):
        if i // step % 2 == parity and (row is None or i // row == (i + step) // row):
            pairs += [(i, i + step), (i + step, i)]
    return lax.ppermute(value, "sfc", pairs)


def body(
    tracers,
    layer_mass,
    layer_mass_next,
    wind,
    spheremp,
    inverse_mass,
    rec_peer,
    rec_slot,
    rec_flip,
    publish_list,
    column_slot_table,
):
    own_index = lax.axis_index("sfc").astype(jnp.int32)
    lev_index = lax.axis_index("lev").astype(jnp.int32)
    sfc_count = lax.axis_size("sfc")
    lev_count = lax.axis_size("lev")
    tracer_count, level_count, points, elems = tracers.shape
    fields = tracer_count * level_count
    block_cols = sfc_count // DEV_ROWS
    own = own_index.reshape(1)
    col_odd = (own_index % block_cols % 2).reshape(1)
    row_odd = (own_index // block_cols % 2).reshape(1)

    weighted, message, info = call(
        functools.partial(flux_kernel, block_cols),
        [((points, fields, elems), F32), ((fields, 256), F32), ((8, 4 * elems), jnp.int32)],
        [
            own,
            tracers.reshape(fields * points, elems),
            layer_mass.reshape(level_count * points, elems),
            wind.reshape(2 * level_count * points, elems),
            spheremp,
            rec_peer,
            rec_slot,
        ],
        steps=2,
        ins_half={1: None, 2: None, 3: None, 4: None},
        outs_half=(0,),
    )
    first = message[:, :128]
    near_a = swap(first, 1, 0, sfc_count, block_cols)
    near_b = swap(first, 1, 1, sfc_count, block_cols)
    local, far, mid = call(
        functools.partial(local_kernel, block_cols),
        [((points, fields, elems), F32), ((12, 256, elems), BF16), ((128, 128), BF16)],
        [own, weighted, rec_peer, rec_slot, rec_flip, publish_list.reshape(-1, 1), info],
    )
    got_one, second = call(
        middle_kernel,
        [((fields, 128), F32), ((fields, 128), F32)],
        [col_odd, near_a, near_b, message, mid],
    )
    over_a = swap(second, block_cols, 0, sfc_count)
    over_b = swap(second, block_cols, 1, sfc_count)
    group_width = 5 * NPG * elems // 4
    next_mass = layer_mass_next.reshape(level_count * points, elems)
    order, rden, rows = call(
        functools.partial(sort_kernel, group_width),
        [((NPG * elems, NPG * elems), BF16), ((NPG, level_count, elems), F32), ((2, sfc_count, 128), F32)],
        [column_slot_table, next_mass, next_mass, spheremp],
        ins_half={1: 0, 2: 1},
    )
    mass, send = call(
        finish_kernel,
        [((fields * points, elems), F32), ((ROWS * sfc_count, fields), F32)],
        [row_odd, local, got_one, over_a, over_b, far, spheremp, inverse_mass, rden, order, rows],
        steps=2,
        ins_half={1: None, 5: None, 6: None, 7: None, 8: None},
        outs_half=(0,),
        scratch=[pltpu.VMEM((2 * fields, NPG * elems), BF16)],
    )
    moved = lax.all_to_all(
        send.reshape(sfc_count, 1, ROWS * fields), "sfc", split_axis=0, concat_axis=0, tiled=True
    ).reshape(ROWS * sfc_count, fields)
    other = lax.ppermute(moved, "lev", [(0, 1), (1, 0)])
    slots = group_width // lev_count
    levels = level_count * lev_count
    mixed, sigma = call(
        physics_kernel,
        [((tracer_count * levels, slots), F32), ((levels, slots), F32)],
        [lev_index.reshape(1), moved, other],
    )
    return (
        mass.reshape(tracers.shape),
        mixed.reshape(tracer_count, levels, slots),
        sigma,
    )


def solution(mesh):
    in_specs = (
        P(None, "lev", None, "sfc"),
        P("lev", None, "sfc"),
        P("lev", None, "sfc"),
        P(None, "lev", None, "sfc"),
        P(None, "sfc"),
        P(None, "sfc"),
        P(None, "sfc"),
        P(None, "sfc"),
        P(None, "sfc"),
        P("sfc"),
        P(None, "sfc"),
    )
    out_specs = (
        P(None, "lev", None, "sfc"),
        P(None, None, ("sfc", "lev")),
        P(None, ("sfc", "lev")),
    )
    return jax.shard_map(body, mesh=mesh, in_specs=in_specs, out_specs=out_specs, check_vma=False)
```

time: 290 us -> 84.4 us (0.29); the launches traced: 286 us -> 83.9 us
  local copies, waits for them, and re-layouts: 151 us -> 11.3 us
  starting transfers between devices: 67.4 us -> 19.7 us
  blocking collectives: 8.8 us -> 30.5 us
  waiting for transfers between devices: 21.7 us -> 1.92 us
  Pallas kernels: 0 us -> 19.7 us
  between operations: 14.9 us -> 0.77 us
  other arithmetic: 13.8 us -> 0 us
  matrix products: 8.46 us -> 0 us
    scatter x5 -> x0, local copies, waits for them, and re-layouts: 70.5 us -> none  [the longest x1 61.9 us: body(): physics_mixing_ratio = jnp.zeros((tracer_count, level_total, phys_dev), j...]
    gather x6 -> x0, local copies, waits for them, and re-layouts: 45.4 us -> none  [the longest x2 21.4 us: body(): jnp.take(stacked, (which * pub_count + pub_slot).reshape(-1), axis=2)]
    all_to_all x3 -> x0, starting transfers between devices: 37.8 us -> none  [the longest x1 15.9 us: body(): lax.all_to_all(send_mix, 'sfc', split_axis=1, concat_axis=1, tiled=True)]
    all_to_all x0 -> x1, blocking collectives: none -> 30.5 us  [body(): lax.all_to_all(send.reshape(sfc_count, 1, ROWS * fields), 'sfc', split_ax...]
    pallas_call x0 -> x6, Pallas kernels: none -> 19.7 us  [call(): pl.pallas_call(kernel, grid=(steps,), out_shape=[jax.ShapeDtypeStruct(sha...]
    all_to_all x3 -> x0, waiting for transfers between devices: 10.1 us -> none  [the longest x1 10.1 us: body(): lax.all_to_all(send_mix, 'sfc', split_axis=1, concat_axis=1, tiled=True)]
    ppermute x8 -> x5, starting transfers between devices: 29.5 us -> 19.7 us  [the longest x4 14.6 us: swap(): return lax.ppermute(value, 'sfc', pairs)]
    unnamed x66 -> x36, local copies, waits for them, and re-layouts: 20.1 us -> 11.2 us
  transfers between devices with their start and end apart: 12 -> 5, of which waited for: 4 -> 2; matrix products, arithmetic and copies ran while one was open for 31% -> 0% of each run, Pallas kernels for 0% -> 7%
where the time goes in v1:
time: 84.4 us; the launch traced here: 83.9 us
  blocking collectives  30.5 us (36%)
  Pallas kernels  19.7 us (23%)
  starting transfers between devices  19.7 us (23%)
  local copies, waits for them, and re-layouts  11.3 us (13%)
  waiting for transfers between devices  1.92 us (2%)
    all_to_all x1, blocking collectives, body(): lax.all_to_all(send.reshape(sfc_count, 1, ROWS * fields), 'sfc', split_ax...  30.5 us
    pallas_call x6, Pallas kernels, call(): pl.pallas_call(kernel, grid=(steps,), out_shape=[jax.ShapeDtypeStruct(sha...  19.7 us
    ppermute x4, starting transfers between devices, swap(): return lax.ppermute(value, 'sfc', pairs)  14.6 us
    unnamed x36, local copies, waits for them, and re-layouts  11.2 us
    ppermute x1, starting transfers between devices, body(): other = lax.ppermute(moved, 'lev', [(0, 1), (1, 0)])  5.13 us
    ppermute x1, waiting for transfers between devices, body(): other = lax.ppermute(moved, 'lev', [(0, 1), (1, 0)])  1.72 us
  transfers between devices with their start and end apart: 5, of which 2 were waited for; matrix products, arithmetic and copies ran while one was open for 0% of the time, Pallas kernels for 7%

profile of v1, /device:TPU:1, one launch (start us, length us, event | category | flops | bytes accessed | tf_op | source)
XLA Modules:
  0.0 83.9 jit_solution(5060108805613818114)
XLA Ops:
  0.6 0.0 copy-start.11
  0.6 0.0 copy-start.17
  0.7 0.0 copy-start
  0.7 1.6 %copy-done = f32[8,16,16,256]{3,2,1,0:T(8,128)S(1)} copy-done((f32[8,16,16,256]{3,2,1,0:T(8,128)S(1)}, f32[8,16,16,256]{3,2,1,0:T(8,128)}, u32[]{:S(2)}) %copy-start) | copy-done | bytes 2097176
  2.3 0.0 copy-start.6
  2.3 1.0 %copy-done.6 = f32[2,16,16,256]{3,2,1,0:T(8,128)S(1)} copy-done((f32[2,16,16,256]{3,2,1,0:T(8,128)S(1)}, f32[2,16,16,256]{3,2,1,0:T(8,128)}, u32[]{:S(2)}) %copy-start.6) | copy-done | bytes 524312
  3.3 0.0 copy-start.7
  3.3 0.9 %copy-done.7 = f32[16,16,256]{2,1,0:T(8,128)S(1)} copy-done((f32[16,16,256]{2,1,0:T(8,128)S(1)}, f32[16,16,256]{2,1,0:T(8,128)}, u32[]{:S(2)}) %copy-start.7) | copy-done | bytes 262168
  4.2 0.0 copy-start.8
  4.3 0.7 copy-done.8
  5.0 0.0 copy-start.10
  5.0 0.7 copy-done.10
  5.7 0.0 copy-start.12
  5.7 0.7 copy-done.12
  6.4 0.0 copy-start.13
  6.4 0.0 copy-start.15
  6.4 0.0 copy-start.5
  6.4 5.4 %shard_map.130 = (f32[16,128,256]{2,1,0:T(8,128)S(1)}, f32[128,256]{1,0:T(8,128)S(1)}, s32[8,1024]{1,0:T(8,128)S(1)}) custom-call(s32[1]{0:T(128)} %bitcast.1.own_ref, f32[2048,256]{1,0:T(8,128)S(1)} %bitcast.15, f32[256,256]{1,0:T(8,128)S(1)} %bitcast.20, f32[512,256]{1,0:T(8,128)S(1)} %bitcast.19, f32[16,256]{1,0:T(8,128)S(1)} %copy-done.8, ...), custom_call_target="tpu_custom_call" | custom-call | tf_op jit(solution)/shard_map/pallas_call | solution.py:427
  11.8 0.0 copy-start.1
  11.8 1.3 %copy-done.1 = f32[16,128,256]{2,1,0:T(8,128)} copy-done((f32[16,128,256]{2,1,0:T(8,128)}, f32[16,128,256]{2,1,0:T(8,128)S(1)}, u32[]{:S(2)}) %copy-start.1) | copy-done | bytes 2097176
  13.1 0.0 copy-start.9
  13.1 0.0 copy-start.16
  13.1 0.0 copy-start.14
  13.1 0.8 collective-permute-start.1
  13.9 4.6 %collective-permute-start = (f32[128,128]{1,0:T(8,128)S(1)}, f32[128,128]{1,0:T(8,128)S(1)}, u32[]{:S(2)}, u32[]{:S(2)}) collective-permute-start(f32[128,128]{1,0:T(8,128)S(1)} %slice.3), channel_id=1, source_target_pairs={{0,2},{2,0},{4,6},{6,4},{8,10},{10,8},{12,14},{14,12},{16,18},{18,... | collective-permute-start | bytes 196616 | tf_op jit(solution)/shard_map/ppermute | solution.py:443
  18.5 0.0 copy-done.17
  18.5 0.1 copy.15.pub_ref
  18.6 0.0 copy-done.11
  18.6 0.0 copy-done.13
  18.6 0.0 copy-done.15
  18.6 0.0 copy-start.2
  18.6 1.6 %copy-done.2 = f32[16,128,256]{2,1,0:T(8,128)S(1)} copy-done((f32[16,128,256]{2,1,0:T(8,128)S(1)}, f32[16,128,256]{2,1,0:T(8,128)}, u32[]{:S(2)}) %copy-start.2) | copy-done | bytes 2097176
  20.2 4.5 %shard_map.131 = (f32[16,128,256]{2,1,0:T(8,128)S(1)}, bf16[12,256,256]{2,1,0:T(8,128)(2,1)S(1)}, bf16[128,128]{1,0:T(8,128)(2,1)S(1)}) custom-call(s32[1]{0:T(128)} %bitcast.1.own_ref, f32[16,128,256]{2,1,0:T(8,128)S(1)} %copy-done.2, s32[8,256]{1,0:T(8,128)S(1)} %copy-done.11, s32[8,256]{1,0:T(8,128)S(1)} %copy-done.13, s32[8,256]{1,0:T(8,128)S(1)} %copy-done.15, ...), custom_call_target="tpu_custom_call" | custom-call | tf_op jit(solution)/shard_map/pallas_call | solution.py:427
  24.7 0.0 copy-start.3
  24.8 1.1 %copy-done.3 = bf16[12,256,256]{2,1,0:T(8,128)(2,1)} copy-done((bf16[12,256,256]{2,1,0:T(8,128)(2,1)}, bf16[12,256,256]{2,1,0:T(8,128)(2,1)S(1)}, u32[]{:S(2)}) %copy-start.3) | copy-done | bytes 1572888
  25.9 0.0 collective-permute-done.1.b_ref
  25.9 0.0 collective-permute-done.a_ref
  25.9 0.2 shard_map.132
  26.0 0.7 collective-permute-start.3
  26.7 8.5 %collective-permute-start.2 = (f32[128,128]{1,0:T(8,128)S(1)}, f32[128,128]{1,0:T(8,128)S(1)}, u32[]{:S(2)}, u32[]{:S(2)}) collective-permute-start(f32[128,128]{1,0:T(8,128)S(1)} %get-tuple-element.24), channel_id=1, source_target_pairs={{0,64},{64,0},{2,66},{66,2},{4,68},{68,4},{6,70},{70,6},{8,72},{72... | collective-permute-start | bytes 196616 | tf_op jit(solution)/shard_map/ppermute | solution.py:443
  35.2 0.0 copy-done.5
  35.3 0.0 copy-done.9
  35.3 0.0 copy-done.16
  35.3 1.4 %shard_map.133 = (bf16[1024,1024]{1,0:T(8,128)(2,1)S(1)}, f32[4,16,256]{2,1,0:T(8,128)S(1)}, f32[2,128,128]{2,1,0:T(8,128)S(1)}) custom-call(s32[4,256]{1,0:T(4,128)S(1)} %copy-done.16, f32[256,256]{1,0:T(8,128)S(1)} %bitcast.16, f32[256,256]{1,0:T(8,128)S(1)} %bitcast.17, f32[16,256]{1,0:T(8,128)S(1)} %copy-done.9), custom_call_target="tpu_custom_call" | custom-call | tf_op jit(solution)/shard_map/pallas_call | solution.py:427
  36.7 0.0 collective-permute-done.3.b_ref
  36.7 0.2 collective-permute-done.2.a_ref
  36.9 0.0 copy-done.14
  36.9 0.0 copy-start.4
  36.9 1.4 %copy-done.4 = bf16[12,256,256]{2,1,0:T(8,128)(2,1)S(1)} copy-done((bf16[12,256,256]{2,1,0:T(8,128)(2,1)S(1)}, bf16[12,256,256]{2,1,0:T(8,128)(2,1)}, u32[]{:S(2)}) %copy-start.4) | copy-done | bytes 1572888
  38.3 4.5 %shard_map.134 = (f32[2048,256]{1,0:T(8,128)}, f32[1280,128]{1,0:T(8,128)S(1)}) custom-call(s32[1]{0:T(128)} %bitcast.odd_ref, f32[16,128,256]{2,1,0:T(8,128)S(1)} %get-tuple-element.20.xd_ref, f32[128,128]{1,0:T(8,128)S(1)} %get-tuple-element.23.one_ref, f32[128,128]{1,0:T(8,128)S(1)} %collective-permute-done.2.a_ref, ...), custom_call_target="tpu_custom_call" | custom-call | tf_op jit(solution)/shard_map/pallas_call | solution.py:427
  42.8 30.5 %all_to_all.5 = f32[128,1,1280]{2,1,0:T(1,128)S(1)} all-to-all(f32[128,1,1280]{2,1,0:T(1,128)S(1)} %bitcast.18), channel_id=1, replica_groups=mesh['sfc'=128,'lev'=2] {'sfc'}, dimensions={0} | all-to-all | bytes 1310720 | tf_op jit(solution)/shard_map/all_to_all | solution.py:518
  73.3 5.1 %collective-permute-start.4 = (f32[1280,128]{1,0:T(8,128)S(1)}, f32[1280,128]{1,0:T(8,128)S(1)}, u32[]{:S(2)}, u32[]{:S(2)}) collective-permute-start(f32[1280,128]{1,0:T(8,128)S(1)} %bitcast.13), channel_id=1, source_target_pairs={{0,1},{1,0},{2,3},{3,2},{4,5},{5,4},{6,7},{7,6},{8,9},{9,8},{10,11... | collective-permute-start | bytes 1966088 | tf_op jit(solution)/shard_map/ppermute | solution.py:521
  78.4 1.7 %collective-permute-done.4.par_ref = f32[1280,128]{1,0:T(8,128)S(1)} collective-permute-done((f32[1280,128]{1,0:T(8,128)S(1)}, f32[1280,128]{1,0:T(8,128)S(1)}, u32[]{:S(2)}, u32[]{:S(2)}) %collective-permute-start.4) | collective-permute-done | bytes 655392 | tf_op jit(solution)/shard_map/ppermute | solution.py:521
  80.1 3.7 %shard_map.135 = (f32[256,640]{1,0:T(8,128)}, f32[32,640]{1,0:T(8,128)}) custom-call(s32[1]{0:T(128)} %bitcast.9.lev_ref, f32[1280,128]{1,0:T(8,128)S(1)} %bitcast.14, f32[1280,128]{1,0:T(8,128)S(1)} %collective-permute-done.4.par_ref), custom_call_target="tpu_custom_call" | custom-call | tf_op jit(solution)/shard_map/pallas_call | solution.py:427
  (1 shorter events, 0.0 us)
Async XLA Ops:
  0.6 17.9 %copy-start.11 = (s32[8,256]{1,0:T(8,128)S(1)}, s32[8,256]{1,0:T(8,128)}, u32[]{:S(2)}) copy-start(s32[8,256]{1,0:T(8,128)} %peer_ref.3) | copy-start | bytes 24580
  0.6 17.8 %copy-start.17 = (s32[64]{0:T(128)S(1)}, s32[64]{0:T(128)}, u32[]{:S(2)}) copy-start(s32[64]{0:T(128)} %param.20) | copy-start | bytes 772
  0.7 1.6 %copy-start = (f32[8,16,16,256]{3,2,1,0:T(8,128)S(1)}, f32[8,16,16,256]{3,2,1,0:T(8,128)}, u32[]{:S(2)}) copy-start(f32[8,16,16,256]{3,2,1,0:T(8,128)} %param.11) | copy-start | bytes 6291460
  2.3 1.0 %copy-start.6 = (f32[2,16,16,256]{3,2,1,0:T(8,128)S(1)}, f32[2,16,16,256]{3,2,1,0:T(8,128)}, u32[]{:S(2)}) copy-start(f32[2,16,16,256]{3,2,1,0:T(8,128)} %param.14) | copy-start | bytes 1572868
  3.3 0.9 %copy-start.7 = (f32[16,16,256]{2,1,0:T(8,128)S(1)}, f32[16,16,256]{2,1,0:T(8,128)}, u32[]{:S(2)}) copy-start(f32[16,16,256]{2,1,0:T(8,128)} %param.12) | copy-start | bytes 786436
  4.2 0.7 copy-start.8
  5.0 0.7 copy-start.10
  5.7 0.7 copy-start.12
  6.4 12.2 %copy-start.13 = (s32[8,256]{1,0:T(8,128)S(1)}, s32[8,256]{1,0:T(8,128)}, u32[]{:S(2)}) copy-start(s32[8,256]{1,0:T(8,128)} %slot_ref.4) | copy-start | bytes 24580
  6.4 12.2 %copy-start.15 = (s32[8,256]{1,0:T(8,128)S(1)}, s32[8,256]{1,0:T(8,128)}, u32[]{:S(2)}) copy-start(s32[8,256]{1,0:T(8,128)} %flip_ref.1) | copy-start | bytes 24580
  6.4 28.9 %copy-start.5 = (f32[16,16,256]{2,1,0:T(8,128)S(1)}, f32[16,16,256]{2,1,0:T(8,128)}, u32[]{:S(2)}) copy-start(f32[16,16,256]{2,1,0:T(8,128)} %param.13) | copy-start | bytes 786436
  11.8 1.3 %copy-start.1 = (f32[16,128,256]{2,1,0:T(8,128)}, f32[16,128,256]{2,1,0:T(8,128)S(1)}, u32[]{:S(2)}) copy-start(f32[16,128,256]{2,1,0:T(8,128)S(1)} %get-tuple-element.18.x_ref) | copy-start | bytes 6291460
  13.1 22.2 %copy-start.9 = (f32[16,256]{1,0:T(8,128)S(1)}, f32[16,256]{1,0:T(8,128)}, u32[]{:S(2)}) copy-start(f32[16,256]{1,0:T(8,128)} %sph_ref.5) | copy-start | bytes 49156
  13.1 22.2 %copy-start.16 = (s32[4,256]{1,0:T(4,128)S(1)}, s32[4,256]{1,0:T(4,128)}, u32[]{:S(2)}) copy-start(s32[4,256]{1,0:T(4,128)} %slot_ref.5) | copy-start | bytes 12292
  13.1 23.8 %copy-start.14 = (f32[16,256]{1,0:T(8,128)S(1)}, f32[16,256]{1,0:T(8,128)}, u32[]{:S(2)}) copy-start(f32[16,256]{1,0:T(8,128)} %inv_ref.1) | copy-start | bytes 49156
  13.1 12.8 %collective-permute-start.1 = (f32[128,128]{1,0:T(8,128)S(1)}, f32[128,128]{1,0:T(8,128)S(1)}, u32[]{:S(2)}, u32[]{:S(2)}) collective-permute-start(f32[128,128]{1,0:T(8,128)S(1)} %slice.3), channel_id=1, source_target_pairs={{2,4},{4,2},{6,8},{8,6},{10,12},{12,10},{14,16},{16,14},{18,20},{2... | collective-permute-start | bytes 196616 | tf_op jit(solution)/shard_map/ppermute | solution.py:443
  13.9 12.0 %collective-permute-start = (f32[128,128]{1,0:T(8,128)S(1)}, f32[128,128]{1,0:T(8,128)S(1)}, u32[]{:S(2)}, u32[]{:S(2)}) collective-permute-start(f32[128,128]{1,0:T(8,128)S(1)} %slice.3), channel_id=1, source_target_pairs={{0,2},{2,0},{4,6},{6,4},{8,10},{10,8},{12,14},{14,12},{16,18},{18,... | collective-permute-start | bytes 196616 | tf_op jit(solution)/shard_map/ppermute | solution.py:443
  18.6 1.6 %copy-start.2 = (f32[16,128,256]{2,1,0:T(8,128)S(1)}, f32[16,128,256]{2,1,0:T(8,128)}, u32[]{:S(2)}) copy-start(f32[16,128,256]{2,1,0:T(8,128)} %copy-done.1) | copy-start | bytes 6291460
  24.7 1.1 %copy-start.3 = (bf16[12,256,256]{2,1,0:T(8,128)(2,1)}, bf16[12,256,256]{2,1,0:T(8,128)(2,1)S(1)}, u32[]{:S(2)}) copy-start(bf16[12,256,256]{2,1,0:T(8,128)(2,1)S(1)} %get-tuple-element.25.far_ref) | copy-start | bytes 4718596
  26.0 10.7 %collective-permute-start.3 = (f32[128,128]{1,0:T(8,128)S(1)}, f32[128,128]{1,0:T(8,128)S(1)}, u32[]{:S(2)}, u32[]{:S(2)}) collective-permute-start(f32[128,128]{1,0:T(8,128)S(1)} %get-tuple-element.24), channel_id=1, source_target_pairs={{64,128},{128,64},{66,130},{130,66},{68,132},{132,68},{70,134},{13... | collective-permute-start | bytes 196616 | tf_op jit(solution)/shard_map/ppermute | solution.py:443
  26.7 10.2 %collective-permute-start.2 = (f32[128,128]{1,0:T(8,128)S(1)}, f32[128,128]{1,0:T(8,128)S(1)}, u32[]{:S(2)}, u32[]{:S(2)}) collective-permute-start(f32[128,128]{1,0:T(8,128)S(1)} %get-tuple-element.24), channel_id=1, source_target_pairs={{0,64},{64,0},{2,66},{66,2},{4,68},{68,4},{6,70},{70,6},{8,72},{72... | collective-permute-start | bytes 196616 | tf_op jit(solution)/shard_map/ppermute | solution.py:443
  36.9 1.4 %copy-start.4 = (bf16[12,256,256]{2,1,0:T(8,128)(2,1)S(1)}, bf16[12,256,256]{2,1,0:T(8,128)(2,1)}, u32[]{:S(2)}) copy-start(bf16[12,256,256]{2,1,0:T(8,128)(2,1)} %copy-done.3) | copy-start | bytes 4718596
  73.3 6.9 %collective-permute-start.4 = (f32[1280,128]{1,0:T(8,128)S(1)}, f32[1280,128]{1,0:T(8,128)S(1)}, u32[]{:S(2)}, u32[]{:S(2)}) collective-permute-start(f32[1280,128]{1,0:T(8,128)S(1)} %bitcast.13), channel_id=1, source_target_pairs={{0,1},{1,0},{2,3},{3,2},{4,5},{5,4},{6,7},{7,6},{8,9},{9,8},{10,11... | collective-permute-start | bytes 1966088 | tf_op jit(solution)/shard_map/ppermute | solution.py:521

commit v2 on v1

v2 whole, which is shorter than its diff:
```python
import functools

import jax
import jax.numpy as jnp
import numpy as np
from jax import lax
from jax.experimental import pallas as pl
from jax.experimental.pallas import tpu as pltpu
from jax.sharding import PartitionSpec as P

F32 = jnp.float32
BF16 = jnp.bfloat16
NPG = 4
DEV_ROWS = 4
SIDE_POINTS = [[0, 1, 2, 3], [3, 7, 11, 15], [12, 13, 14, 15], [0, 4, 8, 12]]
CORNER_POINTS = [0, 3, 12, 15]
CORNER_SIDES = [[(0, 0), (3, 0)], [(0, 3), (1, 0)], [(2, 0), (3, 3)], [(1, 3), (2, 3)]]
EDGE_SLOTS = [(s, m) for s in range(4) for m in (1, 2)]
POINT_NUMBER = {p: c for c, p in enumerate(CORNER_POINTS)}
POINT_NUMBER.update({SIDE_POINTS[s][m]: 4 + n for n, (s, m) in enumerate(EDGE_SLOTS)})
TIME_STEP = 0.05
TOP_PRESSURE = 1.0
MIXING_RATE = 0.8
PER_SIDE = 16
ROWS = 10


def lagrange_derivative():
    gll_points = np.array([-1.0, -1.0 / np.sqrt(5.0), 1.0 / np.sqrt(5.0), 1.0])
    barycentric = np.array(
        [
            1.0
            / np.prod(
                [gll_points[source] - gll_points[middle] for middle in range(4) if middle != source]
            )
            for source in range(4)
        ]
    )
    derivative = np.zeros((4, 4))
    for target in range(4):
        for source in range(4):
            if target != source:
                derivative[target, source] = (
                    barycentric[source]
                    / barycentric[target]
                    / (gll_points[target] - gll_points[source])
                )
        derivative[target, target] = -np.sum(derivative[target])
    return derivative


def iota(shape, dim):
    return lax.broadcasted_iota(jnp.int32, shape, dim)


def hot(mask):
    return jnp.where(mask, 1.0, 0.0).astype(BF16)


def split(x, axis=0):
    high = x.astype(BF16)
    low = (x - high.astype(F32)).astype(BF16)
    return jnp.concatenate([high, low], axis=axis)


def dot_nn(a, b):
    return lax.dot_general(a, b, (((1,), (0,)), ((), ())), preferred_element_type=F32)


def dot_nt(a, b):
    return lax.dot_general(a, b, (((1,), (1,)), ((), ())), preferred_element_type=F32)


def wide(ref, first=0):
    return jnp.concatenate([ref[first + s : first + s + 1, :] for s in range(4)], axis=1)


def facing(peer, own, block_cols):
    ahead = peer - own
    code = jnp.full_like(peer, -1)
    for number, offset in enumerate((1, -1, block_cols, -block_cols)):
        code = jnp.where(ahead == offset, number, code)
    return jnp.where(peer >= 0, code, -1)


def ranks(direction, entry):
    count = direction.shape[1]
    code = jnp.where(direction >= 0, direction * 64 + entry, -1)
    found = jnp.where(iota((256, count), 0) == code, 1.0, 0.0)
    present = jnp.max(found, axis=1, keepdims=True)
    row, col = iota((256, 256), 0), iota((256, 256), 1)
    before = hot((col < row) & (col // 64 == row // 64))
    below = dot_nn(before, jnp.broadcast_to(present, (256, 128)).astype(BF16))
    rank = jnp.sum(found * below[:, :1], axis=0, keepdims=True)
    return rank.astype(jnp.int32)


def flux_kernel(
    block_cols, own_ref, tr_hbm, lm_hbm, wd_hbm, sph_hbm, peer_hbm, slot_hbm, flip_hbm, pub_hbm, table_hbm, next_hbm, inv_hbm,
    x_ref, one_ref, two_ref, info_ref, sph_ref, peer_ref, slot_ref, flip_ref, pub_ref, table_ref, next_ref, inv_ref,
    tr_ref, lm_ref, wd_ref, sems
):
    deriv = lagrange_derivative() * TIME_STEP
    levels = lm_ref.shape[1] // 16
    tracers = tr_ref.shape[1] // lm_ref.shape[1]
    elems = peer_ref.shape[1]
    lanes = tr_ref.shape[2]
    copies = []

    def fetch(src, dst):
        copy = pltpu.make_async_copy(src, dst, sems.at[len(copies)])
        copy.start()
        copies.append(copy)
        return copy

    small = [fetch(peer_hbm, peer_ref), fetch(slot_hbm, slot_ref), fetch(sph_hbm, sph_ref)]
    big = []
    for half in range(2):
        cut = slice(half * lanes, (half + 1) * lanes)
        big.append(
            [
                fetch(lm_hbm.at[:, cut], lm_ref.at[half]),
                fetch(wd_hbm.at[:, cut], wd_ref.at[half]),
                fetch(tr_hbm.at[:, cut], tr_ref.at[half]),
            ]
        )
    later = [fetch(flip_hbm, flip_ref), fetch(pub_hbm, pub_ref), fetch(table_hbm, table_ref), fetch(inv_hbm, inv_ref)]
    for half in range(2):
        later.append(fetch(next_hbm.at[:, half * lanes : (half + 1) * lanes], next_ref.at[half]))

    for copy in small:
        copy.wait()
    direction = facing(wide(peer_ref), own_ref[0], block_cols)
    rank = ranks(direction, jnp.clip(wide(slot_ref), 0, 63))
    usable = (direction >= 0) & (rank < PER_SIDE)
    base = jnp.where(usable, direction * 64 + rank, -1000)
    info_ref[...] = jnp.broadcast_to(base, info_ref.shape)

    for half in range(2):
        cut = slice(half * lanes, (half + 1) * lanes)
        for copy in big[half]:
            copy.wait()
        tr_half, lm_half, wd_half = tr_ref.at[half], lm_ref.at[half], wd_ref.at[half]

        def one(t, carry):
            mass, fa, fb = [], [], []
            for k in range(16):
                tr = tr_half[pl.ds(t * (levels * 16) + k, levels, stride=16), :]
                mk = tr * lm_half[pl.ds(k, levels, stride=16), :]
                mass.append(mk)
                fa.append(mk * wd_half[pl.ds(k, levels, stride=16), :])
                fb.append(mk * wd_half[pl.ds(levels * 16 + k, levels, stride=16), :])
            for k in range(16):
                j, i = k // 4, k % 4
                value = mass[k]
                for other in range(4):
                    if abs(deriv[i, other]) > 1e-12:
                        value = value - deriv[i, other] * fa[4 * j + other]
                    if abs(deriv[j, other]) > 1e-12:
                        value = value - deriv[j, other] * fb[4 * other + i]
                x_ref[k, pl.ds(pl.multiple_of(t * levels, levels), levels), cut] = value * sph_ref[k : k + 1, cut]
            return carry

        lax.fori_loop(0, tracers, one, 0)

    lane = iota((256, elems), 0)
    total = None
    for group in [[pair] for pair in EDGE_SLOTS] + CORNER_SIDES:
        pick = None
        for s, m in group:
            here = lane == base[:, s * elems : (s + 1) * elems] + m * PER_SIDE
            pick = here if pick is None else pick | here
        s, m = group[0]
        part = dot_nt(split(x_ref[SIDE_POINTS[s][m]]), hot(pick))
        total = part if total is None else total + part
    fields = total.shape[0] // 2
    total = total[:fields] + total[fields:]
    one_ref[...] = total[:, :128]
    two_ref[...] = total[:, 128:]
    for copy in later:
        copy.wait()


def arrive(recv, turn, elems, s, m):
    cols = slice(s * elems, (s + 1) * elems)
    turned = jnp.where(turn[:, cols] == 1, 3 - m, m)
    return recv[:, cols] + turned * PER_SIDE


def plan_kernel(
    block_cols, group_width, own_ref, peer_ref, flip_ref, pub_ref, info_ref, table_ref, next_ref, sph_ref, held_ref,
    recv_ref, mid_ref, key_ref, rden_ref, rows_ref
):
    elems = peer_ref.shape[1]
    sides = 4 * elems
    peer, flip = wide(peer_ref), wide(flip_ref)
    at = iota((1, sides), 1)
    entries = pub_ref.shape[1]
    square = iota((entries, entries), 0) == iota((entries, entries), 1)
    listed = jnp.sum(jnp.where(square, pub_ref[...].astype(F32), 0.0), axis=1, keepdims=True).astype(jnp.int32)
    own_code = 4 * (at % elems) + at // elems
    match = jnp.where(listed == own_code, 1.0, 0.0)
    place = jnp.sum(match * iota((entries, sides), 0).astype(F32), axis=0, keepdims=True).astype(jnp.int32)
    direction = facing(peer, own_ref[0], block_cols)
    rank = ranks(direction, place)
    usable = (direction >= 0) & (rank < PER_SIDE)
    start = jnp.where(direction == 0, 64, jnp.where(direction == 1, 0, jnp.where(direction == 2, 192, 128)))
    recv = jnp.where(usable, start + rank, -1000)
    recv_ref[...] = jnp.broadcast_to(recv, recv_ref.shape)
    base = info_ref[:1, :]
    second = jnp.where(base >= 128, base - 128, -1000)
    lane = iota((128, elems), 0)
    sent, got = [], []
    for c in range(4):
        (sa, ma), (sb, mb) = CORNER_SIDES[c]
        got.append(hot((lane == arrive(recv, flip, elems, sa, ma)) | (lane == arrive(recv, flip, elems, sb, mb))))
        here = [lane == second[:, s * elems : (s + 1) * elems] + m * PER_SIDE for s, m in CORNER_SIDES[c]]
        sent.append(hot(here[0] | here[1]))
    mid_ref[...] = dot_nt(jnp.concatenate(got, axis=1), jnp.concatenate(sent, axis=1)).astype(BF16)

    levels = next_ref.shape[1] // 16
    sph = sph_ref[...]
    thicks = []
    for c in range(4):
        den, area = None, None
        for k in range(16):
            if 2 * (k // 8) + k % 4 // 2 != c:
                continue
            weight = sph[k : k + 1, :]
            term = [next_ref.at[half][pl.ds(k, levels, stride=16), :] for half in range(2)]
            term = jnp.concatenate(term, axis=1) * weight
            den = term if den is None else den + term
            area = weight if area is None else area + weight
        rden_ref[:, c * elems : (c + 1) * elems] = 1.0 / den
        thicks.append(den / area)
    thick = jnp.concatenate(thicks, axis=1)
    total = 4 * elems
    slot = wide(table_ref)
    slot_f = slot.astype(F32)
    dest = jnp.floor((slot_f + 0.5) * (1.0 / group_width)).astype(jnp.int32)
    within = (slot - dest * group_width).astype(F32)
    peers = rows_ref.shape[1]
    to = jnp.where(iota((peers, total), 0) == dest, 1.0, 0.0)
    to_b = to.astype(BF16)
    upto = hot(iota((128, 128), 0) < iota((128, 128), 1))
    before = jnp.zeros((peers, 1), F32)
    parts = []
    for block in range(total // 128):
        cols = slice(block * 128, block * 128 + 128)
        parts.append(dot_nn(to_b[:, cols], upto) + before)
        before = before + jnp.sum(to[:, cols], axis=1, keepdims=True)
    rank = jnp.sum(to * jnp.concatenate(parts, axis=1), axis=0, keepdims=True).astype(jnp.int32)
    key = dest * 8 + rank
    key_ref[...] = jnp.broadcast_to(key, key_ref.shape)
    at = iota((128, total), 0)
    spread = jnp.where(at // levels == rank, jnp.concatenate([thick] * (128 // levels), axis=0), 0.0)
    ids = jnp.where(at == rank, within, 0.0)
    both = jnp.concatenate([split(spread), split(ids)], axis=0)
    got = dot_nt(to_b, both)
    rows_ref[0] = got[:, :128] + got[:, 128:256]
    rows_ref[1] = got[:, 256:384] + got[:, 384:]


def local_kernel(
    own_ref, x_ref, peer_ref, slot_ref, flip_ref, recv_ref, sph_ref, inv_ref, rden_ref, xd_ref, far_ref, far_mix_ref, mix_ref
):
    own = own_ref[0]
    elems = peer_ref.shape[1]
    fields = x_ref.shape[1]
    sides = 4 * elems
    peer, slot, flip = wide(peer_ref), wide(slot_ref), wide(flip_ref)
    recv = recv_ref[:1, :]
    lane = iota((256, elems), 0)
    corner_far = []
    for c in range(4):
        (sa, ma), (sb, mb) = CORNER_SIDES[c]
        corner_far.append(hot((lane == arrive(recv, flip, elems, sa, ma)) | (lane == arrive(recv, flip, elems, sb, mb))))
    corner_far = jnp.concatenate(corner_far, axis=1)
    for number, (s, m) in enumerate(EDGE_SLOTS):
        far_ref[4 + number] = hot(lane == arrive(recv, flip, elems, s, m))

    local = peer == own
    slot_c = jnp.clip(slot, 0, 4 * elems - 1)
    near = jnp.where(local, slot_c % 4 * elems + slot_c // 4, -1)

    def corner_source(code, end, ok):
        side = code % 4
        corner = jnp.where(side == 1, 1, jnp.where(side == 2, 2, 0)) + end * jnp.where(side % 2 == 1, 2, 1)
        return jnp.where(ok, corner * elems + code // 4, -1)

    cpeer, cslot, cflip = wide(peer_ref, 4), wide(slot_ref, 4), wide(flip_ref, 4)
    third = corner_source(jnp.clip(cslot, 0, 4 * elems - 1), cflip, cpeer == own)
    source = iota((sides, elems), 0)
    weights = []
    for c in range(4):
        cols = slice(c * elems, (c + 1) * elems)
        weight = jnp.where(source == third[:, cols], 1.0, 0.0)
        for s, m in CORNER_SIDES[c]:
            own_cols = slice(s * elems, (s + 1) * elems)
            end = jnp.where(flip[:, own_cols] == 1, 1 - m // 3, m // 3)
            code = corner_source(slot_c[:, own_cols], end, local[:, own_cols])
            weight = weight + jnp.where(source == code, 1.0, 0.0)
        weights.append(weight.astype(BF16))
    corners = jnp.concatenate([x_ref[p] for p in CORNER_POINTS], axis=1)
    lhs = jnp.concatenate([split(corners), corner_far], axis=0)
    for c in range(4):
        cols = slice(c * elems, (c + 1) * elems)
        got = dot_nn(lhs, weights[c])
        xd_ref[CORNER_POINTS[c]] = corners[:, cols] + got[:fields] + got[fields : 2 * fields]
        far_ref[c] = corner_far[:, cols] + got[2 * fields :].astype(BF16)
    inner = []
    for m in (1, 2):
        inner.append(split(jnp.concatenate([x_ref[SIDE_POINTS[s][m]] for s in range(4)], axis=1)))
    inner = jnp.concatenate(inner, axis=0)
    for s in range(4):
        cols = slice(s * elems, (s + 1) * elems)
        got = dot_nn(inner, hot(source == near[:, cols]))
        one = got[:fields] + got[fields : 2 * fields]
        two = got[2 * fields : 3 * fields] + got[3 * fields :]
        turned = flip[:, cols] == 1
        for m, mine, swapped in ((1, one, two), (2, two, one)):
            p = SIDE_POINTS[s][m]
            xd_ref[p] = x_ref[p] + jnp.where(turned, swapped, mine)
    for p in (5, 6, 9, 10):
        xd_ref[p] = x_ref[p]

    weight = sph_ref[...] * inv_ref[...]
    levels = rden_ref.shape[0]
    for c in range(4):
        cols = slice(c * elems, (c + 1) * elems)
        mix, far_mix = None, None
        for k in range(16):
            if 2 * (k // 8) + k % 4 // 2 != c:
                continue
            wk = weight[k : k + 1, :]
            term = xd_ref[k] * wk
            mix = term if mix is None else mix + term
            if k in POINT_NUMBER:
                term = far_ref[POINT_NUMBER[k]].astype(F32) * wk
                far_mix = term if far_mix is None else far_mix + term
        mix_ref[:, cols] = mix * jnp.concatenate([rden_ref[:, cols]] * (fields // levels), axis=0)
        high = far_mix.astype(BF16)
        far_mix_ref[0, :, cols] = high
        far_mix_ref[1, :, cols] = (far_mix - high.astype(F32)).astype(BF16)


def merge(odd, a, b):
    low = iota(a.shape, 1) < 64
    lower = jnp.where(odd == 1, a, b)
    upper = jnp.where(odd == 1, b, a)
    return jnp.where(low, lower, upper)


def middle_kernel(odd_ref, a_ref, b_ref, two_ref, mid_ref, held_ref, got_ref, out_ref):
    got = merge(odd_ref[0], a_ref[...], b_ref[...])
    got_ref[...] = got
    fields = got.shape[0]
    add = dot_nn(split(got), mid_ref[...])
    out_ref[...] = two_ref[...] + add[:fields] + add[fields:]


def send_kernel(odd_ref, one_ref, a_ref, b_ref, far_mix_ref, mix_ref, rden_ref, key_ref, rows_ref, held_ref, far_held_ref, two_ref, out_ref):
    fields = mix_ref.shape[0]
    levels = rden_ref.shape[0]
    two = merge(odd_ref[0], a_ref[...], b_ref[...])
    two_ref[...] = two
    got = split(jnp.concatenate([one_ref[...], two], axis=1))
    add = dot_nn(got, far_mix_ref[0]) + dot_nn(got, far_mix_ref[1])
    add = add[:fields] + add[fields:]
    mix_hl = split(mix_ref[...] + add * jnp.concatenate([rden_ref[...]] * (fields // levels), axis=0))
    peers = rows_ref.shape[1]
    chunk = 128
    key = key_ref[:1, :]
    row_of = iota((chunk, key.shape[1]), 0)
    for block in range(peers * 8 // chunk):
        res = dot_nt(hot(row_of == key - block * chunk), mix_hl)
        res = res[:, :fields] + res[:, fields:]
        for d in range(chunk // 8):
            row = (block * (chunk // 8) + d) * ROWS
            out_ref[row : row + 8, :] = res[d * 8 : d * 8 + 8, :]
    out_ref[pl.ds(8, peers, stride=ROWS), :] = rows_ref[0]
    out_ref[pl.ds(9, peers, stride=ROWS), :] = rows_ref[1]


def mass_kernel(xd_ref, one_ref, two_ref, far_ref, inv_ref, tm_ref):
    fields = xd_ref.shape[1]
    got = split(jnp.concatenate([one_ref[...], two_ref[...]], axis=1))
    for k in range(16):
        value = xd_ref[k]
        if k in POINT_NUMBER:
            far = dot_nn(got, far_ref[POINT_NUMBER[k]])
            value = value + far[:fields] + far[fields:]
        tm_ref[pl.ds(k, fields, stride=16), :] = value * inv_ref[k : k + 1, :]


def gathered(buf_ref, pick_ref, levels):
    total, fields = buf_ref.shape
    peers = total // ROWS
    slots = pick_ref.shape[0]
    thick = buf_ref[pl.ds(8, peers, stride=ROWS), :]
    spread = hot(iota((total, peers), 0) // ROWS == iota((total, peers), 1))
    rows = dot_nn(spread, split(thick, axis=1))
    keep = iota((total, 128), 1) // levels == iota((total, 128), 0) % ROWS
    rows = split(jnp.where(keep, rows[:, :128] + rows[:, 128:], 0.0), axis=0)
    fold = hot(iota((128, 128), 1) == iota((128, 128), 0) % levels)
    narrow = dot_nn(rows, fold)
    narrow = narrow[:total] + narrow[total:]
    narrow = jnp.where(iota((total, 128), 1) == levels, 1.0, narrow)
    stack = split(jnp.concatenate([buf_ref[...], narrow], axis=1), axis=1)
    width = fields + 128
    outs = []
    for block in range(slots // 128):
        got = dot_nn(pick_ref[block * 128 : (block + 1) * 128, :], stack)
        outs.append(jnp.transpose(got[:, :width] + got[:, width:]))
    return outs


def place_kernel(lev_ref, own_ref, pick_ref, half_ref, *, levels):
    total = own_ref.shape[0]
    peers = total // ROWS
    slots = pick_ref.shape[0]
    ids = own_ref[pl.ds(9, peers, stride=ROWS), :]
    spread = hot(iota((peers, total), 1) // ROWS == iota((peers, total), 0))
    ids_t = jnp.transpose(ids)[:16, :]
    cand = dot_nn(split(ids_t), spread)
    cand = cand[:16] + cand[16:]
    spot = iota((16, total), 1) % ROWS
    key = jnp.sum(jnp.where((spot == iota((16, total), 0)) & (spot < 8), cand, 0.0), axis=0, keepdims=True)
    key = jnp.where(iota((1, total), 1) % ROWS < 8, key, -1e6).astype(jnp.int32)
    key = key - lev_ref[0] * slots
    for block in range(slots // 128):
        pick_ref[block * 128 : (block + 1) * 128, :] = hot(iota((128, total), 0) + block * 128 == key)
    for block, got in enumerate(gathered(own_ref, pick_ref, levels)):
        half_ref[:, block * 128 : (block + 1) * 128] = got


def physics_kernel(lev_ref, half_ref, par_ref, pick_ref, mix_ref, sig_ref):
    lev = lev_ref[0]
    levels2 = sig_ref.shape[0]
    fields = par_ref.shape[1]
    levels = levels2 // 2
    tracers = fields // levels
    for block, other in enumerate(gathered(par_ref, pick_ref, levels)):
        cols = slice(block * 128, (block + 1) * 128)
        mine = half_ref[:, cols]
        first = jnp.where(lev == 0, mine, other)
        last = jnp.where(lev == 0, other, mine)
        thick = jnp.concatenate([first[fields : fields + levels], last[fields : fields + levels]], axis=0)
        live = first[fields + levels : fields + levels + 1]
        running = jnp.zeros_like(live)
        above = []
        for level in range(levels2):
            above.append(running)
            running = running + thick[level : level + 1]
        above = jnp.concatenate(above, axis=0)
        scale = live / (TOP_PRESSURE + running)
        sigma = (TOP_PRESSURE + above + 0.5 * thick) * scale
        sig_ref[:, cols] = sigma
        share = 1.0 / (running + 1.0 - live)
        for t in range(tracers):
            mix = jnp.concatenate([first[t * levels : (t + 1) * levels], last[t * levels : (t + 1) * levels]], axis=0)
            mean = jnp.sum(thick * mix, axis=0, keepdims=True) * share
            mix_ref[t * levels2 : (t + 1) * levels2, cols] = mix + MIXING_RATE * sigma * (mean - mix)


def halved(shape):
    lead = (0,) * (len(shape) - 1)
    return pl.BlockSpec(shape[:-1] + (shape[-1] // 2,), lambda i: lead + (i,))


def call(kernel, outs, ins, hbm=(), held=(), scratch=(), vmem=16):
    specs = []
    for number, value in enumerate(ins):
        space = pltpu.SMEM if value.shape == (1,) else pltpu.HBM if number in hbm else pltpu.VMEM
        space = pl.ANY if number in held else space
        specs.append(pl.BlockSpec(memory_space=space))
    ins = [pltpu.with_memory_space_constraint(x, pltpu.HBM) if n in hbm else x for n, x in enumerate(ins)]
    return pl.pallas_call(
        kernel,
        out_shape=[out[2](*out[:2]) if len(out) > 2 else jax.ShapeDtypeStruct(*out) for out in outs],
        in_specs=specs,
        out_specs=[pl.BlockSpec(memory_space=out[2] if len(out) > 2 else pltpu.VMEM) for out in outs],
        scratch_shapes=list(scratch),
        compiler_params=pltpu.CompilerParams(vmem_limit_bytes=vmem * 1024 * 1024),
    )(*ins)


def swap(value, step, parity, count, row=None):
    pairs = []
    for i in range(count - step):
        if i // step % 2 == parity and (row is None or i // row == (i + step) // row):
            pairs += [(i, i + step), (i + step, i)]
    return lax.ppermute(value, "sfc", pairs)


def body(
    tracers,
    layer_mass,
    layer_mass_next,
    wind,
    spheremp,
    inverse_mass,
    rec_peer,
    rec_slot,
    rec_flip,
    publish_list,
    column_slot_table,
):
    own_index = lax.axis_index("sfc").astype(jnp.int32)
    lev_index = lax.axis_index("lev").astype(jnp.int32)
    sfc_count = lax.axis_size("sfc")
    lev_count = lax.axis_size("lev")
    tracer_count, level_count, points, elems = tracers.shape
    fields = tracer_count * level_count
    block_cols = sfc_count // DEV_ROWS
    own = own_index.reshape(1)
    col_odd = (own_index % block_cols % 2).reshape(1)
    row_odd = (own_index // block_cols % 2).reshape(1)

    rows = level_count * points
    half = elems // 2
    cols = NPG * elems
    ints = jnp.int32
    ins = [
        own,
        tracers.reshape(fields * points, elems),
        layer_mass.reshape(rows, elems),
        wind.reshape(2 * rows, elems),
        spheremp,
        rec_peer,
        rec_slot,
        rec_flip,
        publish_list.reshape(1, -1),
        column_slot_table,
        layer_mass_next.reshape(rows, elems),
        inverse_mass,
    ]
    weighted, first, second, info, sph, peer, slot, flip, pub, table, after, inv = call(
        functools.partial(flux_kernel, block_cols),
        [
            ((points, fields, elems), F32, pltpu.VMEM),
            ((fields, 128), F32),
            ((fields, 128), F32),
            ((8, 4 * elems), ints),
            (spheremp.shape, F32),
            (rec_peer.shape, ints),
            (rec_slot.shape, ints),
            (rec_flip.shape, ints),
            ((1, publish_list.shape[0]), ints),
            (column_slot_table.shape, ints),
            ((2, rows, half), F32),
            (inverse_mass.shape, F32),
        ],
        ins,
        hbm=range(1, len(ins)),
        scratch=[
            pltpu.VMEM((2, fields * points, half), F32),
            pltpu.VMEM((2, rows, half), F32),
            pltpu.VMEM((2, 2 * rows, half), F32),
            pltpu.SemaphoreType.DMA((15,)),
        ],
    )
    near_a = swap(first, 1, 0, sfc_count, block_cols)
    near_b = swap(first, 1, 1, sfc_count, block_cols)
    group_width = 5 * NPG * elems // 4
    recv, mid, key, rden, extra = call(
        functools.partial(plan_kernel, block_cols, group_width),
        [
            ((8, 4 * elems), ints),
            ((128, 128), BF16),
            ((8, cols), ints),
            ((level_count, cols), F32),
            ((2, sfc_count, 128), F32),
        ],
        [own, peer, flip, pub, info, table, after, sph, weighted],
        held=(8,),
    )
    got_one, second = call(
        middle_kernel,
        [((fields, 128), F32), ((fields, 128), F32)],
        [col_odd, near_a, near_b, second, mid, weighted],
        held=(5,),
    )
    over_a = swap(second, block_cols, 0, sfc_count)
    over_b = swap(second, block_cols, 1, sfc_count)
    weighted, _ = lax.optimization_barrier((weighted, second))
    local, far, far_mix, mix = call(
        local_kernel,
        [
            ((points, fields, elems), F32, pltpu.VMEM),
            ((12, 256, elems), BF16, pltpu.VMEM),
            ((2, 256, cols), BF16),
            ((fields, cols), F32),
        ],
        [own, weighted, peer, slot, flip, recv, sph, inv, rden],
    )
    got_two, send = call(
        send_kernel,
        [((fields, 128), F32), ((ROWS * sfc_count, fields), F32)],
        [row_odd, got_one, over_a, over_b, far_mix, mix, rden, key, extra, local, far],
        held=(9, 10),
    )
    moved = lax.all_to_all(
        send.reshape(sfc_count, 1, ROWS * fields), "sfc", split_axis=0, concat_axis=0, tiled=True
    ).reshape(ROWS * sfc_count, fields)
    whole = pl.BlockSpec((fields, 128), lambda i: (0, 0))
    mass = pl.pallas_call(
        mass_kernel,
        grid=(2,),
        out_shape=jax.ShapeDtypeStruct((fields * points, elems), F32),
        in_specs=[halved(local.shape), whole, whole, halved(far.shape), halved(inv.shape)],
        out_specs=halved((fields * points, elems)),
        compiler_params=pltpu.CompilerParams(vmem_limit_bytes=12 * 1024 * 1024),
        cost_estimate=pl.CostEstimate(flops=2 * 256 * 256 * 3072, bytes_accessed=16 * fields * points * elems, transcendentals=0),
    )(local, got_one, got_two, far, inv)
    moved, mass = lax.optimization_barrier((moved, mass))
    other = lax.ppermute(moved, "lev", [(0, 1), (1, 0)])
    slots = group_width // lev_count
    levels = level_count * lev_count
    lev = lev_index.reshape(1)
    pick, own_half = call(
        functools.partial(place_kernel, levels=level_count),
        [((slots, ROWS * sfc_count), BF16), ((fields + 128, slots), F32)],
        [lev, moved],
    )
    mixed, sigma = call(
        physics_kernel,
        [((tracer_count * levels, slots), F32), ((levels, slots), F32)],
        [lev, own_half, other, pick],
    )
    return (
        mass.reshape(tracers.shape),
        mixed.reshape(tracer_count, levels, slots),
        sigma,
    )


def solution(mesh):
    in_specs = (
        P(None, "lev", None, "sfc"),
        P("lev", None, "sfc"),
        P("lev", None, "sfc"),
        P(None, "lev", None, "sfc"),
        P(None, "sfc"),
        P(None, "sfc"),
        P(None, "sfc"),
        P(None, "sfc"),
        P(None, "sfc"),
        P("sfc"),
        P(None, "sfc"),
    )
    out_specs = (
        P(None, "lev", None, "sfc"),
        P(None, None, ("sfc", "lev")),
        P(None, ("sfc", "lev")),
    )
    return jax.shard_map(body, mesh=mesh, in_specs=in_specs, out_specs=out_specs, check_vma=False)
```

time: 84.4 us -> 73 us (0.86)
  blocking collectives: 30.5 us -> 0 us
  starting transfers between devices: 19.7 us -> 34.2 us
  waiting for transfers between devices: 1.92 us -> 12.4 us
  local copies, waits for them, and re-layouts: 11.3 us -> 3 us
  Pallas kernels: 19.7 us -> 22.3 us
    all_to_all x1 -> x0, blocking collectives: 30.5 us -> none  [body(): lax.all_to_all(send.reshape(sfc_count, 1, ROWS * fields), 'sfc', split_ax...]
    all_to_all x0 -> x1, starting transfers between devices: none -> 21.8 us  [body(): lax.all_to_all(send.reshape(sfc_count, 1, ROWS * fields), 'sfc', split_ax...]
    all_to_all x0 -> x1, waiting for transfers between devices: none -> 12.4 us  [body(): lax.all_to_all(send.reshape(sfc_count, 1, ROWS * fields), 'sfc', split_ax...]
    unnamed x36 -> x8, local copies, waits for them, and re-layouts: 11.2 us -> 3 us
    ppermute x4, starting transfers between devices: 14.6 us -> 6.5 us  [swap(): return lax.ppermute(value, 'sfc', pairs)]
    pallas_call x6 -> x8, Pallas kernels: 19.7 us -> 22.3 us  [the longest x7 19.4 us: call(): pl.pallas_call(kernel, out_shape=[out[2](*out[:2]) if len(out) > 2 else j...]
    ppermute x1, waiting for transfers between devices: 1.72 us -> 0.01 us  [body(): other = lax.ppermute(moved, 'lev', [(0, 1), (1, 0)])]
  transfers between devices with their start and end apart: 5 -> 6, of which waited for: 2 -> 1; matrix products, arithmetic and copies ran while one was open for 0% -> 0% of each run, Pallas kernels for 7% -> 15%
where the time goes in v2:
time: 73 us; the launch traced here: 72.7 us
  starting transfers between devices  34.2 us (47%)
  Pallas kernels  22.3 us (31%)
  waiting for transfers between devices  12.4 us (17%)
  local copies, waits for them, and re-layouts  3 us (4%)
  between operations  0.82 us (1%)
    all_to_all x1, starting transfers between devices, body(): lax.all_to_all(send.reshape(sfc_count, 1, ROWS * fields), 'sfc', split_ax...  21.8 us
    pallas_call x7, Pallas kernels, call(): pl.pallas_call(kernel, out_shape=[out[2](*out[:2]) if len(out) > 2 else j...  19.4 us
    all_to_all x1, waiting for transfers between devices, body(): lax.all_to_all(send.reshape(sfc_count, 1, ROWS * fields), 'sfc', split_ax...  12.4 us
    ppermute x4, starting transfers between devices, swap(): return lax.ppermute(value, 'sfc', pairs)  6.5 us
    ppermute x1, starting transfers between devices, body(): other = lax.ppermute(moved, 'lev', [(0, 1), (1, 0)])  5.84 us
    unnamed x8, local copies, waits for them, and re-layouts  3 us
    pallas_call x1, Pallas kernels, body(): pl.pallas_call(mass_kernel, grid=(2,), out_shape=jax.ShapeDtypeStruct((fi...  2.88 us
  transfers between devices with their start and end apart: 6, of which 1 were waited for; matrix products, arithmetic and copies ran while one was open for 0% of the time, Pallas kernels for 15%

profile of v2, /device:TPU:1, one launch (start us, length us, event | category | flops | bytes accessed | tf_op | source)
XLA Modules:
  0.0 72.7 jit_solution(4425265303277768284)
XLA Ops:
  0.6 5.7 %shard_map.130 = (f32[16,128,256]{2,1,0:T(8,128)S(1)}, f32[128,128]{1,0:T(8,128)S(1)}, f32[128,128]{1,0:T(8,128)S(1)}, s32[8,1024]{1,0:T(8,128)S(1)}, f32[16,256...) custom-call(s32[1]{0:T(128)} %bitcast.2.own_ref, ...), custom_call_target="tpu_custom_call" | custom-call | tf_op jit(solution)/shard_map/pallas_call | solution.py:478
  6.4 2.1 %collective-permute-start = (f32[128,128]{1,0:T(8,128)S(1)}, f32[128,128]{1,0:T(8,128)S(1)}, u32[]{:S(2)}, u32[]{:S(2)}) collective-permute-start(f32[128,128]{1,0:T(8,128)S(1)} %get-tuple-element.35), channel_id=1, source_target_pairs={{0,2},{2,0},{4,6},{6,4},{8,10},{10,8},{12,14},{14,12},{16,18},{18,... | collective-permute-start | bytes 196616 | tf_op jit(solution)/shard_map/ppermute | solution.py:493
  8.5 0.7 collective-permute-start.1
  9.2 1.5 %shard_map.131 = (s32[8,1024]{1,0:T(8,128)S(1)}, bf16[128,128]{1,0:T(8,128)(2,1)S(1)}, s32[8,1024]{1,0:T(8,128)S(1)}, f32[16,1024]{1,0:T(8,128)S(1)}, f32[2,128,128]{2,1,0:T(8,128)S(1)}) custom-call(s32[1]{0:T(128)} %bitcast.2.own_ref, s32[8,256]{1,0:T(8,128)S(1)} %get-tuple-element.37.peer_ref, s32[8,256]{1,0:T(8,128)S(1)} %get-tuple-element.38.flip_ref, ...), custom_call_target="tpu_custom_call" | custom-call | tf_op jit(solution)/shard_map/pallas_call | solution.py:478
  10.7 0.0 collective-permute-done.a_ref
  10.7 0.0 collective-permute-done.1.b_ref
  10.7 0.2 shard_map.132
  10.9 3.1 %collective-permute-start.2 = (f32[128,128]{1,0:T(8,128)S(1)}, f32[128,128]{1,0:T(8,128)S(1)}, u32[]{:S(2)}, u32[]{:S(2)}) collective-permute-start(f32[128,128]{1,0:T(8,128)S(1)} %get-tuple-element.47), channel_id=1, source_target_pairs={{0,64},{64,0},{2,66},{66,2},{4,68},{68,4},{6,70},{70,6},{8,72},{72... | collective-permute-start | bytes 196616 | tf_op jit(solution)/shard_map/ppermute | solution.py:493
  13.9 0.7 collective-permute-start.3
  14.6 4.3 %shard_map.133 = (f32[16,128,256]{2,1,0:T(8,128)S(1)}, bf16[12,256,256]{2,1,0:T(8,128)(2,1)S(1)}, bf16[2,256,1024]{2,1,0:T(8,128)(2,1)S(1)}, f32[128,1024]{1,0:T(8,128)S(1)}) custom-call(s32[1]{0:T(128)} %bitcast.2.own_ref, f32[16,128,256]{2,1,0:T(8,128)S(1)} %get-tuple-element.48.held_ref.x_ref, s32[8,256]{1,0:T(8,128)S(1)} %get-tuple-element.37.peer_ref, ...), custom_call_target="tpu_custom_call" | custom-call | tf_op jit(solution)/shard_map/pallas_call | solution.py:478
  19.0 0.0 copy-start
  19.0 0.0 copy-start.2
  19.0 0.0 collective-permute-done.2.a_ref
  19.0 0.0 collective-permute-done.3.b_ref
  19.0 2.7 %shard_map.134 = (f32[128,128]{1,0:T(8,128)S(1)}, f32[1280,128]{1,0:T(8,128)}) custom-call(s32[1]{0:T(128)} %bitcast.odd_ref, f32[128,128]{1,0:T(8,128)S(1)} %get-tuple-element.46.one_ref, f32[128,128]{1,0:T(8,128)S(1)} %collective-permute-done.2.a_ref, f32[128,128]{1,0:T(8,128)S(1)} %collective-permute-done.3.b_ref, ...), custom_call_target="tpu_custom_call" | custom-call | tf_op jit(solution)/shard_map/pallas_call | solution.py:478
  21.7 0.0 copy-done
  21.7 0.0 copy-done.2
  21.7 21.8 %all-to-all-start = ((f32[128,1,1280]{2,1,0:T(1,128)}), f32[128,1,1280]{2,1,0:T(1,128)S(1)}, u32[]{:S(2)}, u32[]{:S(2)}) async-start(f32[128,1,1280]{2,1,0:T(1,128)} %bitcast.8), calls=%async_computation | async-start | bytes 1310720 | tf_op jit(solution)/shard_map/all_to_all | solution.py:603
  43.6 0.0 copy-start.1
  43.6 1.6 %copy-done.1 = f32[16,128,256]{2,1,0:T(8,128)S(1)} copy-done((f32[16,128,256]{2,1,0:T(8,128)S(1)}, f32[16,128,256]{2,1,0:T(8,128)}, u32[]{:S(2)}) %copy-start.1) | copy-done | bytes 2097176
  45.2 0.0 copy-start.3
  45.2 1.4 %copy-done.3 = bf16[12,256,256]{2,1,0:T(8,128)(2,1)S(1)} copy-done((bf16[12,256,256]{2,1,0:T(8,128)(2,1)S(1)}, bf16[12,256,256]{2,1,0:T(8,128)(2,1)}, u32[]{:S(2)}) %copy-start.3) | copy-done | bytes 1572888
  46.6 2.9 %shard_map.135 = f32[2048,256]{1,0:T(8,128)} custom-call(f32[16,128,256]{2,1,0:T(8,128)S(1)} %copy-done.1, f32[128,128]{1,0:T(8,128)S(1)} %get-tuple-element.46.one_ref, f32[128,128]{1,0:T(8,128)S(1)} %get-tuple-element.60.two_ref, bf16[12,256,256]{2,1,0:T(8,128)(2,1)S(1)} %copy-done.3, f32[16,256]{1,0:T(8,128)S(1)} %get-tuple-element.51.inv_ref), custom_call_target="tpu_custom_call" | custom-call | flops 402653184 | bytes 8388608 | tf_op jit(solution)/shard_map/pallas_call | solution.py:607
  49.5 12.4 %all-to-all-done = f32[128,1,1280]{2,1,0:T(1,128)S(1)} async-done(((f32[128,1,1280]{2,1,0:T(1,128)}), f32[128,1,1280]{2,1,0:T(1,128)S(1)}, u32[]{:S(2)}, u32[]{:S(2)}) %all-to-all-start) | async-done | bytes 655392 | tf_op jit(solution)/shard_map/all_to_all | solution.py:603
  61.9 5.8 %collective-permute-start.4 = (f32[1280,128]{1,0:T(8,128)S(1)}, f32[1280,128]{1,0:T(8,128)S(1)}, u32[]{:S(2)}, u32[]{:S(2)}) collective-permute-start(f32[1280,128]{1,0:T(8,128)S(1)} %bitcast.13), channel_id=1, source_target_pairs={{0,1},{1,0},{2,3},{3,2},{4,5},{5,4},{6,7},{7,6},{8,9},{9,8},{10,11... | collective-permute-start | bytes 1966088 | tf_op jit(solution)/shard_map/ppermute | solution.py:617
  67.7 2.1 %shard_map.136 = (bf16[640,1280]{1,0:T(8,128)(2,1)S(1)}, f32[256,640]{1,0:T(8,128)S(1)}) custom-call(s32[1]{0:T(128)} %bitcast.11.lev_ref, f32[1280,128]{1,0:T(8,128)S(1)} %bitcast.14), custom_call_target="tpu_custom_call" | custom-call | tf_op jit(solution)/shard_map/pallas_call | solution.py:478
  69.8 0.0 collective-permute-done.4.par_ref
  69.8 2.9 %shard_map.137 = (f32[256,640]{1,0:T(8,128)}, f32[32,640]{1,0:T(8,128)}) custom-call(s32[1]{0:T(128)} %bitcast.11.lev_ref, f32[256,640]{1,0:T(8,128)S(1)} %get-tuple-element.63.half_ref, f32[1280,128]{1,0:T(8,128)S(1)} %collective-permute-done.4.par_ref, bf16[640,1280]{1,0:T(8,128)(2,1)S(1)} %get-tuple-element.64.pick_ref), custom_call_target="tpu_custom_call" | custom-call | tf_op jit(solution)/shard_map/pallas_call | solution.py:478
Async XLA Ops:
  6.4 4.3 %collective-permute-start = (f32[128,128]{1,0:T(8,128)S(1)}, f32[128,128]{1,0:T(8,128)S(1)}, u32[]{:S(2)}, u32[]{:S(2)}) collective-permute-start(f32[128,128]{1,0:T(8,128)S(1)} %get-tuple-element.35), channel_id=1, source_target_pairs={{0,2},{2,0},{4,6},{6,4},{8,10},{10,8},{12,14},{14,12},{16,18},{18,... | collective-permute-start | bytes 196616 | tf_op jit(solution)/shard_map/ppermute | solution.py:493
  8.5 2.2 %collective-permute-start.1 = (f32[128,128]{1,0:T(8,128)S(1)}, f32[128,128]{1,0:T(8,128)S(1)}, u32[]{:S(2)}, u32[]{:S(2)}) collective-permute-start(f32[128,128]{1,0:T(8,128)S(1)} %get-tuple-element.35), channel_id=1, source_target_pairs={{2,4},{4,2},{6,8},{8,6},{10,12},{12,10},{14,16},{16,14},{18,20},{2... | collective-permute-start | bytes 196616 | tf_op jit(solution)/shard_map/ppermute | solution.py:493
  10.9 8.1 %collective-permute-start.2 = (f32[128,128]{1,0:T(8,128)S(1)}, f32[128,128]{1,0:T(8,128)S(1)}, u32[]{:S(2)}, u32[]{:S(2)}) collective-permute-start(f32[128,128]{1,0:T(8,128)S(1)} %get-tuple-element.47), channel_id=1, source_target_pairs={{0,64},{64,0},{2,66},{66,2},{4,68},{68,4},{6,70},{70,6},{8,72},{72... | collective-permute-start | bytes 196616 | tf_op jit(solution)/shard_map/ppermute | solution.py:493
  13.9 5.1 %collective-permute-start.3 = (f32[128,128]{1,0:T(8,128)S(1)}, f32[128,128]{1,0:T(8,128)S(1)}, u32[]{:S(2)}, u32[]{:S(2)}) collective-permute-start(f32[128,128]{1,0:T(8,128)S(1)} %get-tuple-element.47), channel_id=1, source_target_pairs={{64,128},{128,64},{66,130},{130,66},{68,132},{132,68},{70,134},{13... | collective-permute-start | bytes 196616 | tf_op jit(solution)/shard_map/ppermute | solution.py:493
  19.0 2.8 %copy-start = (f32[16,128,256]{2,1,0:T(8,128)}, f32[16,128,256]{2,1,0:T(8,128)S(1)}, u32[]{:S(2)}) copy-start(f32[16,128,256]{2,1,0:T(8,128)S(1)} %get-tuple-element.57.held_ref.xd_ref) | copy-start | bytes 6291460
  19.0 2.8 %copy-start.2 = (bf16[12,256,256]{2,1,0:T(8,128)(2,1)}, bf16[12,256,256]{2,1,0:T(8,128)(2,1)S(1)}, u32[]{:S(2)}) copy-start(bf16[12,256,256]{2,1,0:T(8,128)(2,1)S(1)} %get-tuple-element.58.far_held_ref.far_ref) | copy-start | bytes 4718596
  21.7 40.1 %all-to-all-start = ((f32[128,1,1280]{2,1,0:T(1,128)}), f32[128,1,1280]{2,1,0:T(1,128)S(1)}, u32[]{:S(2)}, u32[]{:S(2)}) async-start(f32[128,1,1280]{2,1,0:T(1,128)} %bitcast.8), calls=%async_computation | async-start | bytes 1310720 | tf_op jit(solution)/shard_map/all_to_all | solution.py:603
  43.6 1.6 %copy-start.1 = (f32[16,128,256]{2,1,0:T(8,128)S(1)}, f32[16,128,256]{2,1,0:T(8,128)}, u32[]{:S(2)}) copy-start(f32[16,128,256]{2,1,0:T(8,128)} %copy-done) | copy-start | bytes 6291460
  45.2 1.4 %copy-start.3 = (bf16[12,256,256]{2,1,0:T(8,128)(2,1)S(1)}, bf16[12,256,256]{2,1,0:T(8,128)(2,1)}, u32[]{:S(2)}) copy-start(bf16[12,256,256]{2,1,0:T(8,128)(2,1)} %copy-done.2) | copy-start | bytes 4718596
  61.9 7.9 %collective-permute-start.4 = (f32[1280,128]{1,0:T(8,128)S(1)}, f32[1280,128]{1,0:T(8,128)S(1)}, u32[]{:S(2)}, u32[]{:S(2)}) collective-permute-start(f32[1280,128]{1,0:T(8,128)S(1)} %bitcast.13), channel_id=1, source_target_pairs={{0,1},{1,0},{2,3},{3,2},{4,5},{5,4},{6,7},{7,6},{8,9},{9,8},{10,11... | collective-permute-start | bytes 1966088 | tf_op jit(solution)/shard_map/ppermute | solution.py:617

commit v3 on v2

--- a/solution.py
+++ b/solution.py
@@ -57,6 +57,15 @@
     return jnp.where(mask, 1.0, 0.0).astype(BF16)
 
 
+def rows_hot(count, *codes):
+    row = lax.broadcasted_iota(jnp.int16, (count, codes[0].shape[1]), 0)
+    mask = None
+    for code in codes:
+        here = row == code.astype(jnp.int16)
+        mask = here if mask is None else mask | here
+    return jnp.where(mask, jnp.ones((), BF16), jnp.zeros((), BF16))
+
+
 def split(x, axis=0):
     high = x.astype(BF16)
     low = (x - high.astype(F32)).astype(BF16)
@@ -98,7 +107,7 @@
 def flux_kernel(
     block_cols, own_ref, tr_hbm, lm_hbm, wd_hbm, sph_hbm, peer_hbm, slot_hbm, flip_hbm, pub_hbm, table_hbm, next_hbm, inv_hbm,
     x_ref, one_ref, two_ref, info_ref, sph_ref, peer_ref, slot_ref, flip_ref, pub_ref, table_ref, next_ref, inv_ref,
-    tr_ref, lm_ref, wd_ref, sems
+    tr_ref, lm_ref, wd_ref, flow_ref, sems
 ):
     deriv = lagrange_derivative() * TIME_STEP
     levels = lm_ref.shape[1] // 16
@@ -141,15 +150,19 @@
         for copy in big[half]:
             copy.wait()
         tr_half, lm_half, wd_half = tr_ref.at[half], lm_ref.at[half], wd_ref.at[half]
+        for k in range(16):
+            flow_ref[0, k] = lm_half[pl.ds(k, levels, stride=16), :]
+            flow_ref[1, k] = wd_half[pl.ds(k, levels, stride=16), :]
+            flow_ref[2, k] = wd_half[pl.ds(levels * 16 + k, levels, stride=16), :]
 
         def one(t, carry):
             mass, fa, fb = [], [], []
             for k in range(16):
                 tr = tr_half[pl.ds(t * (levels * 16) + k, levels, stride=16), :]
-                mk = tr * lm_half[pl.ds(k, levels, stride=16), :]
+                mk = tr * flow_ref[0, k]
                 mass.append(mk)
-                fa.append(mk * wd_half[pl.ds(k, levels, stride=16), :])
-                fb.append(mk * wd_half[pl.ds(levels * 16 + k, levels, stride=16), :])
+                fa.append(mk * flow_ref[1, k])
+                fb.append(mk * flow_ref[2, k])
             for k in range(16):
                 j, i = k // 4, k % 4
                 value = mass[k]
@@ -163,15 +176,11 @@
 
         lax.fori_loop(0, tracers, one, 0)
 
-    lane = iota((256, elems), 0)
     total = None
     for group in [[pair] for pair in EDGE_SLOTS] + CORNER_SIDES:
-        pick = None
-        for s, m in group:
-            here = lane == base[:, s * elems : (s + 1) * elems] + m * PER_SIDE
-            pick = here if pick is None else pick | here
+        pick = rows_hot(256, *[base[:, s * elems : (s + 1) * elems] + m * PER_SIDE for s, m in group])
         s, m = group[0]
-        part = dot_nt(split(x_ref[SIDE_POINTS[s][m]]), hot(pick))
+        part = dot_nt(split(x_ref[SIDE_POINTS[s][m]]), pick)
         total = part if total is None else total + part
     fields = total.shape[0] // 2
     total = total[:fields] + total[fields:]
@@ -209,13 +218,10 @@
     recv_ref[...] = jnp.broadcast_to(recv, recv_ref.shape)
     base = info_ref[:1, :]
     second = jnp.where(base >= 128, base - 128, -1000)
-    lane = iota((128, elems), 0)
     sent, got = [], []
     for c in range(4):
-        (sa, ma), (sb, mb) = CORNER_SIDES[c]
-        got.append(hot((lane == arrive(recv, flip, elems, sa, ma)) | (lane == arrive(recv, flip, elems, sb, mb))))
-        here = [lane == second[:, s * elems : (s + 1) * elems] + m * PER_SIDE for s, m in CORNER_SIDES[c]]
-        sent.append(hot(here[0] | here[1]))
+        got.append(rows_hot(128, *[arrive(recv, flip, elems, s, m) for s, m in CORNER_SIDES[c]]))
+        sent.append(rows_hot(128, *[second[:, s * elems : (s + 1) * elems] + m * PER_SIDE for s, m in CORNER_SIDES[c]]))
     mid_ref[...] = dot_nt(jnp.concatenate(got, axis=1), jnp.concatenate(sent, axis=1)).astype(BF16)
 
     levels = next_ref.shape[1] // 16
@@ -270,14 +276,12 @@
     sides = 4 * elems
     peer, slot, flip = wide(peer_ref), wide(slot_ref), wide(flip_ref)
     recv = recv_ref[:1, :]
-    lane = iota((256, elems), 0)
     corner_far = []
     for c in range(4):
-        (sa, ma), (sb, mb) = CORNER_SIDES[c]
-        corner_far.append(hot((lane == arrive(recv, flip, elems, sa, ma)) | (lane == arrive(recv, flip, elems, sb, mb))))
+        corner_far.append(rows_hot(256, *[arrive(recv, flip, elems, s, m) for s, m in CORNER_SIDES[c]]))
     corner_far = jnp.concatenate(corner_far, axis=1)
     for number, (s, m) in enumerate(EDGE_SLOTS):
-        far_ref[4 + number] = hot(lane == arrive(recv, flip, elems, s, m))
+        far_ref[4 + number] = rows_hot(256, arrive(recv, flip, elems, s, m))
 
     local = peer == own
     slot_c = jnp.clip(slot, 0, 4 * elems - 1)
@@ -290,17 +294,15 @@
 
     cpeer, cslot, cflip = wide(peer_ref, 4), wide(slot_ref, 4), wide(flip_ref, 4)
     third = corner_source(jnp.clip(cslot, 0, 4 * elems - 1), cflip, cpeer == own)
-    source = iota((sides, elems), 0)
     weights = []
     for c in range(4):
         cols = slice(c * elems, (c + 1) * elems)
-        weight = jnp.where(source == third[:, cols], 1.0, 0.0)
+        codes = [third[:, cols]]
         for s, m in CORNER_SIDES[c]:
             own_cols = slice(s * elems, (s + 1) * elems)
             end = jnp.where(flip[:, own_cols] == 1, 1 - m // 3, m // 3)
-            code = corner_source(slot_c[:, own_cols], end, local[:, own_cols])
-            weight = weight + jnp.where(source == code, 1.0, 0.0)
-        weights.append(weight.astype(BF16))
+            codes.append(corner_source(slot_c[:, own_cols], end, local[:, own_cols]))
+        weights.append(rows_hot(sides, *codes))
     corners = jnp.concatenate([x_ref[p] for p in CORNER_POINTS], axis=1)
     lhs = jnp.concatenate([split(corners), corner_far], axis=0)
     for c in range(4):
@@ -314,7 +316,7 @@
     inner = jnp.concatenate(inner, axis=0)
     for s in range(4):
         cols = slice(s * elems, (s + 1) * elems)
-        got = dot_nn(inner, hot(source == near[:, cols]))
+        got = dot_nn(inner, rows_hot(sides, near[:, cols]))
         one = got[:fields] + got[fields : 2 * fields]
         two = got[2 * fields : 3 * fields] + got[3 * fields :]
         turned = flip[:, cols] == 1
@@ -369,11 +371,10 @@
     add = add[:fields] + add[fields:]
     mix_hl = split(mix_ref[...] + add * jnp.concatenate([rden_ref[...]] * (fields // levels), axis=0))
     peers = rows_ref.shape[1]
-    chunk = 128
+    chunk = 512
     key = key_ref[:1, :]
-    row_of = iota((chunk, key.shape[1]), 0)
     for block in range(peers * 8 // chunk):
-        res = dot_nt(hot(row_of == key - block * chunk), mix_hl)
+        res = dot_nt(rows_hot(chunk, key - block * chunk), mix_hl)
         res = res[:, :fields] + res[:, fields:]
         for d in range(chunk // 8):
             row = (block * (chunk // 8) + d) * ROWS
@@ -382,7 +383,15 @@
     out_ref[pl.ds(9, peers, stride=ROWS), :] = rows_ref[1]
 
 
-def mass_kernel(xd_ref, one_ref, two_ref, far_ref, inv_ref, tm_ref):
+def mass_kernel(xd_ref, one_ref, two_ref, far_ref, inv_ref, tm_ref, frame_ref):
+    @pl.when(pl.program_id(0) == 0)
+    def _():
+        total = frame_ref.shape[0]
+        row, lane = iota((total, 128), 0), iota((total, 128), 1)
+        source = row // ROWS
+        frame_ref[:, :128] = hot(lane == source)
+        frame_ref[:, 128:] = hot(lane // 16 == row - ROWS * source)
+
     fields = xd_ref.shape[1]
     got = split(jnp.concatenate([one_ref[...], two_ref[...]], axis=1))
     for k in range(16):
@@ -393,54 +402,52 @@
         tm_ref[pl.ds(k, fields, stride=16), :] = value * inv_ref[k : k + 1, :]
 
 
-def gathered(buf_ref, pick_ref, levels):
-    total, fields = buf_ref.shape
+def gathered(buf_ref, pick_ref, meta_ref, levels):
+    total = buf_ref.shape[0]
     peers = total // ROWS
     slots = pick_ref.shape[0]
-    thick = buf_ref[pl.ds(8, peers, stride=ROWS), :]
-    spread = hot(iota((total, peers), 0) // ROWS == iota((total, peers), 1))
-    rows = dot_nn(spread, split(thick, axis=1))
-    keep = iota((total, 128), 1) // levels == iota((total, 128), 0) % ROWS
-    rows = split(jnp.where(keep, rows[:, :128] + rows[:, 128:], 0.0), axis=0)
-    fold = hot(iota((128, 128), 1) == iota((128, 128), 0) % levels)
-    narrow = dot_nn(rows, fold)
-    narrow = narrow[:total] + narrow[total:]
-    narrow = jnp.where(iota((total, 128), 1) == levels, 1.0, narrow)
-    stack = split(jnp.concatenate([buf_ref[...], narrow], axis=1), axis=1)
-    width = fields + 128
+    meta = meta_ref[...]
+    thick = dot_nn(meta[:, :128], split(buf_ref[pl.ds(8, peers, stride=ROWS), :], axis=1))
+    thick = (thick[:, :128] + thick[:, 128:]) * meta[:, 128:].astype(F32)
+    row, lane = iota((384, 128), 0), iota((384, 128), 1)
+    fold = hot(jnp.where(row < 256, row % levels, levels) == lane)
+    narrow = dot_nn(jnp.concatenate([split(thick, axis=1), meta[:, :128]], axis=1), fold)
+    stack = split(buf_ref[...], axis=1)
     outs = []
     for block in range(slots // 128):
-        got = dot_nn(pick_ref[block * 128 : (block + 1) * 128, :], stack)
-        outs.append(jnp.transpose(got[:, :width] + got[:, width:]))
+        rows = slice(block * 128, (block + 1) * 128)
+        got = dot_nn(pick_ref[rows, :], stack)
+        outs.append(jnp.concatenate([jnp.transpose(got[:, :128] + got[:, 128:]), jnp.transpose(narrow[rows])], axis=0))
     return outs
 
 
-def place_kernel(lev_ref, own_ref, pick_ref, half_ref, *, levels):
+def place_kernel(lev_ref, own_ref, frame_ref, pick_ref, meta_ref, half_ref, *, levels):
     total = own_ref.shape[0]
     peers = total // ROWS
     slots = pick_ref.shape[0]
     ids = own_ref[pl.ds(9, peers, stride=ROWS), :]
-    spread = hot(iota((peers, total), 1) // ROWS == iota((peers, total), 0))
     ids_t = jnp.transpose(ids)[:16, :]
-    cand = dot_nn(split(ids_t), spread)
+    cand = dot_nt(split(ids_t), frame_ref[:, :128])
     cand = cand[:16] + cand[16:]
     spot = iota((16, total), 1) % ROWS
     key = jnp.sum(jnp.where((spot == iota((16, total), 0)) & (spot < 8), cand, 0.0), axis=0, keepdims=True)
-    key = jnp.where(iota((1, total), 1) % ROWS < 8, key, -1e6).astype(jnp.int32)
+    key = jnp.where(iota((1, total), 1) % ROWS < 8, key, -9999.0).astype(jnp.int32)
     key = key - lev_ref[0] * slots
     for block in range(slots // 128):
-        pick_ref[block * 128 : (block + 1) * 128, :] = hot(iota((128, total), 0) + block * 128 == key)
-    for block, got in enumerate(gathered(own_ref, pick_ref, levels)):
+        rows = slice(block * 128, (block + 1) * 128)
+        pick_ref[rows, :] = rows_hot(128, key - block * 128)
+        meta_ref[rows, :] = dot_nn(pick_ref[rows, :], frame_ref[...]).astype(BF16)
+    for block, got in enumerate(gathered(own_ref, pick_ref, meta_ref, levels)):
         half_ref[:, block * 128 : (block + 1) * 128] = got
 
 
-def physics_kernel(lev_ref, half_ref, par_ref, pick_ref, mix_ref, sig_ref):
+def physics_kernel(lev_ref, half_ref, par_ref, pick_ref, meta_ref, mix_ref, sig_ref):
     lev = lev_ref[0]
     levels2 = sig_ref.shape[0]
     fields = par_ref.shape[1]
     levels = levels2 // 2
     tracers = fields // levels
-    for block, other in enumerate(gathered(par_ref, pick_ref, levels)):
+    for block, other in enumerate(gathered(par_ref, pick_ref, meta_ref, levels)):
         cols = slice(block * 128, (block + 1) * 128)
         mine = half_ref[:, cols]
         first = jnp.where(lev == 0, mine, other)
@@ -557,6 +564,7 @@
             pltpu.VMEM((2, fields * points, half), F32),
             pltpu.VMEM((2, rows, half), F32),
             pltpu.VMEM((2, 2 * rows, half), F32),
+            pltpu.VMEM((3, points, level_count, half), F32),
             pltpu.SemaphoreType.DMA((15,)),
         ],
     )
@@ -604,29 +612,32 @@
         send.reshape(sfc_count, 1, ROWS * fields), "sfc", split_axis=0, concat_axis=0, tiled=True
     ).reshape(ROWS * sfc_count, fields)
     whole = pl.BlockSpec((fields, 128), lambda i: (0, 0))
-    mass = pl.pallas_call(
+    mass, frame = pl.pallas_call(
         mass_kernel,
         grid=(2,),
-        out_shape=jax.ShapeDtypeStruct((fields * points, elems), F32),
+        out_shape=[
+            jax.ShapeDtypeStruct((fields * points, elems), F32),
+            jax.ShapeDtypeStruct((ROWS * sfc_count, 256), BF16),
+        ],
         in_specs=[halved(local.shape), whole, whole, halved(far.shape), halved(inv.shape)],
-        out_specs=halved((fields * points, elems)),
+        out_specs=[halved((fields * points, elems)), pl.BlockSpec((ROWS * sfc_count, 256), lambda i: (0, 0))],
         compiler_params=pltpu.CompilerParams(vmem_limit_bytes=12 * 1024 * 1024),
         cost_estimate=pl.CostEstimate(flops=2 * 256 * 256 * 3072, bytes_accessed=16 * fields * points * elems, transcendentals=0),
     )(local, got_one, got_two, far, inv)
-    moved, mass = lax.optimization_barrier((moved, mass))
+    moved, mass, frame = lax.optimization_barrier((moved, mass, frame))
     other = lax.ppermute(moved, "lev", [(0, 1), (1, 0)])
     slots = group_width // lev_count
     levels = level_count * lev_count
     lev = lev_index.reshape(1)
-    pick, own_half = call(
+    pick, meta, own_half = call(
         functools.partial(place_kernel, levels=level_count),
-        [((slots, ROWS * sfc_count), BF16), ((fields + 128, slots), F32)],
-        [lev, moved],
+        [((slots, ROWS * sfc_count), BF16), ((slots, 256), BF16), ((fields + 128, slots), F32)],
+        [lev, moved, frame],
     )
     mixed, sigma = call(
         physics_kernel,
         [((tracer_count * levels, slots), F32), ((levels, slots), F32)],
-        [lev, own_half, other, pick],
+        [lev, own_half, other, pick, meta],
     )
     return (
         mass.reshape(tracers.shape),

time: 73 us -> 69.4 us (0.951)
  Pallas kernels: 22.3 us -> 17.6 us
  starting transfers between devices: 34.2 us -> 35.3 us
    pallas_call x7, Pallas kernels: 19.4 us -> 14.4 us  [call(): pl.pallas_call(kernel, out_shape=[out[2](*out[:2]) if len(out) > 2 else j...]
    all_to_all x1, starting transfers between devices: 21.8 us -> 23 us  [body(): lax.all_to_all(send.reshape(sfc_count, 1, ROWS * fields), 'sfc', split_ax...]
  transfers between devices with their start and end apart: 6 -> 6, of which waited for: 1 -> 2; matrix products, arithmetic and copies ran while one was open for 0% -> 0% of each run, Pallas kernels for 15% -> 13%
where the time goes in v3:
time: 69.4 us; the launch traced here: 69.1 us
  starting transfers between devices  35.3 us (51%)
  Pallas kernels  17.6 us (25%)
  waiting for transfers between devices  12.4 us (18%)
  local copies, waits for them, and re-layouts  3 us (4%)
  between operations  0.82 us (1%)
    all_to_all x1, starting transfers between devices, body(): lax.all_to_all(send.reshape(sfc_count, 1, ROWS * fields), 'sfc', split_ax...  23 us
    pallas_call x7, Pallas kernels, call(): pl.pallas_call(kernel, out_shape=[out[2](*out[:2]) if len(out) > 2 else j...  14.4 us
    all_to_all x1, waiting for transfers between devices, body(): lax.all_to_all(send.reshape(sfc_count, 1, ROWS * fields), 'sfc', split_ax...  12.3 us
    ppermute x4, starting transfers between devices, swap(): return lax.ppermute(value, 'sfc', pairs)  6.5 us
    ppermute x1, starting transfers between devices, body(): other = lax.ppermute(moved, 'lev', [(0, 1), (1, 0)])  5.84 us
    pallas_call x1, Pallas kernels, body(): pl.pallas_call(mass_kernel, grid=(2,), out_shape=[jax.ShapeDtypeStruct((f...  3.19 us
    unnamed x8, local copies, waits for them, and re-layouts  3 us
  transfers between devices with their start and end apart: 6, of which 2 were waited for; matrix products, arithmetic and copies ran while one was open for 0% of the time, Pallas kernels for 13%

profile of v3, /device:TPU:1, one launch (start us, length us, event | category | flops | bytes accessed | tf_op | source)
XLA Modules:
  0.0 69.1 jit_solution(2086425051927915650)
XLA Ops:
  0.6 4.3 %shard_map.130 = (f32[16,128,256]{2,1,0:T(8,128)S(1)}, f32[128,128]{1,0:T(8,128)S(1)}, f32[128,128]{1,0:T(8,128)S(1)}, s32[8,1024]{1,0:T(8,128)S(1)}, f32[16,256...) custom-call(s32[1]{0:T(128)} %bitcast.2.own_ref, ...), custom_call_target="tpu_custom_call" | custom-call | tf_op jit(solution)/shard_map/pallas_call | solution.py:485
  5.0 2.1 %collective-permute-start = (f32[128,128]{1,0:T(8,128)S(1)}, f32[128,128]{1,0:T(8,128)S(1)}, u32[]{:S(2)}, u32[]{:S(2)}) collective-permute-start(f32[128,128]{1,0:T(8,128)S(1)} %get-tuple-element.39), channel_id=1, source_target_pairs={{0,2},{2,0},{4,6},{6,4},{8,10},{10,8},{12,14},{14,12},{16,18},{18,... | collective-permute-start | bytes 196616 | tf_op jit(solution)/shard_map/ppermute | solution.py:500
  7.1 0.7 collective-permute-start.1
  7.8 1.3 %shard_map.131 = (s32[8,1024]{1,0:T(8,128)S(1)}, bf16[128,128]{1,0:T(8,128)(2,1)S(1)}, s32[8,1024]{1,0:T(8,128)S(1)}, f32[16,1024]{1,0:T(8,128)S(1)}, f32[2,128,128]{2,1,0:T(8,128)S(1)}) custom-call(s32[1]{0:T(128)} %bitcast.2.own_ref, s32[8,256]{1,0:T(8,128)S(1)} %get-tuple-element.41.peer_ref, s32[8,256]{1,0:T(8,128)S(1)} %get-tuple-element.42.flip_ref, ...), custom_call_target="tpu_custom_call" | custom-call | tf_op jit(solution)/shard_map/pallas_call | solution.py:485
  9.1 0.0 collective-permute-done.a_ref
  9.1 0.0 collective-permute-done.1.b_ref
  9.1 0.2 shard_map.132
  9.3 3.1 %collective-permute-start.2 = (f32[128,128]{1,0:T(8,128)S(1)}, f32[128,128]{1,0:T(8,128)S(1)}, u32[]{:S(2)}, u32[]{:S(2)}) collective-permute-start(f32[128,128]{1,0:T(8,128)S(1)} %get-tuple-element.51), channel_id=1, source_target_pairs={{0,64},{64,0},{2,66},{66,2},{4,68},{68,4},{6,70},{70,6},{8,72},{72... | collective-permute-start | bytes 196616 | tf_op jit(solution)/shard_map/ppermute | solution.py:500
  12.4 0.7 collective-permute-start.3
  13.1 3.1 %shard_map.133 = (f32[16,128,256]{2,1,0:T(8,128)S(1)}, bf16[12,256,256]{2,1,0:T(8,128)(2,1)S(1)}, bf16[2,256,1024]{2,1,0:T(8,128)(2,1)S(1)}, f32[128,1024]{1,0:T(8,128)S(1)}) custom-call(s32[1]{0:T(128)} %bitcast.2.own_ref, f32[16,128,256]{2,1,0:T(8,128)S(1)} %get-tuple-element.52.held_ref.x_ref, s32[8,256]{1,0:T(8,128)S(1)} %get-tuple-element.41.peer_ref, ...), custom_call_target="tpu_custom_call" | custom-call | tf_op jit(solution)/shard_map/pallas_call | solution.py:485
  16.2 0.0 copy-start
  16.2 0.0 copy-start.2
  16.2 0.0 collective-permute-done.2.a_ref
  16.2 0.0 collective-permute-done.3.b_ref
  16.2 2.0 %shard_map.134 = (f32[128,128]{1,0:T(8,128)S(1)}, f32[1280,128]{1,0:T(8,128)}) custom-call(s32[1]{0:T(128)} %bitcast.odd_ref, f32[128,128]{1,0:T(8,128)S(1)} %get-tuple-element.50.one_ref, f32[128,128]{1,0:T(8,128)S(1)} %collective-permute-done.2.a_ref, f32[128,128]{1,0:T(8,128)S(1)} %collective-permute-done.3.b_ref, ...), custom_call_target="tpu_custom_call" | custom-call | tf_op jit(solution)/shard_map/pallas_call | solution.py:485
  18.2 0.0 copy-done
  18.2 0.0 copy-done.2
  18.2 23.0 %all-to-all-start = ((f32[128,1,1280]{2,1,0:T(1,128)}), f32[128,1,1280]{2,1,0:T(1,128)S(1)}, u32[]{:S(2)}, u32[]{:S(2)}) async-start(f32[128,1,1280]{2,1,0:T(1,128)} %bitcast.8), calls=%async_computation | async-start | bytes 1310720 | tf_op jit(solution)/shard_map/all_to_all | solution.py:611
  41.2 0.0 copy-start.1
  41.2 1.6 %copy-done.1 = f32[16,128,256]{2,1,0:T(8,128)S(1)} copy-done((f32[16,128,256]{2,1,0:T(8,128)S(1)}, f32[16,128,256]{2,1,0:T(8,128)}, u32[]{:S(2)}) %copy-start.1) | copy-done | bytes 2097176
  42.8 0.0 copy-start.3
  42.8 1.4 %copy-done.3 = bf16[12,256,256]{2,1,0:T(8,128)(2,1)S(1)} copy-done((bf16[12,256,256]{2,1,0:T(8,128)(2,1)S(1)}, bf16[12,256,256]{2,1,0:T(8,128)(2,1)}, u32[]{:S(2)}) %copy-start.3) | copy-done | bytes 1572888
  44.2 3.2 %shard_map.135 = (f32[2048,256]{1,0:T(8,128)}, bf16[1280,256]{1,0:T(8,128)(2,1)S(1)}) custom-call(f32[16,128,256]{2,1,0:T(8,128)S(1)} %copy-done.1, f32[128,128]{1,0:T(8,128)S(1)} %get-tuple-element.50.one_ref, f32[128,128]{1,0:T(8,128)S(1)} %get-tuple-element.64.two_ref, bf16[12,256,256]{2,1,0:T(8,128)(2,1)S(1)} %copy-done.3, ...), custom_call_target="tpu_custom_call" | custom-call | flops 402653184 | bytes 8388608 | tf_op jit(solution)/shard_map/pallas_call | solution.py:615
  47.4 12.3 %all-to-all-done = f32[128,1,1280]{2,1,0:T(1,128)S(1)} async-done(((f32[128,1,1280]{2,1,0:T(1,128)}), f32[128,1,1280]{2,1,0:T(1,128)S(1)}, u32[]{:S(2)}, u32[]{:S(2)}) %all-to-all-start) | async-done | bytes 655392 | tf_op jit(solution)/shard_map/all_to_all | solution.py:611
  59.6 5.8 %collective-permute-start.4 = (f32[1280,128]{1,0:T(8,128)S(1)}, f32[1280,128]{1,0:T(8,128)S(1)}, u32[]{:S(2)}, u32[]{:S(2)}) collective-permute-start(f32[1280,128]{1,0:T(8,128)S(1)} %bitcast.13), channel_id=1, source_target_pairs={{0,1},{1,0},{2,3},{3,2},{4,5},{5,4},{6,7},{7,6},{8,9},{9,8},{10,11... | collective-permute-start | bytes 1966088 | tf_op jit(solution)/shard_map/ppermute | solution.py:628
  65.5 1.6 %shard_map.136 = (bf16[640,1280]{1,0:T(8,128)(2,1)S(1)}, bf16[640,256]{1,0:T(8,128)(2,1)S(1)}, f32[256,640]{1,0:T(8,128)S(1)}) custom-call(s32[1]{0:T(128)} %bitcast.11.lev_ref, f32[1280,128]{1,0:T(8,128)S(1)} %bitcast.14, bf16[1280,256]{1,0:T(8,128)(2,1)S(1)} %get-tuple-element.69.frame_ref), custom_call_target="tpu_custom_call" | custom-call | tf_op jit(solution)/shard_map/pallas_call | solution.py:485
  67.1 0.1 collective-permute-done.4.par_ref
  67.2 1.9 %shard_map.137 = (f32[256,640]{1,0:T(8,128)}, f32[32,640]{1,0:T(8,128)}) custom-call(s32[1]{0:T(128)} %bitcast.11.lev_ref, f32[256,640]{1,0:T(8,128)S(1)} %get-tuple-element.70.half_ref, f32[1280,128]{1,0:T(8,128)S(1)} %collective-permute-done.4.par_ref, bf16[640,1280]{1,0:T(8,128)(2,1)S(1)} %get-tuple-element.71.pick_ref, ...), custom_call_target="tpu_custom_call" | custom-call | tf_op jit(solution)/shard_map/pallas_call | solution.py:485
Async XLA Ops:
  5.0 4.2 %collective-permute-start = (f32[128,128]{1,0:T(8,128)S(1)}, f32[128,128]{1,0:T(8,128)S(1)}, u32[]{:S(2)}, u32[]{:S(2)}) collective-permute-start(f32[128,128]{1,0:T(8,128)S(1)} %get-tuple-element.39), channel_id=1, source_target_pairs={{0,2},{2,0},{4,6},{6,4},{8,10},{10,8},{12,14},{14,12},{16,18},{18,... | collective-permute-start | bytes 196616 | tf_op jit(solution)/shard_map/ppermute | solution.py:500
  7.1 2.1 %collective-permute-start.1 = (f32[128,128]{1,0:T(8,128)S(1)}, f32[128,128]{1,0:T(8,128)S(1)}, u32[]{:S(2)}, u32[]{:S(2)}) collective-permute-start(f32[128,128]{1,0:T(8,128)S(1)} %get-tuple-element.39), channel_id=1, source_target_pairs={{2,4},{4,2},{6,8},{8,6},{10,12},{12,10},{14,16},{16,14},{18,20},{2... | collective-permute-start | bytes 196616 | tf_op jit(solution)/shard_map/ppermute | solution.py:500
  9.3 6.9 %collective-permute-start.2 = (f32[128,128]{1,0:T(8,128)S(1)}, f32[128,128]{1,0:T(8,128)S(1)}, u32[]{:S(2)}, u32[]{:S(2)}) collective-permute-start(f32[128,128]{1,0:T(8,128)S(1)} %get-tuple-element.51), channel_id=1, source_target_pairs={{0,64},{64,0},{2,66},{66,2},{4,68},{68,4},{6,70},{70,6},{8,72},{72... | collective-permute-start | bytes 196616 | tf_op jit(solution)/shard_map/ppermute | solution.py:500
  12.4 3.8 %collective-permute-start.3 = (f32[128,128]{1,0:T(8,128)S(1)}, f32[128,128]{1,0:T(8,128)S(1)}, u32[]{:S(2)}, u32[]{:S(2)}) collective-permute-start(f32[128,128]{1,0:T(8,128)S(1)} %get-tuple-element.51), channel_id=1, source_target_pairs={{64,128},{128,64},{66,130},{130,66},{68,132},{132,68},{70,134},{13... | collective-permute-start | bytes 196616 | tf_op jit(solution)/shard_map/ppermute | solution.py:500
  16.2 2.0 %copy-start = (f32[16,128,256]{2,1,0:T(8,128)}, f32[16,128,256]{2,1,0:T(8,128)S(1)}, u32[]{:S(2)}) copy-start(f32[16,128,256]{2,1,0:T(8,128)S(1)} %get-tuple-element.61.held_ref.xd_ref) | copy-start | bytes 6291460
  16.2 2.0 %copy-start.2 = (bf16[12,256,256]{2,1,0:T(8,128)(2,1)}, bf16[12,256,256]{2,1,0:T(8,128)(2,1)S(1)}, u32[]{:S(2)}) copy-start(bf16[12,256,256]{2,1,0:T(8,128)(2,1)S(1)} %get-tuple-element.62.far_held_ref.far_ref) | copy-start | bytes 4718596
  18.2 41.4 %all-to-all-start = ((f32[128,1,1280]{2,1,0:T(1,128)}), f32[128,1,1280]{2,1,0:T(1,128)S(1)}, u32[]{:S(2)}, u32[]{:S(2)}) async-start(f32[128,1,1280]{2,1,0:T(1,128)} %bitcast.8), calls=%async_computation | async-start | bytes 1310720 | tf_op jit(solution)/shard_map/all_to_all | solution.py:611
  41.2 1.6 %copy-start.1 = (f32[16,128,256]{2,1,0:T(8,128)S(1)}, f32[16,128,256]{2,1,0:T(8,128)}, u32[]{:S(2)}) copy-start(f32[16,128,256]{2,1,0:T(8,128)} %copy-done) | copy-start | bytes 6291460
  42.8 1.4 %copy-start.3 = (bf16[12,256,256]{2,1,0:T(8,128)(2,1)S(1)}, bf16[12,256,256]{2,1,0:T(8,128)(2,1)}, u32[]{:S(2)}) copy-start(bf16[12,256,256]{2,1,0:T(8,128)(2,1)} %copy-done.2) | copy-start | bytes 4718596
  59.6 7.6 %collective-permute-start.4 = (f32[1280,128]{1,0:T(8,128)S(1)}, f32[1280,128]{1,0:T(8,128)S(1)}, u32[]{:S(2)}, u32[]{:S(2)}) collective-permute-start(f32[1280,128]{1,0:T(8,128)S(1)} %bitcast.13), channel_id=1, source_target_pairs={{0,1},{1,0},{2,3},{3,2},{4,5},{5,4},{6,7},{7,6},{8,9},{9,8},{10,11... | collective-permute-start | bytes 1966088 | tf_op jit(solution)/shard_map/ppermute | solution.py:628

commit v4 on v3

--- a/solution.py
+++ b/solution.py
@@ -105,8 +105,8 @@
 
 
 def flux_kernel(
-    block_cols, own_ref, tr_hbm, lm_hbm, wd_hbm, sph_hbm, peer_hbm, slot_hbm, flip_hbm, pub_hbm, table_hbm, next_hbm, inv_hbm,
-    x_ref, one_ref, two_ref, info_ref, sph_ref, peer_ref, slot_ref, flip_ref, pub_ref, table_ref, next_ref, inv_ref,
+    block_cols, own_ref, odd_ref, tr_hbm, lm_hbm, wd_hbm, sph_hbm, peer_hbm, slot_hbm, flip_hbm, pub_hbm, table_hbm, next_hbm, inv_hbm,
+    x_ref, one_a_ref, one_b_ref, two_ref, info_ref, sph_ref, peer_ref, slot_ref, flip_ref, pub_ref, table_ref, next_ref, inv_ref,
     tr_ref, lm_ref, wd_ref, flow_ref, sems
 ):
     deriv = lagrange_derivative() * TIME_STEP
@@ -133,10 +133,6 @@
                 fetch(tr_hbm.at[:, cut], tr_ref.at[half]),
             ]
         )
-    later = [fetch(flip_hbm, flip_ref), fetch(pub_hbm, pub_ref), fetch(table_hbm, table_ref), fetch(inv_hbm, inv_ref)]
-    for half in range(2):
-        later.append(fetch(next_hbm.at[:, half * lanes : (half + 1) * lanes], next_ref.at[half]))
-
     for copy in small:
         copy.wait()
     direction = facing(wide(peer_ref), own_ref[0], block_cols)
@@ -144,6 +140,9 @@
     usable = (direction >= 0) & (rank < PER_SIDE)
     base = jnp.where(usable, direction * 64 + rank, -1000)
     info_ref[...] = jnp.broadcast_to(base, info_ref.shape)
+    later = [fetch(flip_hbm, flip_ref), fetch(pub_hbm, pub_ref), fetch(table_hbm, table_ref), fetch(inv_hbm, inv_ref)]
+    for half in range(2):
+        later.append(fetch(next_hbm.at[:, half * lanes : (half + 1) * lanes], next_ref.at[half]))
 
     for half in range(2):
         cut = slice(half * lanes, (half + 1) * lanes)
@@ -184,7 +183,7 @@
         total = part if total is None else total + part
     fields = total.shape[0] // 2
     total = total[:fields] + total[fields:]
-    one_ref[...] = total[:, :128]
+    one_a_ref[...], one_b_ref[...] = pack(odd_ref[0], total[:, :128])
     two_ref[...] = total[:, 128:]
     for copy in later:
         copy.wait()
@@ -346,19 +345,31 @@
         far_mix_ref[1, :, cols] = (far_mix - high.astype(F32)).astype(BF16)
 
 
+def pack(odd, msg):
+    half = msg.shape[0] // 2
+    low = iota((half, 128), 1) < 64
+    top, bottom = msg[:half], msg[half:]
+    above = jnp.where(low, top, pltpu.roll(bottom, 64, 1))
+    below = jnp.where(low, pltpu.roll(top, 64, 1), bottom)
+    return jnp.where(odd == 1, below, above), jnp.where(odd == 1, above, below)
+
+
 def merge(odd, a, b):
     low = iota(a.shape, 1) < 64
     lower = jnp.where(odd == 1, a, b)
     upper = jnp.where(odd == 1, b, a)
-    return jnp.where(low, lower, upper)
-
-
-def middle_kernel(odd_ref, a_ref, b_ref, two_ref, mid_ref, held_ref, got_ref, out_ref):
+    top = jnp.where(low, lower, pltpu.roll(upper, 64, 1))
+    bottom = jnp.where(low, pltpu.roll(lower, 64, 1), upper)
+    return jnp.concatenate([top, bottom], axis=0)
+
+
+def middle_kernel(odd_ref, row_odd_ref, a_ref, b_ref, two_ref, mid_ref, held_ref, got_ref, out_a_ref, out_b_ref):
     got = merge(odd_ref[0], a_ref[...], b_ref[...])
     got_ref[...] = got
     fields = got.shape[0]
     add = dot_nn(split(got), mid_ref[...])
-    out_ref[...] = two_ref[...] + add[:fields] + add[fields:]
+    msg = two_ref[...] + add[:fields] + add[fields:]
+    out_a_ref[...], out_b_ref[...] = pack(row_odd_ref[0], msg)
 
 
 def send_kernel(odd_ref, one_ref, a_ref, b_ref, far_mix_ref, mix_ref, rden_ref, key_ref, rows_ref, held_ref, far_held_ref, two_ref, out_ref):
@@ -530,6 +541,7 @@
     ints = jnp.int32
     ins = [
         own,
+        col_odd,
         tracers.reshape(fields * points, elems),
         layer_mass.reshape(rows, elems),
         wind.reshape(2 * rows, elems),
@@ -542,11 +554,12 @@
         layer_mass_next.reshape(rows, elems),
         inverse_mass,
     ]
-    weighted, first, second, info, sph, peer, slot, flip, pub, table, after, inv = call(
+    weighted, first_a, first_b, second, info, sph, peer, slot, flip, pub, table, after, inv = call(
         functools.partial(flux_kernel, block_cols),
         [
             ((points, fields, elems), F32, pltpu.VMEM),
-            ((fields, 128), F32),
+            ((fields // 2, 128), F32),
+            ((fields // 2, 128), F32),
             ((fields, 128), F32),
             ((8, 4 * elems), ints),
             (spheremp.shape, F32),
@@ -559,7 +572,7 @@
             (inverse_mass.shape, F32),
         ],
         ins,
-        hbm=range(1, len(ins)),
+        hbm=range(2, len(ins)),
         scratch=[
             pltpu.VMEM((2, fields * points, half), F32),
             pltpu.VMEM((2, rows, half), F32),
@@ -568,8 +581,8 @@
             pltpu.SemaphoreType.DMA((15,)),
         ],
     )
-    near_a = swap(first, 1, 0, sfc_count, block_cols)
-    near_b = swap(first, 1, 1, sfc_count, block_cols)
+    near_a = swap(first_a, 1, 0, sfc_count, block_cols)
+    near_b = swap(first_b, 1, 1, sfc_count, block_cols)
     group_width = 5 * NPG * elems // 4
     recv, mid, key, rden, extra = call(
         functools.partial(plan_kernel, block_cols, group_width),
@@ -583,15 +596,15 @@
         [own, peer, flip, pub, info, table, after, sph, weighted],
         held=(8,),
     )
-    got_one, second = call(
+    got_one, second_a, second_b = call(
         middle_kernel,
-        [((fields, 128), F32), ((fields, 128), F32)],
-        [col_odd, near_a, near_b, second, mid, weighted],
-        held=(5,),
-    )
-    over_a = swap(second, block_cols, 0, sfc_count)
-    over_b = swap(second, block_cols, 1, sfc_count)
-    weighted, _ = lax.optimization_barrier((weighted, second))
+        [((fields, 128), F32), ((fields // 2, 128), F32), ((fields // 2, 128), F32)],
+        [col_odd, row_odd, near_a, near_b, second, mid, weighted],
+        held=(6,),
+    )
+    over_a = swap(second_a, block_cols, 0, sfc_count)
+    over_b = swap(second_b, block_cols, 1, sfc_count)
+    weighted, _ = lax.optimization_barrier((weighted, second_a))
     local, far, far_mix, mix = call(
         local_kernel,
         [

time: 69.4 us -> 67.7 us (0.976)
  starting transfers between devices: 35.3 us -> 33.4 us
    all_to_all x1, starting transfers between devices: 23 us -> 15.6 us  [body(): lax.all_to_all(send.reshape(sfc_count, 1, ROWS * fields), 'sfc', split_ax...]
    ppermute x4, starting transfers between devices: 6.5 us -> 12 us  [swap(): return lax.ppermute(value, 'sfc', pairs)]
  transfers between devices with their start and end apart: 6 -> 6, of which waited for: 2 -> 2; matrix products, arithmetic and copies ran while one was open for 0% -> 0% of each run, Pallas kernels for 13% -> 14%
where the time goes in v4:
time: 67.7 us; the launch traced here: 67.4 us
  starting transfers between devices  33.4 us (49%)
  Pallas kernels  17.8 us (26%)
  waiting for transfers between devices  12.4 us (18%)
  local copies, waits for them, and re-layouts  3 us (4%)
  between operations  0.82 us (1%)
    all_to_all x1, starting transfers between devices, body(): lax.all_to_all(send.reshape(sfc_count, 1, ROWS * fields), 'sfc', split_ax...  15.6 us
    pallas_call x7, Pallas kernels, call(): pl.pallas_call(kernel, out_shape=[out[2](*out[:2]) if len(out) > 2 else j...  14.7 us
    all_to_all x1, waiting for transfers between devices, body(): lax.all_to_all(send.reshape(sfc_count, 1, ROWS * fields), 'sfc', split_ax...  12.3 us
    ppermute x4, starting transfers between devices, swap(): return lax.ppermute(value, 'sfc', pairs)  12 us
    ppermute x1, starting transfers between devices, body(): other = lax.ppermute(moved, 'lev', [(0, 1), (1, 0)])  5.84 us
    pallas_call x1, Pallas kernels, body(): pl.pallas_call(mass_kernel, grid=(2,), out_shape=[jax.ShapeDtypeStruct((f...  3.19 us
    unnamed x8, local copies, waits for them, and re-layouts  3 us
  transfers between devices with their start and end apart: 6, of which 2 were waited for; matrix products, arithmetic and copies ran while one was open for 0% of the time, Pallas kernels for 14%

profile of v4, /device:TPU:1, one launch (start us, length us, event | category | flops | bytes accessed | tf_op | source)
XLA Modules:
  0.0 67.4 jit_solution(287883069377818311)
XLA Ops:
  0.7 4.4 %shard_map.130 = (f32[16,128,256]{2,1,0:T(8,128)S(1)}, f32[64,128]{1,0:T(8,128)S(1)}, f32[64,128]{1,0:T(8,128)S(1)}, f32[128,128]{1,0:T(8,128)S(1)}, s32[8,1024]...) custom-call(s32[1]{0:T(128)} %bitcast.2.own_ref, ...), custom_call_target="tpu_custom_call" | custom-call | tf_op jit(solution)/shard_map/pallas_call | solution.py:496
  5.0 2.1 %collective-permute-start = (f32[64,128]{1,0:T(8,128)S(1)}, f32[64,128]{1,0:T(8,128)S(1)}, u32[]{:S(2)}, u32[]{:S(2)}) collective-permute-start(f32[64,128]{1,0:T(8,128)S(1)} %get-tuple-element.41), channel_id=1, source_target_pairs={{0,2},{2,0},{4,6},{6,4},{8,10},{10,8},{12,14},{14,12},{16,18},{18,... | collective-permute-start | bytes 98312 | tf_op jit(solution)/shard_map/ppermute | solution.py:511
  7.2 0.7 collective-permute-start.1
  7.9 1.3 %shard_map.131 = (s32[8,1024]{1,0:T(8,128)S(1)}, bf16[128,128]{1,0:T(8,128)(2,1)S(1)}, s32[8,1024]{1,0:T(8,128)S(1)}, f32[16,1024]{1,0:T(8,128)S(1)}, f32[2,128,128]{2,1,0:T(8,128)S(1)}) custom-call(s32[1]{0:T(128)} %bitcast.2.own_ref, s32[8,256]{1,0:T(8,128)S(1)} %get-tuple-element.44.peer_ref, s32[8,256]{1,0:T(8,128)S(1)} %get-tuple-element.45.flip_ref, ...), custom_call_target="tpu_custom_call" | custom-call | tf_op jit(solution)/shard_map/pallas_call | solution.py:496
  9.2 0.0 collective-permute-done.a_ref
  9.2 0.0 collective-permute-done.1.b_ref
  9.2 0.3 shard_map.132
  9.5 0.7 collective-permute-start.3
  10.2 8.5 %collective-permute-start.2 = (f32[64,128]{1,0:T(8,128)S(1)}, f32[64,128]{1,0:T(8,128)S(1)}, u32[]{:S(2)}, u32[]{:S(2)}) collective-permute-start(f32[64,128]{1,0:T(8,128)S(1)} %get-tuple-element.54), channel_id=1, source_target_pairs={{0,64},{64,0},{2,66},{66,2},{4,68},{68,4},{6,70},{70,6},{8,72},{72... | collective-permute-start | bytes 98312 | tf_op jit(solution)/shard_map/ppermute | solution.py:511
  18.7 3.1 %shard_map.133 = (f32[16,128,256]{2,1,0:T(8,128)S(1)}, bf16[12,256,256]{2,1,0:T(8,128)(2,1)S(1)}, bf16[2,256,1024]{2,1,0:T(8,128)(2,1)S(1)}, f32[128,1024]{1,0:T(8,128)S(1)}) custom-call(s32[1]{0:T(128)} %bitcast.2.own_ref, f32[16,128,256]{2,1,0:T(8,128)S(1)} %get-tuple-element.56.held_ref.x_ref, s32[8,256]{1,0:T(8,128)S(1)} %get-tuple-element.44.peer_ref, ...), custom_call_target="tpu_custom_call" | custom-call | tf_op jit(solution)/shard_map/pallas_call | solution.py:496
  21.8 0.0 copy-start
  21.8 0.0 copy-start.2
  21.9 0.0 collective-permute-done.3.b_ref
  21.9 0.0 collective-permute-done.2.a_ref
  21.9 2.0 %shard_map.134 = (f32[128,128]{1,0:T(8,128)S(1)}, f32[1280,128]{1,0:T(8,128)}) custom-call(s32[1]{0:T(128)} %bitcast.row_odd_ref.odd_ref, f32[128,128]{1,0:T(8,128)S(1)} %get-tuple-element.53.one_ref, f32[64,128]{1,0:T(8,128)S(1)} %collective-permute-done.2.a_ref, f32[64,128]{1,0:T(8,128)S(1)} %collective-permute-done.3.b_ref, ...), custom_call_target="tpu_custom_call" | custom-call | tf_op jit(solution)/shard_map/pallas_call | solution.py:496
  23.9 0.0 copy-done
  23.9 0.0 copy-done.2
  23.9 15.6 %all-to-all-start = ((f32[128,1,1280]{2,1,0:T(1,128)}), f32[128,1,1280]{2,1,0:T(1,128)S(1)}, u32[]{:S(2)}, u32[]{:S(2)}) async-start(f32[128,1,1280]{2,1,0:T(1,128)} %bitcast.8), calls=%async_computation | async-start | bytes 1310720 | tf_op jit(solution)/shard_map/all_to_all | solution.py:624
  39.5 0.0 copy-start.1
  39.5 1.6 %copy-done.1 = f32[16,128,256]{2,1,0:T(8,128)S(1)} copy-done((f32[16,128,256]{2,1,0:T(8,128)S(1)}, f32[16,128,256]{2,1,0:T(8,128)}, u32[]{:S(2)}) %copy-start.1) | copy-done | bytes 2097176
  41.1 0.0 copy-start.3
  41.1 1.4 %copy-done.3 = bf16[12,256,256]{2,1,0:T(8,128)(2,1)S(1)} copy-done((bf16[12,256,256]{2,1,0:T(8,128)(2,1)S(1)}, bf16[12,256,256]{2,1,0:T(8,128)(2,1)}, u32[]{:S(2)}) %copy-start.3) | copy-done | bytes 1572888
  42.5 3.2 %shard_map.135 = (f32[2048,256]{1,0:T(8,128)}, bf16[1280,256]{1,0:T(8,128)(2,1)S(1)}) custom-call(f32[16,128,256]{2,1,0:T(8,128)S(1)} %copy-done.1, f32[128,128]{1,0:T(8,128)S(1)} %get-tuple-element.53.one_ref, f32[128,128]{1,0:T(8,128)S(1)} %get-tuple-element.68.two_ref, bf16[12,256,256]{2,1,0:T(8,128)(2,1)S(1)} %copy-done.3, ...), custom_call_target="tpu_custom_call" | custom-call | flops 402653184 | bytes 8388608 | tf_op jit(solution)/shard_map/pallas_call | solution.py:628
  45.7 12.3 %all-to-all-done = f32[128,1,1280]{2,1,0:T(1,128)S(1)} async-done(((f32[128,1,1280]{2,1,0:T(1,128)}), f32[128,1,1280]{2,1,0:T(1,128)S(1)}, u32[]{:S(2)}, u32[]{:S(2)}) %all-to-all-start) | async-done | bytes 655392 | tf_op jit(solution)/shard_map/all_to_all | solution.py:624
  58.0 5.8 %collective-permute-start.4 = (f32[1280,128]{1,0:T(8,128)S(1)}, f32[1280,128]{1,0:T(8,128)S(1)}, u32[]{:S(2)}, u32[]{:S(2)}) collective-permute-start(f32[1280,128]{1,0:T(8,128)S(1)} %bitcast.13), channel_id=1, source_target_pairs={{0,1},{1,0},{2,3},{3,2},{4,5},{5,4},{6,7},{7,6},{8,9},{9,8},{10,11... | collective-permute-start | bytes 1966088 | tf_op jit(solution)/shard_map/ppermute | solution.py:641
  63.8 1.6 %shard_map.136 = (bf16[640,1280]{1,0:T(8,128)(2,1)S(1)}, bf16[640,256]{1,0:T(8,128)(2,1)S(1)}, f32[256,640]{1,0:T(8,128)S(1)}) custom-call(s32[1]{0:T(128)} %bitcast.11.lev_ref, f32[1280,128]{1,0:T(8,128)S(1)} %bitcast.14, bf16[1280,256]{1,0:T(8,128)(2,1)S(1)} %get-tuple-element.73.frame_ref), custom_call_target="tpu_custom_call" | custom-call | tf_op jit(solution)/shard_map/pallas_call | solution.py:496
  65.4 0.1 collective-permute-done.4.par_ref
  65.5 1.9 %shard_map.137 = (f32[256,640]{1,0:T(8,128)}, f32[32,640]{1,0:T(8,128)}) custom-call(s32[1]{0:T(128)} %bitcast.11.lev_ref, f32[256,640]{1,0:T(8,128)S(1)} %get-tuple-element.74.half_ref, f32[1280,128]{1,0:T(8,128)S(1)} %collective-permute-done.4.par_ref, bf16[640,1280]{1,0:T(8,128)(2,1)S(1)} %get-tuple-element.75.pick_ref, ...), custom_call_target="tpu_custom_call" | custom-call | tf_op jit(solution)/shard_map/pallas_call | solution.py:496
Async XLA Ops:
  5.0 4.2 %collective-permute-start = (f32[64,128]{1,0:T(8,128)S(1)}, f32[64,128]{1,0:T(8,128)S(1)}, u32[]{:S(2)}, u32[]{:S(2)}) collective-permute-start(f32[64,128]{1,0:T(8,128)S(1)} %get-tuple-element.41), channel_id=1, source_target_pairs={{0,2},{2,0},{4,6},{6,4},{8,10},{10,8},{12,14},{14,12},{16,18},{18,... | collective-permute-start | bytes 98312 | tf_op jit(solution)/shard_map/ppermute | solution.py:511
  7.2 2.1 %collective-permute-start.1 = (f32[64,128]{1,0:T(8,128)S(1)}, f32[64,128]{1,0:T(8,128)S(1)}, u32[]{:S(2)}, u32[]{:S(2)}) collective-permute-start(f32[64,128]{1,0:T(8,128)S(1)} %get-tuple-element.42), channel_id=1, source_target_pairs={{2,4},{4,2},{6,8},{8,6},{10,12},{12,10},{14,16},{16,14},{18,20},{2... | collective-permute-start | bytes 98312 | tf_op jit(solution)/shard_map/ppermute | solution.py:511
  9.5 12.3 %collective-permute-start.3 = (f32[64,128]{1,0:T(8,128)S(1)}, f32[64,128]{1,0:T(8,128)S(1)}, u32[]{:S(2)}, u32[]{:S(2)}) collective-permute-start(f32[64,128]{1,0:T(8,128)S(1)} %get-tuple-element.55), channel_id=1, source_target_pairs={{64,128},{128,64},{66,130},{130,66},{68,132},{132,68},{70,134},{13... | collective-permute-start | bytes 98312 | tf_op jit(solution)/shard_map/ppermute | solution.py:511
  10.2 11.7 %collective-permute-start.2 = (f32[64,128]{1,0:T(8,128)S(1)}, f32[64,128]{1,0:T(8,128)S(1)}, u32[]{:S(2)}, u32[]{:S(2)}) collective-permute-start(f32[64,128]{1,0:T(8,128)S(1)} %get-tuple-element.54), channel_id=1, source_target_pairs={{0,64},{64,0},{2,66},{66,2},{4,68},{68,4},{6,70},{70,6},{8,72},{72... | collective-permute-start | bytes 98312 | tf_op jit(solution)/shard_map/ppermute | solution.py:511
  21.8 2.0 %copy-start = (f32[16,128,256]{2,1,0:T(8,128)}, f32[16,128,256]{2,1,0:T(8,128)S(1)}, u32[]{:S(2)}) copy-start(f32[16,128,256]{2,1,0:T(8,128)S(1)} %get-tuple-element.65.held_ref.xd_ref) | copy-start | bytes 6291460
  21.8 2.0 %copy-start.2 = (bf16[12,256,256]{2,1,0:T(8,128)(2,1)}, bf16[12,256,256]{2,1,0:T(8,128)(2,1)S(1)}, u32[]{:S(2)}) copy-start(bf16[12,256,256]{2,1,0:T(8,128)(2,1)S(1)} %get-tuple-element.66.far_held_ref.far_ref) | copy-start | bytes 4718596
  23.9 34.1 %all-to-all-start = ((f32[128,1,1280]{2,1,0:T(1,128)}), f32[128,1,1280]{2,1,0:T(1,128)S(1)}, u32[]{:S(2)}, u32[]{:S(2)}) async-start(f32[128,1,1280]{2,1,0:T(1,128)} %bitcast.8), calls=%async_computation | async-start | bytes 1310720 | tf_op jit(solution)/shard_map/all_to_all | solution.py:624
  39.5 1.6 %copy-start.1 = (f32[16,128,256]{2,1,0:T(8,128)S(1)}, f32[16,128,256]{2,1,0:T(8,128)}, u32[]{:S(2)}) copy-start(f32[16,128,256]{2,1,0:T(8,128)} %copy-done) | copy-start | bytes 6291460
  41.1 1.4 %copy-start.3 = (bf16[12,256,256]{2,1,0:T(8,128)(2,1)S(1)}, bf16[12,256,256]{2,1,0:T(8,128)(2,1)}, u32[]{:S(2)}) copy-start(bf16[12,256,256]{2,1,0:T(8,128)(2,1)} %copy-done.2) | copy-start | bytes 4718596
  58.0 7.6 %collective-permute-start.4 = (f32[1280,128]{1,0:T(8,128)S(1)}, f32[1280,128]{1,0:T(8,128)S(1)}, u32[]{:S(2)}, u32[]{:S(2)}) collective-permute-start(f32[1280,128]{1,0:T(8,128)S(1)} %bitcast.13), channel_id=1, source_target_pairs={{0,1},{1,0},{2,3},{3,2},{4,5},{5,4},{6,7},{7,6},{8,9},{9,8},{10,11... | collective-permute-start | bytes 1966088 | tf_op jit(solution)/shard_map/ppermute | solution.py:641

commit v5 on v4

--- a/solution.py
+++ b/solution.py
@@ -130,9 +130,11 @@
             [
                 fetch(lm_hbm.at[:, cut], lm_ref.at[half]),
                 fetch(wd_hbm.at[:, cut], wd_ref.at[half]),
-                fetch(tr_hbm.at[:, cut], tr_ref.at[half]),
             ]
         )
+        for part in range(2):
+            rows = pl.ds(part * (tr_ref.shape[1] // 2), tr_ref.shape[1] // 2)
+            big[half].append(fetch(tr_hbm.at[rows, cut], tr_ref.at[half, rows]))
     for copy in small:
         copy.wait()
     direction = facing(wide(peer_ref), own_ref[0], block_cols)
@@ -146,7 +148,7 @@
 
     for half in range(2):
         cut = slice(half * lanes, (half + 1) * lanes)
-        for copy in big[half]:
+        for copy in big[half][:2]:
             copy.wait()
         tr_half, lm_half, wd_half = tr_ref.at[half], lm_ref.at[half], wd_ref.at[half]
         for k in range(16):
@@ -173,7 +175,9 @@
                 x_ref[k, pl.ds(pl.multiple_of(t * levels, levels), levels), cut] = value * sph_ref[k : k + 1, cut]
             return carry
 
-        lax.fori_loop(0, tracers, one, 0)
+        for part in range(2):
+            big[half][2 + part].wait()
+            lax.fori_loop(part * (tracers // 2), (part + 1) * (tracers // 2), one, 0)
 
     total = None
     for group in [[pair] for pair in EDGE_SLOTS] + CORNER_SIDES:
@@ -341,8 +345,9 @@
                 far_mix = term if far_mix is None else far_mix + term
         mix_ref[:, cols] = mix * jnp.concatenate([rden_ref[:, cols]] * (fields // levels), axis=0)
         high = far_mix.astype(BF16)
-        far_mix_ref[0, :, cols] = high
-        far_mix_ref[1, :, cols] = (far_mix - high.astype(F32)).astype(BF16)
+        far_mix_ref[:256, cols] = high
+        far_mix_ref[256:512, cols] = high
+        far_mix_ref[512:, cols] = (far_mix - high.astype(F32)).astype(BF16)
 
 
 def pack(odd, msg):
@@ -377,9 +382,8 @@
     levels = rden_ref.shape[0]
     two = merge(odd_ref[0], a_ref[...], b_ref[...])
     two_ref[...] = two
-    got = split(jnp.concatenate([one_ref[...], two], axis=1))
-    add = dot_nn(got, far_mix_ref[0]) + dot_nn(got, far_mix_ref[1])
-    add = add[:fields] + add[fields:]
+    got = split(jnp.concatenate([one_ref[...], two], axis=1), axis=1)
+    add = dot_nn(jnp.concatenate([got, got[:, :256]], axis=1), far_mix_ref[...])
     mix_hl = split(mix_ref[...] + add * jnp.concatenate([rden_ref[...]] * (fields // levels), axis=0))
     peers = rows_ref.shape[1]
     chunk = 512
@@ -578,7 +582,7 @@
             pltpu.VMEM((2, rows, half), F32),
             pltpu.VMEM((2, 2 * rows, half), F32),
             pltpu.VMEM((3, points, level_count, half), F32),
-            pltpu.SemaphoreType.DMA((15,)),
+            pltpu.SemaphoreType.DMA((17,)),
         ],
     )
     near_a = swap(first_a, 1, 0, sfc_count, block_cols)
@@ -610,7 +614,7 @@
         [
             ((points, fields, elems), F32, pltpu.VMEM),
             ((12, 256, elems), BF16, pltpu.VMEM),
-            ((2, 256, cols), BF16),
+            ((768, cols), BF16),
             ((fields, cols), F32),
         ],
         [own, weighted, peer, slot, flip, recv, sph, inv, rden],

time: 67.7 us -> 67.5 us (level)
  no operation moved by 1% of the time
where the time goes in v5:
time: 67.5 us; the launch traced here: 67.2 us
  starting transfers between devices  33.3 us (49%)
  Pallas kernels  17.7 us (26%)
  waiting for transfers between devices  12.4 us (18%)
  local copies, waits for them, and re-layouts  3 us (4%)
  between operations  0.82 us (1%)
    all_to_all x1, starting transfers between devices, body(): lax.all_to_all(send.reshape(sfc_count, 1, ROWS * fields), 'sfc', split_ax...  15.5 us
    pallas_call x7, Pallas kernels, call(): pl.pallas_call(kernel, out_shape=[out[2](*out[:2]) if len(out) > 2 else j...  14.5 us
    all_to_all x1, waiting for transfers between devices, body(): lax.all_to_all(send.reshape(sfc_count, 1, ROWS * fields), 'sfc', split_ax...  12.3 us
    ppermute x4, starting transfers between devices, swap(): return lax.ppermute(value, 'sfc', pairs)  12 us
    ppermute x1, starting transfers between devices, body(): other = lax.ppermute(moved, 'lev', [(0, 1), (1, 0)])  5.84 us
    pallas_call x1, Pallas kernels, body(): pl.pallas_call(mass_kernel, grid=(2,), out_shape=[jax.ShapeDtypeStruct((f...  3.19 us
    unnamed x8, local copies, waits for them, and re-layouts  3 us
  transfers between devices with their start and end apart: 6, of which 2 were waited for; matrix products, arithmetic and copies ran while one was open for 0% of the time, Pallas kernels for 14%

profile of v5, /device:TPU:1, one launch (start us, length us, event | category | flops | bytes accessed | tf_op | source)
XLA Modules:
  0.0 67.2 jit_solution(3951820098912843218)
XLA Ops:
  0.7 4.2 %shard_map.130 = (f32[16,128,256]{2,1,0:T(8,128)S(1)}, f32[64,128]{1,0:T(8,128)S(1)}, f32[64,128]{1,0:T(8,128)S(1)}, f32[128,128]{1,0:T(8,128)S(1)}, s32[8,1024]...) custom-call(s32[1]{0:T(128)} %bitcast.2.own_ref, ...), custom_call_target="tpu_custom_call" | custom-call | tf_op jit(solution)/shard_map/pallas_call | solution.py:500
  4.9 2.1 %collective-permute-start = (f32[64,128]{1,0:T(8,128)S(1)}, f32[64,128]{1,0:T(8,128)S(1)}, u32[]{:S(2)}, u32[]{:S(2)}) collective-permute-start(f32[64,128]{1,0:T(8,128)S(1)} %get-tuple-element.41), channel_id=1, source_target_pairs={{0,2},{2,0},{4,6},{6,4},{8,10},{10,8},{12,14},{14,12},{16,18},{18,... | collective-permute-start | bytes 98312 | tf_op jit(solution)/shard_map/ppermute | solution.py:515
  7.0 0.7 collective-permute-start.1
  7.7 1.3 %shard_map.131 = (s32[8,1024]{1,0:T(8,128)S(1)}, bf16[128,128]{1,0:T(8,128)(2,1)S(1)}, s32[8,1024]{1,0:T(8,128)S(1)}, f32[16,1024]{1,0:T(8,128)S(1)}, f32[2,128,128]{2,1,0:T(8,128)S(1)}) custom-call(s32[1]{0:T(128)} %bitcast.2.own_ref, s32[8,256]{1,0:T(8,128)S(1)} %get-tuple-element.44.peer_ref, s32[8,256]{1,0:T(8,128)S(1)} %get-tuple-element.45.flip_ref, ...), custom_call_target="tpu_custom_call" | custom-call | tf_op jit(solution)/shard_map/pallas_call | solution.py:500
  9.1 0.0 collective-permute-done.a_ref
  9.1 0.0 collective-permute-done.1.b_ref
  9.1 0.3 shard_map.132
  9.4 0.7 collective-permute-start.3
  10.1 8.5 %collective-permute-start.2 = (f32[64,128]{1,0:T(8,128)S(1)}, f32[64,128]{1,0:T(8,128)S(1)}, u32[]{:S(2)}, u32[]{:S(2)}) collective-permute-start(f32[64,128]{1,0:T(8,128)S(1)} %get-tuple-element.54), channel_id=1, source_target_pairs={{0,64},{64,0},{2,66},{66,2},{4,68},{68,4},{6,70},{70,6},{8,72},{72... | collective-permute-start | bytes 98312 | tf_op jit(solution)/shard_map/ppermute | solution.py:515
  18.6 3.1 %shard_map.133 = (f32[16,128,256]{2,1,0:T(8,128)S(1)}, bf16[12,256,256]{2,1,0:T(8,128)(2,1)S(1)}, bf16[768,1024]{1,0:T(8,128)(2,1)S(1)}, f32[128,1024]{1,0:T(8,128)S(1)}) custom-call(s32[1]{0:T(128)} %bitcast.2.own_ref, f32[16,128,256]{2,1,0:T(8,128)S(1)} %get-tuple-element.56.held_ref.x_ref, s32[8,256]{1,0:T(8,128)S(1)} %get-tuple-element.44.peer_ref, ...), custom_call_target="tpu_custom_call" | custom-call | tf_op jit(solution)/shard_map/pallas_call | solution.py:500
  21.7 0.0 copy-start
  21.7 0.0 copy-start.2
  21.7 0.0 collective-permute-done.3.b_ref
  21.7 0.0 collective-permute-done.2.a_ref
  21.8 2.0 %shard_map.134 = (f32[128,128]{1,0:T(8,128)S(1)}, f32[1280,128]{1,0:T(8,128)}) custom-call(s32[1]{0:T(128)} %bitcast.row_odd_ref.odd_ref, f32[128,128]{1,0:T(8,128)S(1)} %get-tuple-element.53.one_ref, f32[64,128]{1,0:T(8,128)S(1)} %collective-permute-done.2.a_ref, f32[64,128]{1,0:T(8,128)S(1)} %collective-permute-done.3.b_ref, ...), custom_call_target="tpu_custom_call" | custom-call | tf_op jit(solution)/shard_map/pallas_call | solution.py:500
  23.8 0.0 copy-done
  23.8 0.0 copy-done.2
  23.8 15.5 %all-to-all-start = ((f32[128,1,1280]{2,1,0:T(1,128)}), f32[128,1,1280]{2,1,0:T(1,128)S(1)}, u32[]{:S(2)}, u32[]{:S(2)}) async-start(f32[128,1,1280]{2,1,0:T(1,128)} %bitcast.8), calls=%async_computation | async-start | bytes 1310720 | tf_op jit(solution)/shard_map/all_to_all | solution.py:628
  39.3 0.0 copy-start.1
  39.3 1.6 %copy-done.1 = f32[16,128,256]{2,1,0:T(8,128)S(1)} copy-done((f32[16,128,256]{2,1,0:T(8,128)S(1)}, f32[16,128,256]{2,1,0:T(8,128)}, u32[]{:S(2)}) %copy-start.1) | copy-done | bytes 2097176
  40.9 0.0 copy-start.3
  40.9 1.4 %copy-done.3 = bf16[12,256,256]{2,1,0:T(8,128)(2,1)S(1)} copy-done((bf16[12,256,256]{2,1,0:T(8,128)(2,1)S(1)}, bf16[12,256,256]{2,1,0:T(8,128)(2,1)}, u32[]{:S(2)}) %copy-start.3) | copy-done | bytes 1572888
  42.3 3.2 %shard_map.135 = (f32[2048,256]{1,0:T(8,128)}, bf16[1280,256]{1,0:T(8,128)(2,1)S(1)}) custom-call(f32[16,128,256]{2,1,0:T(8,128)S(1)} %copy-done.1, f32[128,128]{1,0:T(8,128)S(1)} %get-tuple-element.53.one_ref, f32[128,128]{1,0:T(8,128)S(1)} %get-tuple-element.68.two_ref, bf16[12,256,256]{2,1,0:T(8,128)(2,1)S(1)} %copy-done.3, ...), custom_call_target="tpu_custom_call" | custom-call | flops 402653184 | bytes 8388608 | tf_op jit(solution)/shard_map/pallas_call | solution.py:632
  45.5 12.3 %all-to-all-done = f32[128,1,1280]{2,1,0:T(1,128)S(1)} async-done(((f32[128,1,1280]{2,1,0:T(1,128)}), f32[128,1,1280]{2,1,0:T(1,128)S(1)}, u32[]{:S(2)}, u32[]{:S(2)}) %all-to-all-start) | async-done | bytes 655392 | tf_op jit(solution)/shard_map/all_to_all | solution.py:628
  57.7 5.8 %collective-permute-start.4 = (f32[1280,128]{1,0:T(8,128)S(1)}, f32[1280,128]{1,0:T(8,128)S(1)}, u32[]{:S(2)}, u32[]{:S(2)}) collective-permute-start(f32[1280,128]{1,0:T(8,128)S(1)} %bitcast.13), channel_id=1, source_target_pairs={{0,1},{1,0},{2,3},{3,2},{4,5},{5,4},{6,7},{7,6},{8,9},{9,8},{10,11... | collective-permute-start | bytes 1966088 | tf_op jit(solution)/shard_map/ppermute | solution.py:645
  63.6 1.6 %shard_map.136 = (bf16[640,1280]{1,0:T(8,128)(2,1)S(1)}, bf16[640,256]{1,0:T(8,128)(2,1)S(1)}, f32[256,640]{1,0:T(8,128)S(1)}) custom-call(s32[1]{0:T(128)} %bitcast.11.lev_ref, f32[1280,128]{1,0:T(8,128)S(1)} %bitcast.14, bf16[1280,256]{1,0:T(8,128)(2,1)S(1)} %get-tuple-element.73.frame_ref), custom_call_target="tpu_custom_call" | custom-call | tf_op jit(solution)/shard_map/pallas_call | solution.py:500
  65.2 0.1 collective-permute-done.4.par_ref
  65.3 1.9 %shard_map.137 = (f32[256,640]{1,0:T(8,128)}, f32[32,640]{1,0:T(8,128)}) custom-call(s32[1]{0:T(128)} %bitcast.11.lev_ref, f32[256,640]{1,0:T(8,128)S(1)} %get-tuple-element.74.half_ref, f32[1280,128]{1,0:T(8,128)S(1)} %collective-permute-done.4.par_ref, bf16[640,1280]{1,0:T(8,128)(2,1)S(1)} %get-tuple-element.75.pick_ref, ...), custom_call_target="tpu_custom_call" | custom-call | tf_op jit(solution)/shard_map/pallas_call | solution.py:500
Async XLA Ops:
  4.9 4.2 %collective-permute-start = (f32[64,128]{1,0:T(8,128)S(1)}, f32[64,128]{1,0:T(8,128)S(1)}, u32[]{:S(2)}, u32[]{:S(2)}) collective-permute-start(f32[64,128]{1,0:T(8,128)S(1)} %get-tuple-element.41), channel_id=1, source_target_pairs={{0,2},{2,0},{4,6},{6,4},{8,10},{10,8},{12,14},{14,12},{16,18},{18,... | collective-permute-start | bytes 98312 | tf_op jit(solution)/shard_map/ppermute | solution.py:515
  7.0 2.1 %collective-permute-start.1 = (f32[64,128]{1,0:T(8,128)S(1)}, f32[64,128]{1,0:T(8,128)S(1)}, u32[]{:S(2)}, u32[]{:S(2)}) collective-permute-start(f32[64,128]{1,0:T(8,128)S(1)} %get-tuple-element.42), channel_id=1, source_target_pairs={{2,4},{4,2},{6,8},{8,6},{10,12},{12,10},{14,16},{16,14},{18,20},{2... | collective-permute-start | bytes 98312 | tf_op jit(solution)/shard_map/ppermute | solution.py:515
  9.4 12.3 %collective-permute-start.3 = (f32[64,128]{1,0:T(8,128)S(1)}, f32[64,128]{1,0:T(8,128)S(1)}, u32[]{:S(2)}, u32[]{:S(2)}) collective-permute-start(f32[64,128]{1,0:T(8,128)S(1)} %get-tuple-element.55), channel_id=1, source_target_pairs={{64,128},{128,64},{66,130},{130,66},{68,132},{132,68},{70,134},{13... | collective-permute-start | bytes 98312 | tf_op jit(solution)/shard_map/ppermute | solution.py:515
  10.1 11.7 %collective-permute-start.2 = (f32[64,128]{1,0:T(8,128)S(1)}, f32[64,128]{1,0:T(8,128)S(1)}, u32[]{:S(2)}, u32[]{:S(2)}) collective-permute-start(f32[64,128]{1,0:T(8,128)S(1)} %get-tuple-element.54), channel_id=1, source_target_pairs={{0,64},{64,0},{2,66},{66,2},{4,68},{68,4},{6,70},{70,6},{8,72},{72... | collective-permute-start | bytes 98312 | tf_op jit(solution)/shard_map/ppermute | solution.py:515
  21.7 2.0 %copy-start = (f32[16,128,256]{2,1,0:T(8,128)}, f32[16,128,256]{2,1,0:T(8,128)S(1)}, u32[]{:S(2)}) copy-start(f32[16,128,256]{2,1,0:T(8,128)S(1)} %get-tuple-element.65.held_ref.xd_ref) | copy-start | bytes 6291460
  21.7 2.0 %copy-start.2 = (bf16[12,256,256]{2,1,0:T(8,128)(2,1)}, bf16[12,256,256]{2,1,0:T(8,128)(2,1)S(1)}, u32[]{:S(2)}) copy-start(bf16[12,256,256]{2,1,0:T(8,128)(2,1)S(1)} %get-tuple-element.66.far_held_ref.far_ref) | copy-start | bytes 4718596
  23.8 34.0 %all-to-all-start = ((f32[128,1,1280]{2,1,0:T(1,128)}), f32[128,1,1280]{2,1,0:T(1,128)S(1)}, u32[]{:S(2)}, u32[]{:S(2)}) async-start(f32[128,1,1280]{2,1,0:T(1,128)} %bitcast.8), calls=%async_computation | async-start | bytes 1310720 | tf_op jit(solution)/shard_map/all_to_all | solution.py:628
  39.3 1.6 %copy-start.1 = (f32[16,128,256]{2,1,0:T(8,128)S(1)}, f32[16,128,256]{2,1,0:T(8,128)}, u32[]{:S(2)}) copy-start(f32[16,128,256]{2,1,0:T(8,128)} %copy-done) | copy-start | bytes 6291460
  40.9 1.4 %copy-start.3 = (bf16[12,256,256]{2,1,0:T(8,128)(2,1)S(1)}, bf16[12,256,256]{2,1,0:T(8,128)(2,1)}, u32[]{:S(2)}) copy-start(bf16[12,256,256]{2,1,0:T(8,128)(2,1)} %copy-done.2) | copy-start | bytes 4718596
  57.7 7.6 %collective-permute-start.4 = (f32[1280,128]{1,0:T(8,128)S(1)}, f32[1280,128]{1,0:T(8,128)S(1)}, u32[]{:S(2)}, u32[]{:S(2)}) collective-permute-start(f32[1280,128]{1,0:T(8,128)S(1)} %bitcast.13), channel_id=1, source_target_pairs={{0,1},{1,0},{2,3},{3,2},{4,5},{5,4},{6,7},{7,6},{8,9},{9,8},{10,11... | collective-permute-start | bytes 1966088 | tf_op jit(solution)/shard_map/ppermute | solution.py:645

commit v6 on v5

--- a/solution.py
+++ b/solution.py
@@ -456,8 +456,9 @@
         half_ref[:, block * 128 : (block + 1) * 128] = got
 
 
-def physics_kernel(lev_ref, half_ref, par_ref, pick_ref, meta_ref, mix_ref, sig_ref):
+def physics_kernel(lev_ref, half_ref, par_ref, pick_ref, meta_ref, mix_hbm, sig_hbm, mix_ref, sig_ref, sems):
     lev = lev_ref[0]
+    copies = []
     levels2 = sig_ref.shape[0]
     fields = par_ref.shape[1]
     levels = levels2 // 2
@@ -483,6 +484,11 @@
             mix = jnp.concatenate([first[t * levels : (t + 1) * levels], last[t * levels : (t + 1) * levels]], axis=0)
             mean = jnp.sum(thick * mix, axis=0, keepdims=True) * share
             mix_ref[t * levels2 : (t + 1) * levels2, cols] = mix + MIXING_RATE * sigma * (mean - mix)
+        for src, dst in ((mix_ref, mix_hbm), (sig_ref, sig_hbm)):
+            copies.append(pltpu.make_async_copy(src.at[:, cols], dst.at[:, cols], sems.at[len(copies)]))
+            copies[-1].start()
+    for copy in copies:
+        copy.wait()
 
 
 def halved(shape):
@@ -653,8 +659,13 @@
     )
     mixed, sigma = call(
         physics_kernel,
-        [((tracer_count * levels, slots), F32), ((levels, slots), F32)],
+        [((tracer_count * levels, slots), F32, pltpu.HBM), ((levels, slots), F32, pltpu.HBM)],
         [lev, own_half, other, pick, meta],
+        scratch=[
+            pltpu.VMEM((tracer_count * levels, slots), F32),
+            pltpu.VMEM((levels, slots), F32),
+            pltpu.SemaphoreType.DMA((2 * slots // 128,)),
+        ],
     )
     return (
         mass.reshape(tracers.shape),

time: 67.5 us -> 67.4 us (level)
  no operation moved by 1% of the time
where the time goes in v6:
time: 67.4 us; the launch traced here: 67.1 us
  starting transfers between devices  33.3 us (49%)
  Pallas kernels  17.7 us (26%)
  waiting for transfers between devices  12.4 us (18%)
  local copies, waits for them, and re-layouts  3 us (4%)
  between operations  0.82 us (1%)
    all_to_all x1, starting transfers between devices, body(): lax.all_to_all(send.reshape(sfc_count, 1, ROWS * fields), 'sfc', split_ax...  15.5 us
    pallas_call x7, Pallas kernels, call(): pl.pallas_call(kernel, out_shape=[out[2](*out[:2]) if len(out) > 2 else j...  14.5 us
    all_to_all x1, waiting for transfers between devices, body(): lax.all_to_all(send.reshape(sfc_count, 1, ROWS * fields), 'sfc', split_ax...  12.3 us
    ppermute x4, starting transfers between devices, swap(): return lax.ppermute(value, 'sfc', pairs)  12 us
    ppermute x1, starting transfers between devices, body(): other = lax.ppermute(moved, 'lev', [(0, 1), (1, 0)])  5.84 us
    pallas_call x1, Pallas kernels, body(): pl.pallas_call(mass_kernel, grid=(2,), out_shape=[jax.ShapeDtypeStruct((f...  3.19 us
    unnamed x8, local copies, waits for them, and re-layouts  3 us
  transfers between devices with their start and end apart: 6, of which 2 were waited for; matrix products, arithmetic and copies ran while one was open for 0% of the time, Pallas kernels for 14%

profile of v6, /device:TPU:1, one launch (start us, length us, event | category | flops | bytes accessed | tf_op | source)
XLA Modules:
  0.0 67.1 jit_solution(7046811644294185977)
XLA Ops:
  0.7 4.2 %shard_map.130 = (f32[16,128,256]{2,1,0:T(8,128)S(1)}, f32[64,128]{1,0:T(8,128)S(1)}, f32[64,128]{1,0:T(8,128)S(1)}, f32[128,128]{1,0:T(8,128)S(1)}, s32[8,1024]...) custom-call(s32[1]{0:T(128)} %bitcast.2.own_ref, ...), custom_call_target="tpu_custom_call" | custom-call | tf_op jit(solution)/shard_map/pallas_call | solution.py:506
  4.9 2.1 %collective-permute-start = (f32[64,128]{1,0:T(8,128)S(1)}, f32[64,128]{1,0:T(8,128)S(1)}, u32[]{:S(2)}, u32[]{:S(2)}) collective-permute-start(f32[64,128]{1,0:T(8,128)S(1)} %get-tuple-element.41), channel_id=1, source_target_pairs={{0,2},{2,0},{4,6},{6,4},{8,10},{10,8},{12,14},{14,12},{16,18},{18,... | collective-permute-start | bytes 98312 | tf_op jit(solution)/shard_map/ppermute | solution.py:521
  7.0 0.7 collective-permute-start.1
  7.7 1.3 %shard_map.131 = (s32[8,1024]{1,0:T(8,128)S(1)}, bf16[128,128]{1,0:T(8,128)(2,1)S(1)}, s32[8,1024]{1,0:T(8,128)S(1)}, f32[16,1024]{1,0:T(8,128)S(1)}, f32[2,128,128]{2,1,0:T(8,128)S(1)}) custom-call(s32[1]{0:T(128)} %bitcast.2.own_ref, s32[8,256]{1,0:T(8,128)S(1)} %get-tuple-element.44.peer_ref, s32[8,256]{1,0:T(8,128)S(1)} %get-tuple-element.45.flip_ref, ...), custom_call_target="tpu_custom_call" | custom-call | tf_op jit(solution)/shard_map/pallas_call | solution.py:506
  9.1 0.0 collective-permute-done.a_ref
  9.1 0.0 collective-permute-done.1.b_ref
  9.1 0.3 shard_map.132
  9.4 0.7 collective-permute-start.3
  10.1 8.5 %collective-permute-start.2 = (f32[64,128]{1,0:T(8,128)S(1)}, f32[64,128]{1,0:T(8,128)S(1)}, u32[]{:S(2)}, u32[]{:S(2)}) collective-permute-start(f32[64,128]{1,0:T(8,128)S(1)} %get-tuple-element.54), channel_id=1, source_target_pairs={{0,64},{64,0},{2,66},{66,2},{4,68},{68,4},{6,70},{70,6},{8,72},{72... | collective-permute-start | bytes 98312 | tf_op jit(solution)/shard_map/ppermute | solution.py:521
  18.6 3.1 %shard_map.133 = (f32[16,128,256]{2,1,0:T(8,128)S(1)}, bf16[12,256,256]{2,1,0:T(8,128)(2,1)S(1)}, bf16[768,1024]{1,0:T(8,128)(2,1)S(1)}, f32[128,1024]{1,0:T(8,128)S(1)}) custom-call(s32[1]{0:T(128)} %bitcast.2.own_ref, f32[16,128,256]{2,1,0:T(8,128)S(1)} %get-tuple-element.56.held_ref.x_ref, s32[8,256]{1,0:T(8,128)S(1)} %get-tuple-element.44.peer_ref, ...), custom_call_target="tpu_custom_call" | custom-call | tf_op jit(solution)/shard_map/pallas_call | solution.py:506
  21.7 0.0 copy-start
  21.7 0.0 copy-start.2
  21.7 0.0 collective-permute-done.3.b_ref
  21.7 0.0 collective-permute-done.2.a_ref
  21.8 2.0 %shard_map.134 = (f32[128,128]{1,0:T(8,128)S(1)}, f32[1280,128]{1,0:T(8,128)}) custom-call(s32[1]{0:T(128)} %bitcast.row_odd_ref.odd_ref, f32[128,128]{1,0:T(8,128)S(1)} %get-tuple-element.53.one_ref, f32[64,128]{1,0:T(8,128)S(1)} %collective-permute-done.2.a_ref, f32[64,128]{1,0:T(8,128)S(1)} %collective-permute-done.3.b_ref, ...), custom_call_target="tpu_custom_call" | custom-call | tf_op jit(solution)/shard_map/pallas_call | solution.py:506
  23.8 0.0 copy-done
  23.8 0.0 copy-done.2
  23.8 15.5 %all-to-all-start = ((f32[128,1,1280]{2,1,0:T(1,128)}), f32[128,1,1280]{2,1,0:T(1,128)S(1)}, u32[]{:S(2)}, u32[]{:S(2)}) async-start(f32[128,1,1280]{2,1,0:T(1,128)} %bitcast.8), calls=%async_computation | async-start | bytes 1310720 | tf_op jit(solution)/shard_map/all_to_all | solution.py:634
  39.3 0.0 copy-start.1
  39.3 1.6 %copy-done.1 = f32[16,128,256]{2,1,0:T(8,128)S(1)} copy-done((f32[16,128,256]{2,1,0:T(8,128)S(1)}, f32[16,128,256]{2,1,0:T(8,128)}, u32[]{:S(2)}) %copy-start.1) | copy-done | bytes 2097176
  40.9 0.0 copy-start.3
  40.9 1.4 %copy-done.3 = bf16[12,256,256]{2,1,0:T(8,128)(2,1)S(1)} copy-done((bf16[12,256,256]{2,1,0:T(8,128)(2,1)S(1)}, bf16[12,256,256]{2,1,0:T(8,128)(2,1)}, u32[]{:S(2)}) %copy-start.3) | copy-done | bytes 1572888
  42.3 3.2 %shard_map.135 = (f32[2048,256]{1,0:T(8,128)}, bf16[1280,256]{1,0:T(8,128)(2,1)S(1)}) custom-call(f32[16,128,256]{2,1,0:T(8,128)S(1)} %copy-done.1, f32[128,128]{1,0:T(8,128)S(1)} %get-tuple-element.53.one_ref, f32[128,128]{1,0:T(8,128)S(1)} %get-tuple-element.68.two_ref, bf16[12,256,256]{2,1,0:T(8,128)(2,1)S(1)} %copy-done.3, ...), custom_call_target="tpu_custom_call" | custom-call | flops 402653184 | bytes 8388608 | tf_op jit(solution)/shard_map/pallas_call | solution.py:638
  45.5 12.3 %all-to-all-done = f32[128,1,1280]{2,1,0:T(1,128)S(1)} async-done(((f32[128,1,1280]{2,1,0:T(1,128)}), f32[128,1,1280]{2,1,0:T(1,128)S(1)}, u32[]{:S(2)}, u32[]{:S(2)}) %all-to-all-start) | async-done | bytes 655392 | tf_op jit(solution)/shard_map/all_to_all | solution.py:634
  57.7 5.8 %collective-permute-start.4 = (f32[1280,128]{1,0:T(8,128)S(1)}, f32[1280,128]{1,0:T(8,128)S(1)}, u32[]{:S(2)}, u32[]{:S(2)}) collective-permute-start(f32[1280,128]{1,0:T(8,128)S(1)} %bitcast.13), channel_id=1, source_target_pairs={{0,1},{1,0},{2,3},{3,2},{4,5},{5,4},{6,7},{7,6},{8,9},{9,8},{10,11... | collective-permute-start | bytes 1966088 | tf_op jit(solution)/shard_map/ppermute | solution.py:651
  63.6 1.6 %shard_map.136 = (bf16[640,1280]{1,0:T(8,128)(2,1)S(1)}, bf16[640,256]{1,0:T(8,128)(2,1)S(1)}, f32[256,640]{1,0:T(8,128)S(1)}) custom-call(s32[1]{0:T(128)} %bitcast.11.lev_ref, f32[1280,128]{1,0:T(8,128)S(1)} %bitcast.14, bf16[1280,256]{1,0:T(8,128)(2,1)S(1)} %get-tuple-element.73.frame_ref), custom_call_target="tpu_custom_call" | custom-call | tf_op jit(solution)/shard_map/pallas_call | solution.py:506
  65.2 0.1 collective-permute-done.4.par_ref
  65.3 1.8 %shard_map.137 = (f32[256,640]{1,0:T(8,128)}, f32[32,640]{1,0:T(8,128)}) custom-call(s32[1]{0:T(128)} %bitcast.11.lev_ref, f32[256,640]{1,0:T(8,128)S(1)} %get-tuple-element.74.half_ref, f32[1280,128]{1,0:T(8,128)S(1)} %collective-permute-done.4.par_ref, bf16[640,1280]{1,0:T(8,128)(2,1)S(1)} %get-tuple-element.75.pick_ref, ...), custom_call_target="tpu_custom_call" | custom-call | tf_op jit(solution)/shard_map/pallas_call | solution.py:506
Async XLA Ops:
  4.9 4.2 %collective-permute-start = (f32[64,128]{1,0:T(8,128)S(1)}, f32[64,128]{1,0:T(8,128)S(1)}, u32[]{:S(2)}, u32[]{:S(2)}) collective-permute-start(f32[64,128]{1,0:T(8,128)S(1)} %get-tuple-element.41), channel_id=1, source_target_pairs={{0,2},{2,0},{4,6},{6,4},{8,10},{10,8},{12,14},{14,12},{16,18},{18,... | collective-permute-start | bytes 98312 | tf_op jit(solution)/shard_map/ppermute | solution.py:521
  7.0 2.1 %collective-permute-start.1 = (f32[64,128]{1,0:T(8,128)S(1)}, f32[64,128]{1,0:T(8,128)S(1)}, u32[]{:S(2)}, u32[]{:S(2)}) collective-permute-start(f32[64,128]{1,0:T(8,128)S(1)} %get-tuple-element.42), channel_id=1, source_target_pairs={{2,4},{4,2},{6,8},{8,6},{10,12},{12,10},{14,16},{16,14},{18,20},{2... | collective-permute-start | bytes 98312 | tf_op jit(solution)/shard_map/ppermute | solution.py:521
  9.4 12.3 %collective-permute-start.3 = (f32[64,128]{1,0:T(8,128)S(1)}, f32[64,128]{1,0:T(8,128)S(1)}, u32[]{:S(2)}, u32[]{:S(2)}) collective-permute-start(f32[64,128]{1,0:T(8,128)S(1)} %get-tuple-element.55), channel_id=1, source_target_pairs={{64,128},{128,64},{66,130},{130,66},{68,132},{132,68},{70,134},{13... | collective-permute-start | bytes 98312 | tf_op jit(solution)/shard_map/ppermute | solution.py:521
  10.1 11.7 %collective-permute-start.2 = (f32[64,128]{1,0:T(8,128)S(1)}, f32[64,128]{1,0:T(8,128)S(1)}, u32[]{:S(2)}, u32[]{:S(2)}) collective-permute-start(f32[64,128]{1,0:T(8,128)S(1)} %get-tuple-element.54), channel_id=1, source_target_pairs={{0,64},{64,0},{2,66},{66,2},{4,68},{68,4},{6,70},{70,6},{8,72},{72... | collective-permute-start | bytes 98312 | tf_op jit(solution)/shard_map/ppermute | solution.py:521
  21.7 2.0 %copy-start = (f32[16,128,256]{2,1,0:T(8,128)}, f32[16,128,256]{2,1,0:T(8,128)S(1)}, u32[]{:S(2)}) copy-start(f32[16,128,256]{2,1,0:T(8,128)S(1)} %get-tuple-element.65.held_ref.xd_ref) | copy-start | bytes 6291460
  21.7 2.0 %copy-start.2 = (bf16[12,256,256]{2,1,0:T(8,128)(2,1)}, bf16[12,256,256]{2,1,0:T(8,128)(2,1)S(1)}, u32[]{:S(2)}) copy-start(bf16[12,256,256]{2,1,0:T(8,128)(2,1)S(1)} %get-tuple-element.66.far_held_ref.far_ref) | copy-start | bytes 4718596
  23.8 34.0 %all-to-all-start = ((f32[128,1,1280]{2,1,0:T(1,128)}), f32[128,1,1280]{2,1,0:T(1,128)S(1)}, u32[]{:S(2)}, u32[]{:S(2)}) async-start(f32[128,1,1280]{2,1,0:T(1,128)} %bitcast.8), calls=%async_computation | async-start | bytes 1310720 | tf_op jit(solution)/shard_map/all_to_all | solution.py:634
  39.3 1.6 %copy-start.1 = (f32[16,128,256]{2,1,0:T(8,128)S(1)}, f32[16,128,256]{2,1,0:T(8,128)}, u32[]{:S(2)}) copy-start(f32[16,128,256]{2,1,0:T(8,128)} %copy-done) | copy-start | bytes 6291460
  40.9 1.4 %copy-start.3 = (bf16[12,256,256]{2,1,0:T(8,128)(2,1)S(1)}, bf16[12,256,256]{2,1,0:T(8,128)(2,1)}, u32[]{:S(2)}) copy-start(bf16[12,256,256]{2,1,0:T(8,128)(2,1)} %copy-done.2) | copy-start | bytes 4718596
  57.7 7.6 %collective-permute-start.4 = (f32[1280,128]{1,0:T(8,128)S(1)}, f32[1280,128]{1,0:T(8,128)S(1)}, u32[]{:S(2)}, u32[]{:S(2)}) collective-permute-start(f32[1280,128]{1,0:T(8,128)S(1)} %bitcast.13), channel_id=1, source_target_pairs={{0,1},{1,0},{2,3},{3,2},{4,5},{5,4},{6,7},{7,6},{8,9},{9,8},{10,11... | collective-permute-start | bytes 1966088 | tf_op jit(solution)/shard_map/ppermute | solution.py:651
